TPU v7x, 256 devices: a whole 4x4x8 slice. The times are simulated.
256 devices in a mesh: gx: 32 (over z_hi, x, core), gy: 8 (over z_lo, y).
Axes of the slice: x: 4, y: 4, z: 8 (z_hi: 4, z_lo: 2; z = z_hi * 2 + z_lo), core: 2. Of those that a mesh axis runs over, the one named last changes fastest.
Arguments:
- displacement: float32 [3, 128, 256, 128], P(None, 'gx', 'gy'), may hold values from -4 to 4
- rhs: float32 [3, 128, 256, 128], P(None, 'gx', 'gy'), may hold values from -6 to 6
- labels: int32 [128, 256, 128], P('gx', 'gy'), may hold values from 0 to 7
- stiffness: float32 [8, 6], replicated, may hold values from -6 to 20, as said below
- rows: int32 [32, 8, 1024], P('gx', 'gy'), may hold values from 0 to 16383, as said below
- counts: int32 [32, 8], P('gx', 'gy'), may hold values from 128 to 1024, as said below
- multipliers: float32 [3, 32, 8, 1024], P(None, 'gx', 'gy'), may hold values from -6 to 6
Outputs:
- smoothed: float32 [3, 128, 256, 128], P(None, 'gx', 'gy')
- coarse: float32 [3, 64, 128, 64], P(None, 'gx')
- updated: float32 [3, 32, 8, 1024], P(None, 'gx', 'gy')
Inputs may be any that keep to these rules, and one draw needn't show every extreme that they name: `rows`: each block's 1024 entries are distinct cell numbers (x * 32 + y) * 128 + z of that block. `counts`: some block has all 1024 slots live in every draw. `stiffness`: diagonal entries are positive; each off-diagonal entry is at most 0.3 times the geometric mean of its two diagonal entries.
All inputs are finite; a program needn't handle non-finite values.
Results may differ from a plain program's by a relative error of at most 0.00002.
Values sent between devices are 32-bit elements; how exact they have to be, the bound alone decides.
No kernel may reach another device: no remote copies, remote signals or barrier semaphores. Data moves between devices by JAX's collectives and lax.ppermute only.
A program may use at most 192 MiB of HBM per device.

v0:
```python
import jax
import jax.numpy as jnp
from jax import lax
from jax.experimental import pallas as pl
from jax.experimental.pallas import tpu as pltpu
from jax.sharding import PartitionSpec as P

SYMMETRIC_INDEX = ((0, 3, 4), (3, 1, 5), (4, 5, 2))
DAMPING = 0.6
MASS_SHIFT = 1.0
PENALTY = 1.0

CX, CY, NZ, SLOTS = 4, 32, 128, 1024
N_GX, N_GY = 32, 8
NX, NY = CX * N_GX, CY * N_GY
LABELS = 8
HALO = 3
PX = CX + 2 * HALO
PR = PX - 2
EDGE = 16
LAB0 = 3 * PX
RHS0 = LAB0 + PX
FIELDS = RHS0 + 3 * PR
SIDE = (3 * HALO + HALO + 3 * (HALO - 1)) * CY
IFACE = SIDE
SLOT_ROWS = SLOTS // 128
UP_ROWS = SIDE + 4 * SLOT_ROWS
VMEM = pl.BlockSpec(memory_space=pltpu.VMEM)
SMEM = pl.BlockSpec(memory_space=pltpu.SMEM)
HBM = pl.BlockSpec(memory_space=pltpu.HBM)
F32 = jnp.float32
BF16 = jnp.bfloat16
PARAMS = pltpu.CompilerParams(vmem_limit_bytes=48 * 1024 * 1024)


def f32(*shape):
    return jax.ShapeDtypeStruct(shape, F32)


def pieces_of(value):
    high = value.astype(BF16)
    rest = value - high.astype(F32)
    middle = rest.astype(BF16)
    low = (rest - middle.astype(F32)).astype(BF16)
    return (high, middle, low)


def slot_number():
    return lax.broadcasted_iota(jnp.int32, (SLOT_ROWS, 128), 0) * 128 + lax.broadcasted_iota(
        jnp.int32, (SLOT_ROWS, 128), 1
    )


def pack_x(
    count, disp_in, rhs_in, labels_in, cells_in, mult_in,
    up, down, disp, rhs, labels, cells, mult,
    raw_labels, raw_cells, arrived,
):
    pairs = (
        (cells_in, raw_cells), (labels_in, raw_labels), (disp_in, disp), (rhs_in, rhs), (mult_in, mult)
    )
    copies = [pltpu.make_async_copy(a, b, arrived.at[i]) for i, (a, b) in enumerate(pairs)]
    for copy in copies:
        copy.start()
    for copy in copies[:2]:
        copy.wait()
    live = slot_number() < count[0, 0]
    live_cells = jnp.where(live, raw_cells[...], -1)
    cells[...] = live_cells
    up[pl.ds(IFACE, SLOT_ROWS), :] = live_cells.astype(F32)
    labels[...] = raw_labels[...].astype(F32)
    for k in range(HALO):
        row = (3 * HALO + k) * CY
        up[pl.ds(row, CY), :] = raw_labels[pl.ds((CX - HALO + k) * CY, CY), :].astype(F32)
        down[pl.ds(row, CY), :] = raw_labels[pl.ds(k * CY, CY), :].astype(F32)
    for copy in copies[2:]:
        copy.wait()
    for c in range(3):
        for k in range(HALO):
            row = (c * HALO + k) * CY
            up[pl.ds(row, CY), :] = disp[pl.ds((c * CX + CX - HALO + k) * CY, CY), :]
            down[pl.ds(row, CY), :] = disp[pl.ds((c * CX + k) * CY, CY), :]
        for k in range(HALO - 1):
            row = (4 * HALO + c * (HALO - 1) + k) * CY
            up[pl.ds(row, CY), :] = rhs[pl.ds((c * CX + CX - HALO + 1 + k) * CY, CY), :]
            down[pl.ds(row, CY), :] = rhs[pl.ds((c * CX + k) * CY, CY), :]
        up[pl.ds(IFACE + (1 + c) * SLOT_ROWS, SLOT_ROWS), :] = mult[c]


def paired(array, j):
    return jnp.concatenate([array[2 * j : 2 * j + 1], array[2 * j + 1 : 2 * j + 2]], axis=1)


def spread(cells, mult, first, columns):
    column = jnp.where(cells < 0, -1, cells // NZ - first)
    depth = cells % NZ
    total = jnp.zeros((10 * columns, NZ), F32)
    parts = [piece for c in range(3) for piece in pieces_of(mult[c])]
    for j in range(SLOT_ROWS // 2):
        at_column = lax.broadcasted_iota(jnp.int32, (columns, 256), 0) == paired(column, j)
        at_depth = lax.broadcasted_iota(jnp.int32, (NZ, 256), 0) == paired(depth, j)
        left = [jnp.where(at_column, paired(piece.astype(F32), j), 0.0).astype(BF16) for piece in parts]
        left.append(jnp.where(at_column, 1.0, 0.0).astype(BF16))
        total = total + lax.dot_general(
            jnp.concatenate(left, axis=0),
            jnp.where(at_depth, 1.0, 0.0).astype(BF16),
            (((1,), (1,)), ((), ())),
            preferred_element_type=F32,
        )
    part = [total[i * columns : (i + 1) * columns] for i in range(10)]
    return [part[3 * c] + part[3 * c + 1] + part[3 * c + 2] for c in range(3)] + [part[9]]


def spread_own(cells, mult, dense):
    values = spread(cells[...], [mult[c] for c in range(3)], 0, CX * CY)
    for i in range(4):
        dense[i] = values[i]


def inside_x():
    here = lax.axis_index("gx")
    return (
        jnp.where(here > 0, 1.0, 0.0).astype(F32),
        jnp.where(here < N_GX - 1, 1.0, 0.0).astype(F32),
    )


def pack_y(disp, rhs, labels, before, after, dense, up, down):
    near, far = inside_x()
    for out, start in ((up, CY - HALO), (down, 0)):
        for k in range(HALO):
            y = start + k
            for c in range(3):
                at = c * PX
                out[k, pl.ds(at, HALO), :] = near * before[pl.ds(c * HALO * CY + y, HALO, stride=CY), :]
                out[k, pl.ds(at + HALO, CX), :] = disp[pl.ds(c * CX * CY + y, CX, stride=CY), :]
                out[k, pl.ds(at + HALO + CX, HALO), :] = far * after[pl.ds(c * HALO * CY + y, HALO, stride=CY), :]
                at = RHS0 + c * PR
                row = (4 * HALO + c * (HALO - 1)) * CY + y
                out[k, pl.ds(at, HALO - 1), :] = before[pl.ds(row, HALO - 1, stride=CY), :]
                out[k, pl.ds(at + HALO - 1, CX), :] = rhs[pl.ds(c * CX * CY + y, CX, stride=CY), :]
                out[k, pl.ds(at + HALO - 1 + CX, HALO - 1), :] = after[pl.ds(row, HALO - 1, stride=CY), :]
            row = 3 * HALO * CY + y
            out[k, pl.ds(LAB0, HALO), :] = near * before[pl.ds(row, HALO, stride=CY), :]
            out[k, pl.ds(LAB0 + HALO, CX), :] = labels[pl.ds(y, CX, stride=CY), :]
            out[k, pl.ds(LAB0 + HALO + CX, HALO), :] = far * after[pl.ds(row, HALO, stride=CY), :]


def times(k, v):
    return [
        k[SYMMETRIC_INDEX[c][0]] * v[0] + k[SYMMETRIC_INDEX[c][1]] * v[1] + k[SYMMETRIC_INDEX[c][2]] * v[2]
        for c in range(3)
    ]


class Stencil:
    def __init__(self, rows, entry, fields, row_inside, scratch):
        self.rows, self.entry, self.fields, self.row_inside = rows, entry, fields, row_inside
        self.coeff, self.total, self.scale, self.flux = scratch
        lane = lax.broadcasted_iota(jnp.int32, (1, NZ), 1)
        self.not_first = jnp.where(lane == 0, 0.0, 0.5)
        self.not_last = jnp.where(lane == NZ - 1, 0.0, 0.5)
        self.ends = jnp.where((lane == 0) | (lane == NZ - 1), 16.0, 0.0)

    def get(self, ref, j):
        return ref[pl.ds(j * self.rows, self.rows), :]

    def put(self, ref, j, value):
        ref[pl.ds(j * self.rows, self.rows), :] = value

    def inside(self, p, value):
        x = lax.axis_index("gx") * CX + p - HALO
        if HALO <= p < HALO + CX:
            keep = self.row_inside
        else:
            keep = (x >= 0) & (x < NX)
            if self.row_inside is not None:
                keep = self.row_inside & keep
        return value if keep is None else jnp.where(keep, value, 0.0)

    def summed(self, ref, j, edge=None):
        f = self.get(ref, j)
        f = (f + f) + (self.get(ref, j - 1) + self.get(ref, j + 1))
        f = (f + f) + (pltpu.roll(f, 1, 0) + pltpu.roll(f, self.rows - 1, 0))
        f = f + (pltpu.roll(f, 1, 1) * self.not_first + pltpu.roll(f, NZ - 1, 1) * self.not_last)
        if edge is not None:
            f = f + self.ends * (0.5 * edge)
        return f + f

    def coefficients(self):
        for p in range(PX):
            label = self.get(self.fields, LAB0 + p)
            k = [jnp.broadcast_to(self.entry(0, e), label.shape) for e in range(6)]
            for m in range(1, LABELS):
                at = label == float(m)
                k = [jnp.where(at, self.entry(m, e), k[e]) for e in range(6)]
            for e in range(6):
                self.put(self.coeff, e * PX + p, k[e])
            self.push(self.flux, p, [self.get(self.fields, c * PX + p) for c in range(3)])
        for p in range(1, PX - 1):
            for e in range(6):
                k = self.get(self.coeff, e * PX + p)
                around = self.summed(self.coeff, e * PX + p, self.entry(0, e))
                self.put(self.total, e * PX + p, 64.0 * k + around)
                if e < 3:
                    self.put(self.scale, e * PX + p, DAMPING / (MASS_SHIFT + 6.0 * k + 0.125 * around))

    def push(self, flux, p, v):
        pushed = times([self.get(self.coeff, e * PX + p) for e in range(6)], v)
        for c in range(3):
            self.put(flux, c * PX + p, pushed[c])

    def image(self, p, v_ref, flux):
        v = [self.get(v_ref, c * PX + p) for c in range(3)]
        k = [self.get(self.coeff, e * PX + p) for e in range(6)]
        m = [self.get(self.total, e * PX + p) for e in range(6)]
        around = [self.summed(v_ref, c * PX + p) for c in range(3)]
        pushed = [self.summed(flux, c * PX + p) for c in range(3)]
        mine, theirs = times(m, v), times(k, around)
        return v, [MASS_SHIFT * v[c] + 0.125 * (mine[c] - theirs[c] - pushed[c]) for c in range(3)]

    def right_side(self, c, p):
        return self.get(self.fields, RHS0 + c * PR + p - 1)

    def sweep(self, first, v_ref, flux, to_ref, to_flux, settle):
        for p in range(first, PX - first):
            v, a = self.image(p, v_ref, flux)
            new = []
            for c in range(3):
                value = v[c] + (self.right_side(c, p) - a[c]) * self.get(self.scale, c * PX + p)
                value = settle(c, p, self.inside(p, value))
                self.put(to_ref, c * PX + p, value)
                new.append(value)
            self.push(to_flux, p, new)

    def restrict(self, v_ref, flux, dense, settled):
        def forced(c, x):
            jump = self.get(v_ref, c * PX + x + HALO) - self.get(v_ref, c * PX + x + HALO + 1)
            value, live = dense(c, x), dense(3, x)
            return jump, jnp.where(live > 0.5, value + PENALTY * jump, 0.0)

        pulled = [forced(c, -1)[1] for c in range(3)]
        sums = []
        for x in range(CX):
            v, a = self.image(x + HALO, v_ref, flux)
            for c in range(3):
                jump, pushed = forced(c, x)
                settled(c, x, v[c], jump)
                part = self.right_side(c, x + HALO) - a[c] - (pushed - pulled[c])
                pulled[c] = pushed
                if x % 2 == 0:
                    sums.append(part)
                else:
                    sums[x // 2 * 3 + c] = sums[x // 2 * 3 + c] + part
        return sums


def to_edge(value, ref, j):
    ref[pl.ds(j * EDGE + HALO, 5), :] = value[:5]
    ref[pl.ds(j * EDGE + 8, 4), :] = value[CY - 4 :]


def inner_part(
    stiffness, disp, rhs, labels, before, after, dense,
    smoothed, jumps, residual, edge_fields, edge_first, edge_second, edge_dense, table,
    fields, coeff, total, scale, flux, first, flux_first, second, flux_second,
):
    near, far = inside_x()
    zero = jnp.zeros((EDGE, NZ), F32)

    def place(j, value):
        fields[pl.ds(j * CY, CY), :] = value
        edge_fields[pl.ds(j * EDGE, EDGE), :] = zero
        to_edge(value, edge_fields, j)

    def part(ref, k):
        return ref[pl.ds(k * CY, CY), :]

    for c in range(3):
        for k in range(HALO):
            place(c * PX + k, near * part(before, c * HALO + k))
            place(c * PX + HALO + CX + k, far * part(after, c * HALO + k))
        for k in range(CX):
            place(c * PX + HALO + k, part(disp, c * CX + k))
            place(RHS0 + c * PR + HALO - 1 + k, part(rhs, c * CX + k))
        for k in range(HALO - 1):
            row = 4 * HALO + c * (HALO - 1) + k
            place(RHS0 + c * PR + k, part(before, row))
            place(RHS0 + c * PR + HALO - 1 + CX + k, part(after, row))
    for k in range(HALO):
        place(LAB0 + k, near * part(before, 3 * HALO + k))
        place(LAB0 + HALO + CX + k, far * part(after, 3 * HALO + k))
    for k in range(CX):
        place(LAB0 + HALO + k, part(labels, k))
    for m in range(LABELS):
        for e in range(6):
            table[pl.ds(m * 6 + e, 1), :] = jnp.full((1, NZ), stiffness[m, e], F32)

    cells = before[pl.ds(IFACE, SLOT_ROWS), :].astype(jnp.int32)
    mult = [before[pl.ds(IFACE + (1 + c) * SLOT_ROWS, SLOT_ROWS), :] for c in range(3)]
    dense_before = spread(cells, mult, (CX - 1) * CY, CY)
    dense_before[3] = dense_before[3] * near
    for i in range(4):
        to_edge(dense_before[i], edge_dense, i * (CX + 1))
        for x in range(CX):
            to_edge(dense[i, pl.ds(x * CY, CY), :], edge_dense, i * (CX + 1) + 1 + x)

    grid = Stencil(CY, lambda m, e: stiffness[m, e], fields, None, (coeff, total, scale, flux))
    grid.coefficients()

    def keep(ref, count):
        def settle(c, p, value):
            to_edge(value, ref, c * count + p - (PX - count) // 2)
            return value

        return settle

    grid.sweep(1, fields, flux, first, flux_first, keep(edge_first, PX - 2))
    grid.sweep(2, first, flux_first, second, flux_second, keep(edge_second, PX - 4))

    def settled(c, x, v, jump):
        smoothed[pl.ds((c * CX + x) * CY, CY), :] = v
        jumps[pl.ds((c * CX + x) * CY, CY), :] = jump

    def cell_values(i, x):
        return dense_before[i] if x < 0 else dense[i, pl.ds(x * CY, CY), :]

    sums = grid.restrict(second, flux_second, cell_values, settled)
    for i in range(6):
        residual[pl.ds(i * CY, CY), :] = sums[i]


def edge_part(
    y_before, y_after, inner_smoothed, inner_jumps, inner_residual,
    edge_fields, edge_first, edge_second, edge_dense, table,
    smoothed, jumps, message,
    fields, coeff, total, scale, flux, first, flux_first, second, flux_second, coarse,
):
    here_y = lax.axis_index("gy")
    low = jnp.where(here_y > 0, 1.0, 0.0).astype(F32)
    high = jnp.where(here_y < N_GY - 1, 1.0, 0.0).astype(F32)
    fields[...] = edge_fields[...]
    for k in range(HALO):
        fields[pl.ds(k, FIELDS, stride=EDGE), :] = low * y_before[k]
        fields[pl.ds(8 + 4 + k, FIELDS, stride=EDGE), :] = high * y_after[k]
    smoothed[...] = inner_smoothed[...]
    jumps[...] = inner_jumps[...]
    coarse[...] = inner_residual[...]

    row = lax.broadcasted_iota(jnp.int32, (EDGE, NZ), 0)
    y = here_y * CY + jnp.where(row < 8, row - HALO, row + CY - 12)
    row_inside = (y >= 0) & (y < NY)

    grid = Stencil(
        EDGE, lambda m, e: table[pl.ds(m * 6 + e, 1), :], fields, row_inside, (coeff, total, scale, flux)
    )
    grid.coefficients()

    def join(ref, count, depth):
        outer = (row < HALO + depth) | (row >= 12 - depth)

        def settle(c, p, value):
            return jnp.where(outer, value, grid.get(ref, c * count + p - (PX - count) // 2))

        return settle

    grid.sweep(1, fields, flux, first, flux_first, join(edge_first, PX - 2, 1))
    grid.sweep(2, first, flux_first, second, flux_second, join(edge_second, PX - 4, 2))

    def settled(c, x, v, jump):
        at = (c * CX + x) * CY
        for ref, value in ((smoothed, v), (jumps, jump)):
            ref[pl.ds(at, 2), :] = value[HALO : HALO + 2]
            ref[pl.ds(at + CY - 2, 2), :] = value[10:12]

    sums = grid.restrict(
        second, flux_second, lambda i, x: grid.get(edge_dense, i * (CX + 1) + 1 + x), settled
    )
    for i in range(6):
        coarse[pl.ds(i * CY, 3), :] = sums[i][HALO : HALO + 3]
        coarse[pl.ds(i * CY + CY - 3, 3), :] = sums[i][9:12]

    out = jnp.zeros((3 * CY // 2, NZ), F32)
    lane_in = lax.broadcasted_iota(jnp.int32, (NZ, NZ), 0)
    lane_out = lax.broadcasted_iota(jnp.int32, (NZ, NZ), 1)
    for x in range(2):
        at = 3 * x * CY
        rows = coarse[pl.ds(at, 3 * CY // 2, stride=2), :] + coarse[pl.ds(at + 1, 3 * CY // 2, stride=2), :]
        pick = jnp.where(lane_in // 2 + x * (NZ // 2) == lane_out, 1.0, 0.0).astype(BF16)
        for piece in pieces_of(rows):
            out = out + jnp.dot(piece, pick, preferred_element_type=F32)
    for s in range(N_GY):
        message[s] = out


def finish(
    cells, mult, jumps, smoothed, gathered,
    smoothed_out, updated_out, coarse_out,
    updated, coarse, done,
):
    copies = [
        pltpu.make_async_copy(smoothed, smoothed_out, done.at[0]),
        pltpu.make_async_copy(coarse, coarse_out, done.at[1]),
        pltpu.make_async_copy(updated, updated_out, done.at[2]),
    ]
    copies[0].start()
    for c in range(3):
        parts = [gathered[s, pl.ds(c * CY // 2, CY // 2), :] for s in range(N_GY)]
        coarse[c] = jnp.transpose(jnp.concatenate(parts, axis=0))
    copies[1].start()
    live = cells[...] >= 0
    column, depth = cells[...] // NZ, cells[...] % NZ
    block = CX * CY
    left = jnp.concatenate(
        [jnp.concatenate(pieces_of(jumps[pl.ds(c * block, block), :]), axis=1) for c in range(3)], axis=0
    )
    for j in range(SLOT_ROWS):
        at_depth = lax.broadcasted_iota(jnp.int32, (NZ, 128), 0) == depth[j : j + 1]
        right = jnp.where(at_depth, 1.0, 0.0).astype(BF16)
        picked = jnp.dot(left, jnp.concatenate([right] * 3, axis=0), preferred_element_type=F32)
        at_column = lax.broadcasted_iota(jnp.int32, (block, 128), 0) == column[j : j + 1]
        for c in range(3):
            jump = jnp.sum(
                jnp.where(at_column, picked[c * block : (c + 1) * block], 0.0), axis=0, keepdims=True
            )
            old = mult[c, j : j + 1, :]
            updated[c, j : j + 1, :] = jnp.where(live[j : j + 1], old + PENALTY * jump, old)
    copies[2].start()
    for copy in copies:
        copy.wait()


def cost(flops, nbytes):
    return pl.CostEstimate(flops=flops, bytes_accessed=nbytes, transcendentals=0)


def in_hbm(array):
    return pltpu.with_memory_space_constraint(array, pltpu.HBM)


def scratch_of(rows):
    wide = pltpu.VMEM((3 * PX * rows, NZ), F32)
    six = pltpu.VMEM((6 * PX * rows, NZ), F32)
    return [pltpu.VMEM((FIELDS * rows, NZ), F32), six, six] + [wide] * 6


def call(kernel, outs, ins, out_specs=None, scratch=(), flops=1_000_000):
    return pl.pallas_call(
        kernel,
        out_shape=outs,
        in_specs=ins,
        out_specs=out_specs or [VMEM] * len(outs),
        scratch_shapes=list(scratch),
        compiler_params=PARAMS,
        cost_estimate=cost(flops, 1_000_000),
    )


def body(displacement, rhs, labels, stiffness, rows, counts, multipliers):
    block = CX * CY
    up, down, disp, rhs, labels, cells, mult = call(
        pack_x,
        [
            f32(UP_ROWS, NZ), f32(SIDE, NZ), f32(3 * block, NZ), f32(3 * block, NZ), f32(block, NZ),
            jax.ShapeDtypeStruct((SLOT_ROWS, 128), jnp.int32), f32(3, SLOT_ROWS, 128),
        ],
        [SMEM] + [HBM] * 5,
        scratch=[
            pltpu.VMEM((block, NZ), jnp.int32),
            pltpu.VMEM((SLOT_ROWS, 128), jnp.int32),
            pltpu.SemaphoreType.DMA((5,)),
        ],
    )(
        counts,
        in_hbm(displacement.reshape(3 * block, NZ)),
        in_hbm(rhs.reshape(3 * block, NZ)),
        in_hbm(labels.reshape(block, NZ)),
        in_hbm(rows.reshape(SLOT_ROWS, 128)),
        in_hbm(multipliers.reshape(3, SLOT_ROWS, 128)),
    )
    ring = [(i, (i + 1) % N_GX) for i in range(N_GX)]
    before = lax.ppermute(up, "gx", ring)
    after = lax.ppermute(down, "gx", [(j, i) for i, j in ring])
    (dense,) = call(spread_own, [f32(4, block, NZ)], [VMEM] * 2, flops=300_000_000)(cells, mult)
    y_up, y_down = call(pack_y, [f32(HALO, FIELDS, NZ)] * 2, [VMEM] * 6)(disp, rhs, labels, before, after, dense)
    ring = [(i, (i + 1) % N_GY) for i in range(N_GY)]
    y_before = lax.ppermute(y_up, "gy", ring)
    y_after = lax.ppermute(y_down, "gy", [(j, i) for i, j in ring])
    inner = call(
        inner_part,
        [
            f32(3 * block, NZ), f32(3 * block, NZ), f32(6 * CY, NZ), f32(FIELDS * EDGE, NZ),
            f32(3 * PR * EDGE, NZ), f32(3 * (PR - 2) * EDGE, NZ), f32(4 * (CX + 1) * EDGE, NZ), f32(LABELS * 6, NZ),
        ],
        [SMEM] + [VMEM] * 6,
        scratch=scratch_of(CY),
        flops=1_000_000_000,
    )(stiffness, disp, rhs, labels, before, after, dense)
    smoothed, jumps, message = call(
        edge_part,
        [f32(3 * block, NZ), f32(3 * block, NZ), f32(N_GY, 3 * CY // 2, NZ)],
        [VMEM] * 10,
        scratch=scratch_of(EDGE) + [pltpu.VMEM((6 * CY, NZ), F32)],
    )(y_before, y_after, *inner)
    gathered = lax.all_to_all(message, "gy", 0, 0)
    smoothed, updated, coarse = call(
        finish,
        [pltpu.HBM(s, F32) for s in ((3 * block, NZ), (3, SLOT_ROWS, 128), (3, CX // 2 * NZ // 2, NY // 2))],
        [VMEM] * 5,
        out_specs=[HBM] * 3,
        scratch=[
            pltpu.VMEM((3, SLOT_ROWS, 128), F32),
            pltpu.VMEM((3, CX // 2 * NZ // 2, NY // 2), F32),
            pltpu.SemaphoreType.DMA((3,)),
        ],
    )(cells, mult, jumps, smoothed, gathered)
    coarse = jnp.swapaxes(coarse.reshape(3, CX // 2, NZ // 2, NY // 2), 2, 3)
    return (smoothed.reshape(3, CX, CY, NZ), coarse, updated.reshape(3, 1, 1, SLOTS))


def solution(mesh):
    return jax.shard_map(
        body,
        mesh=mesh,
        in_specs=(
            P(None, "gx", "gy", None),
            P(None, "gx", "gy", None),
            P("gx", "gy", None),
            P(),
            P("gx", "gy", None),
            P("gx", "gy"),
            P(None, "gx", "gy", None),
        ),
        out_specs=(P(None, "gx", "gy", None), P(None, "gx", None, None), P(None, "gx", "gy", None)),
        check_vma=False,
    )
```

profile of v0, /device:TPU:71, one launch (start us, length us, event | category | flops | bytes accessed | tf_op | source)
XLA Modules:
  0.0 40.9 jit_solution(14627826358515147316)
XLA Ops:
  1.3 1.2 %shard_map.94 = (f32[608,128]{1,0:T(8,128)S(1)}, f32[576,128]{1,0:T(8,128)S(1)}, f32[384,128]{1,0:T(8,128)S(1)}, f32[384,128]{1,0:T(8,128)S(1)}, f32[128,128]{1,...) custom-call(s32[1,1]{1,0:T(1,128)S(6)} %copy.12.count, f32[384,128]{1,0:T(8,128)} %bitcast.10, ...), custom_call_target="tpu_custom_call" | custom-call | flops 1000000 | bytes 1000000 | tf_op jit(solution)/shard_map/pallas_call | solution.py:461
  2.4 4.8 %collective-permute-start = (f32[608,128]{1,0:T(8,128)S(1)}, f32[608,128]{1,0:T(8,128)S(1)}, u32[]{:S(2)}, u32[]{:S(2)}) collective-permute-start(f32[608,128]{1,0:T(8,128)S(1)} %get-tuple-element.31), channel_id=1, source_target_pairs={{0,8},{8,16},{16,24},{24,32},{32,40},{40,48},{48,56},{56,64},{64,7... | collective-permute-start | bytes 933896 | tf_op jit(solution)/shard_map/ppermute | solution.py:482
  7.2 0.0 collective-permute-start.1
  7.2 0.8 %shard_map.95.dense = f32[4,128,128]{2,1,0:T(8,128)S(1)} custom-call(s32[8,128]{1,0:T(8,128)S(1)} %get-tuple-element.26.cells, f32[3,8,128]{2,1,0:T(8,128)S(1)} %get-tuple-element.27.mult), custom_call_target="tpu_custom_call" | custom-call | flops 300000000 | bytes 1000000 | tf_op jit(solution)/shard_map/pallas_call | solution.py:484
  8.1 12.5 %collective-permute-done.1.after = f32[576,128]{1,0:T(8,128)S(1)} collective-permute-done((f32[576,128]{1,0:T(8,128)S(1)}, f32[576,128]{1,0:T(8,128)S(1)}, u32[]{:S(2)}, u32[]{:S(2)}) %collective-permute-start.1) | collective-permute-done | bytes 294944 | tf_op jit(solution)/shard_map/ppermute | solution.py:483
  20.6 0.0 collective-permute-done.before
  20.6 0.0 copy-start
  20.6 0.2 shard_map.96
  20.8 1.4 %collective-permute-start.2 = (f32[3,64,128]{2,1,0:T(8,128)S(1)}, f32[3,64,128]{2,1,0:T(8,128)S(1)}, u32[]{:S(2)}, u32[]{:S(2)}) collective-permute-start(f32[3,64,128]{2,1,0:T(8,128)S(1)} %get-tuple-element.33), channel_id=1, source_target_pairs={{0,1},{1,2},{2,3},{3,4},{4,5},{5,6},{6,7},{7,0},{8,9},{9,10},{10,1... | collective-permute-start | bytes 294920 | tf_op jit(solution)/shard_map/ppermute | solution.py:487
  22.1 2.6 %collective-permute-start.3 = (f32[3,64,128]{2,1,0:T(8,128)S(1)}, f32[3,64,128]{2,1,0:T(8,128)S(1)}, u32[]{:S(2)}, u32[]{:S(2)}) collective-permute-start(f32[3,64,128]{2,1,0:T(8,128)S(1)} %get-tuple-element.34), channel_id=1, source_target_pairs={{1,0},{2,1},{3,2},{4,3},{5,4},{6,5},{7,6},{0,7},{9,8},{10,9},{11,1... | collective-permute-start | bytes 294920 | tf_op jit(solution)/shard_map/ppermute | solution.py:488
  24.7 0.0 copy-done
  24.7 3.4 %shard_map.97 = (f32[384,128]{1,0:T(8,128)S(1)}, f32[384,128]{1,0:T(8,128)S(1)}, f32[192,128]{1,0:T(8,128)S(1)}, f32[1024,128]{1,0:T(8,128)S(1)}, f32[384,128]{1...) custom-call(f32[8,6]{1,0:T(8,128)S(1)} %copy-done, ...), custom_call_target="tpu_custom_call" | custom-call | flops 1000000000 | bytes 1000000 | tf_op jit(solution)/shard_map/pallas_call | solution.py:489
  28.2 0.0 collective-permute-done.2.y_before
  28.2 0.0 collective-permute-done.3.y_after
  28.2 1.6 %shard_map.98 = (f32[384,128]{1,0:T(8,128)S(1)}, f32[384,128]{1,0:T(8,128)S(1)}, f32[8,48,128]{2,1,0:T(8,128)S(1)}) custom-call(f32[3,64,128]{2,1,0:T(8,128)S(1)} %collective-permute-done.2.y_before, f32[3,64,128]{2,1,0:T(8,128)S(1)} %collective-permute-done.3.y_after, f32[384,128]{1,0:T(8,128)S(1)} %get-tuple-element.35.inner_smoothed, ...), custom_call_target="tpu_custom_call" | custom-call | flops 1000000 | bytes 1000000 | tf_op jit(solution)/shard_map/pallas_call | solution.py:499
  29.8 9.6 %all_to_all.5.gathered = f32[8,48,128]{2,1,0:T(8,128)S(1)} all-to-all(f32[8,48,128]{2,1,0:T(8,128)S(1)} %get-tuple-element.45), channel_id=1, replica_groups=mesh['gx'=32,'gy'=8] {'gy'}, dimensions={0} | all-to-all | bytes 393216 | tf_op jit(solution)/shard_map/all_to_all | solution.py:505
  39.4 1.4 %shard_map.99 = (f32[384,128]{1,0:T(8,128)}, f32[3,8,128]{2,1,0:T(8,128)}, f32[3,128,128]{2,1,0:T(8,128)}) custom-call(s32[8,128]{1,0:T(8,128)S(1)} %get-tuple-element.26.cells, f32[3,8,128]{2,1,0:T(8,128)S(1)} %get-tuple-element.27.mult, f32[384,128]{1,0:T(8,128)S(1)} %get-tuple-element.43.jumps, f32[384,128]{1,0:T(8,128)S(1)} %get-tuple-element.44.smoothed, ...), custom_call_target="tpu_custom_call" | custom-call | flops 1000000 | bytes 1000000 | tf_op jit(solution)/shard_map/pallas_call | solution.py:506
Async XLA Ops:
  2.4 18.2 %collective-permute-start = (f32[608,128]{1,0:T(8,128)S(1)}, f32[608,128]{1,0:T(8,128)S(1)}, u32[]{:S(2)}, u32[]{:S(2)}) collective-permute-start(f32[608,128]{1,0:T(8,128)S(1)} %get-tuple-element.31), channel_id=1, source_target_pairs={{0,8},{8,16},{16,24},{24,32},{32,40},{40,48},{48,56},{56,64},{64,7... | collective-permute-start | bytes 933896 | tf_op jit(solution)/shard_map/ppermute | solution.py:482
  7.2 13.4 %collective-permute-start.1 = (f32[576,128]{1,0:T(8,128)S(1)}, f32[576,128]{1,0:T(8,128)S(1)}, u32[]{:S(2)}, u32[]{:S(2)}) collective-permute-start(f32[576,128]{1,0:T(8,128)S(1)} %get-tuple-element.32), channel_id=1, source_target_pairs={{8,0},{16,8},{24,16},{32,24},{40,32},{48,40},{56,48},{64,56},{72,6... | collective-permute-start | bytes 884744 | tf_op jit(solution)/shard_map/ppermute | solution.py:483
  20.6 4.1 %copy-start = (f32[8,6]{1,0:T(8,128)S(1)}, f32[8,6]{1,0:T(8,128)}, u32[]{:S(2)}) copy-start(f32[8,6]{1,0:T(8,128)} %stiffness.1) | copy-start | bytes 580
  20.8 7.4 %collective-permute-start.2 = (f32[3,64,128]{2,1,0:T(8,128)S(1)}, f32[3,64,128]{2,1,0:T(8,128)S(1)}, u32[]{:S(2)}, u32[]{:S(2)}) collective-permute-start(f32[3,64,128]{2,1,0:T(8,128)S(1)} %get-tuple-element.33), channel_id=1, source_target_pairs={{0,1},{1,2},{2,3},{3,4},{4,5},{5,6},{6,7},{7,0},{8,9},{9,10},{10,1... | collective-permute-start | bytes 294920 | tf_op jit(solution)/shard_map/ppermute | solution.py:487
  22.1 6.1 %collective-permute-start.3 = (f32[3,64,128]{2,1,0:T(8,128)S(1)}, f32[3,64,128]{2,1,0:T(8,128)S(1)}, u32[]{:S(2)}, u32[]{:S(2)}) collective-permute-start(f32[3,64,128]{2,1,0:T(8,128)S(1)} %get-tuple-element.34), channel_id=1, source_target_pairs={{1,0},{2,1},{3,2},{4,3},{5,4},{6,5},{7,6},{0,7},{9,8},{10,9},{11,1... | collective-permute-start | bytes 294920 | tf_op jit(solution)/shard_map/ppermute | solution.py:488
where the time goes:
time: 41 us; the launch traced here: 40.9 us
  waiting for transfers between devices  12.6 us (31%)
  blocking collectives  9.64 us (24%)
  starting transfers between devices  8.73 us (21%)
  Pallas kernels  8.6 us (21%)
  between operations  1.33 us (3%)
    ppermute x1, waiting for transfers between devices, body(): after = lax.ppermute(down, 'gx', [(j, i) for i, j in ring])  12.5 us
    all_to_all x1, blocking collectives, body(): gathered = lax.all_to_all(message, 'gy', 0, 0)  9.64 us
    ppermute x1, starting transfers between devices, body(): before = lax.ppermute(up, 'gx', ring)  4.75 us
    pallas_call x1, Pallas kernels, body(): call(inner_part, [f32(3 * block, NZ), f32(3 * block, NZ), f32(6 * CY, NZ)...  3.44 us
    ppermute x1, starting transfers between devices, body(): y_after = lax.ppermute(y_down, 'gy', [(j, i) for i, j in ring])  2.6 us
    pallas_call x1, Pallas kernels, body(): call(edge_part, [f32(3 * block, NZ), f32(3 * block, NZ), f32(N_GY, 3 * CY...  1.57 us
    pallas_call x1, Pallas kernels, body(): call(finish, [pltpu.HBM(s, F32) for s in ((3 * block, NZ), (3, SLOT_ROWS,...  1.44 us
    ppermute x1, starting transfers between devices, body(): y_before = lax.ppermute(y_up, 'gy', ring)  1.37 us
  transfers between devices with their start and end apart: 4, of which 1 were waited for; matrix products, arithmetic and copies ran while one was open for 0% of the time, Pallas kernels for 10%

commit v1 on v0

v1 whole, which is shorter than its diff:
```python
import jax
import jax.numpy as jnp
from jax import lax
from jax.experimental import pallas as pl
from jax.experimental.pallas import tpu as pltpu
from jax.sharding import PartitionSpec as P

SYMMETRIC_INDEX = ((0, 3, 4), (3, 1, 5), (4, 5, 2))
DAMPING = 0.6
MASS_SHIFT = 1.0
PENALTY = 1.0

CX, CY, NZ, SLOTS = 4, 32, 128, 1024
N_GX, N_GY = 32, 8
NX, NY = CX * N_GX, CY * N_GY
LABELS = 8
HALO = 3
PX = CX + 2 * HALO
PR = PX - 2
ROWS = 40
TILE = ROWS - CY
LAB0 = 3 * PX
RHS0 = LAB0 + PX
FIELDS = RHS0 + 3 * PR
OWN_LAB0 = 3 * CX
OWN_RHS0 = OWN_LAB0 + CX
OWN = OWN_RHS0 + 3 * CX
SIDE = 3 * HALO + HALO + 3 * (HALO - 1)
SLOT_ROWS = SLOTS // 128
IFACE = 4 * SLOT_ROWS
VMEM = pl.BlockSpec(memory_space=pltpu.VMEM)
SMEM = pl.BlockSpec(memory_space=pltpu.SMEM)
HBM = pl.BlockSpec(memory_space=pltpu.HBM)
F32 = jnp.float32
BF16 = jnp.bfloat16
PARAMS = pltpu.CompilerParams(vmem_limit_bytes=32 * 1024 * 1024)


def f32(*shape):
    return jax.ShapeDtypeStruct(shape, F32)


def pieces_of(value):
    high = value.astype(BF16)
    rest = value - high.astype(F32)
    middle = rest.astype(BF16)
    low = (rest - middle.astype(F32)).astype(BF16)
    return (high, middle, low)


def odd(axis):
    return lax.rem(lax.axis_index(axis), 2)


def rows_of(j, height):
    return pl.ds(j * height if isinstance(j, int) else pl.multiple_of(j * height, height), height)


def sent_planes():
    place = 0
    for first, depth in [(c * CX, HALO) for c in range(3)] + [(OWN_LAB0, HALO)] + [
        (OWN_RHS0 + c * CX, HALO - 1) for c in range(3)
    ]:
        for k in range(depth):
            yield place, first, k
            place += 1


def halo_planes():
    place = 0
    for first, depth in [(c * PX, HALO) for c in range(3)] + [(LAB0, HALO)] + [
        (RHS0 + c * PR - 1, HALO - 1) for c in range(3)
    ]:
        for k in range(depth):
            yield place, first, k
            place += 1


def slot_number():
    return lax.broadcasted_iota(jnp.int32, (SLOT_ROWS, 128), 0) * 128 + lax.broadcasted_iota(
        jnp.int32, (SLOT_ROWS, 128), 1
    )


def pack_first(
    count, disp, rhs, labels, cells_in, mult_in,
    far, y_pair, y_other, own, cells, mult,
    raw_labels, raw_cells, arrived,
):
    flip = odd("gx")
    pairs = [(cells_in, raw_cells), (mult_in, mult)]
    for g in range(CX):
        x = g + flip * (CX - 1 - 2 * g)
        pairs.append((labels.at[rows_of(x, CY)], raw_labels.at[rows_of(g, CY)]))
        for c in range(3):
            pairs.append((disp.at[rows_of(c * CX + x, CY)], own.at[rows_of(c * CX + g, CY)]))
            pairs.append((rhs.at[rows_of(c * CX + x, CY)], own.at[rows_of(OWN_RHS0 + c * CX + g, CY)]))
    copies = [pltpu.make_async_copy(a, b, arrived.at[i]) for i, (a, b) in enumerate(pairs)]
    for copy in copies:
        copy.start()
    for copy in copies:
        copy.wait()
    block_plane = raw_cells[...] // (CY * NZ)
    turned = raw_cells[...] + flip * (CX - 1 - 2 * block_plane) * (CY * NZ)
    live_cells = jnp.where(slot_number() < count[0, 0], turned, -1)
    cells[...] = live_cells
    own[pl.ds(OWN_LAB0 * CY, CX * CY), :] = raw_labels[...].astype(F32)
    for place, first, k in sent_planes():
        far[rows_of(place, CY), :] = own[rows_of(first + k, CY), :]
    far[pl.ds(SIDE * CY, SLOT_ROWS), :] = live_cells.astype(F32)
    for c in range(3):
        far[pl.ds(SIDE * CY + (1 + c) * SLOT_ROWS, SLOT_ROWS), :] = mult[c]
    up = odd("gy") == 0
    for k in range(HALO):
        first = own[pl.ds(k, OWN, stride=CY), :]
        last = own[pl.ds(CY - HALO + k, OWN, stride=CY), :]
        y_pair[k] = jnp.where(up, last, first)
        y_other[k] = jnp.where(up, first, last)


def pack_second(own, cells, mult, y_pair, y_other, dense, near, corner, wide):
    here = lax.axis_index("gy")
    to = 1 - odd("gx")
    up = odd("gy") == 0
    low = jnp.where(here > 0, 1.0, 0.0).astype(F32)
    high = jnp.where(here < N_GY - 1, 1.0, 0.0).astype(F32)
    for j in range(OWN):
        wide[pl.ds(j * ROWS, CY), :] = own[rows_of(j, CY), :]
    for k in range(HALO):
        after = jnp.where(up, y_pair[k], y_other[k])
        before = jnp.where(up, y_other[k], y_pair[k])
        wide[pl.ds(CY + k, OWN, stride=ROWS), :] = high * after
        wide[pl.ds(ROWS - HALO + k, OWN, stride=ROWS), :] = low * before
    for k in range(CY + HALO, ROWS - HALO):
        wide[pl.ds(k, OWN, stride=ROWS), :] = jnp.zeros((OWN, NZ), F32)
    for place, first, k in sent_planes():
        corner[rows_of(place, TILE), :] = wide[pl.ds((first + k) * ROWS + CY, TILE), :]
        near[to, rows_of(place, ROWS), :] = wide[rows_of(first + CX - 1 - k, ROWS), :]
    near[to, pl.ds(SIDE * ROWS, SLOT_ROWS), :] = cells[...].astype(F32)
    for c in range(3):
        near[to, pl.ds(SIDE * ROWS + (1 + c) * SLOT_ROWS, SLOT_ROWS), :] = mult[c]


def paired(array, j):
    return jnp.concatenate([array[2 * j : 2 * j + 1], array[2 * j + 1 : 2 * j + 2]], axis=1)


def spread(cells, mult, first, columns):
    column = jnp.where(cells < 0, -1, cells // NZ - first)
    depth = cells % NZ
    total = jnp.zeros((10 * columns, NZ), F32)
    parts = [piece for c in range(3) for piece in pieces_of(mult[c])]
    for j in range(SLOT_ROWS // 2):
        at_column = lax.broadcasted_iota(jnp.int32, (columns, 256), 0) == paired(column, j)
        at_depth = lax.broadcasted_iota(jnp.int32, (NZ, 256), 0) == paired(depth, j)
        left = [jnp.where(at_column, paired(piece.astype(F32), j), 0.0).astype(BF16) for piece in parts]
        left.append(jnp.where(at_column, 1.0, 0.0).astype(BF16))
        total = total + lax.dot_general(
            jnp.concatenate(left, axis=0),
            jnp.where(at_depth, 1.0, 0.0).astype(BF16),
            (((1,), (1,)), ((), ())),
            preferred_element_type=F32,
        )
    part = [total[i * columns : (i + 1) * columns] for i in range(10)]
    return [part[3 * c] + part[3 * c + 1] + part[3 * c + 2] for c in range(3)] + [part[9]]


def spread_own(cells, mult, dense):
    values = spread(cells[...], [mult[c] for c in range(3)], 0, CX * CY)
    for i in range(4):
        dense[i] = values[i]


def is_inside():
    here = lax.axis_index("gx")
    return jnp.where((here > 0) & (here < N_GX - 1), 1.0, 0.0).astype(F32)


def spread_before(far, near, dense, last, ribbon):
    flip = odd("gx")

    def at(i):
        a = far[pl.ds(SIDE * CY + i * SLOT_ROWS, SLOT_ROWS), :]
        b = near[0, pl.ds(SIDE * ROWS + i * SLOT_ROWS, SLOT_ROWS), :]
        return jnp.where(flip == 1, b, a)

    values = spread(at(0).astype(jnp.int32), [at(1 + c) for c in range(3)], flip * (CX - 1) * CY, CY)
    values[3] = values[3] * jnp.where(flip == 1, 1.0, is_inside())
    for i in range(4):
        ribbon[i, pl.ds(0, CY), :] = values[i]
        ribbon[i, pl.ds(CY, CX * CY), :] = dense[i]
        ribbon[i, pl.ds((CX + 1) * CY, CY), :] = values[i]


def times(k, v):
    return [
        k[SYMMETRIC_INDEX[c][0]] * v[0] + k[SYMMETRIC_INDEX[c][1]] * v[1] + k[SYMMETRIC_INDEX[c][2]] * v[2]
        for c in range(3)
    ]


class Split:
    def __init__(self, at, low, high):
        self.at, self.low, self.high = at, low, high

    def of(self, c, p, count=PX, base=0):
        ref = self.low if p < self.at else self.high
        return ref, rows_of(base + c * count + p, ROWS)


class Stencil:
    def __init__(self, entry, fields, coeff, total, scale, flux):
        self.entry, self.fields, self.coeff, self.total, self.scale, self.flux = (
            entry, fields, coeff, total, scale, flux
        )
        lane = lax.broadcasted_iota(jnp.int32, (1, NZ), 1)
        self.not_first = jnp.where(lane == 0, 0.0, 0.5)
        self.not_last = jnp.where(lane == NZ - 1, 0.0, 0.5)
        self.ends = jnp.where((lane == 0) | (lane == NZ - 1), 16.0, 0.0)
        row = lax.broadcasted_iota(jnp.int32, (ROWS, NZ), 0)
        y = lax.axis_index("gy") * CY + jnp.where(row < CY + HALO, row, row - ROWS)
        self.row_inside = (y >= 0) & (y < NY) & ((row < CY + HALO) | (row >= ROWS - HALO))

    def get(self, split, c, p):
        ref, at = split.of(c, p)
        return ref[at, :]

    def put(self, split, c, p, value):
        ref, at = split.of(c, p)
        ref[at, :] = value

    def label(self, p):
        ref, at = self.fields.of(0, p, base=LAB0)
        return ref[at, :]

    def right_side(self, c, p):
        ref, at = self.fields.of(c, p, count=PR, base=RHS0 - 1)
        return ref[at, :]

    def summed(self, split, c, p, edge=None):
        f = self.get(split, c, p)
        f = (f + f) + (self.get(split, c, p - 1) + self.get(split, c, p + 1))
        f = (f + f) + (pltpu.roll(f, 1, 0) + pltpu.roll(f, ROWS - 1, 0))
        f = f + (pltpu.roll(f, 1, 1) * self.not_first + pltpu.roll(f, NZ - 1, 1) * self.not_last)
        if edge is not None:
            f = f + self.ends * (0.5 * edge)
        return f + f

    def coefficients(self, planes):
        for p in planes:
            label = self.label(p)
            k = [jnp.broadcast_to(self.entry(0, e), label.shape) for e in range(6)]
            for m in range(1, LABELS):
                at = label == float(m)
                k = [jnp.where(at, self.entry(m, e), k[e]) for e in range(6)]
            for e in range(6):
                self.put(self.coeff, e, p, k[e])
            self.push(self.flux, p, [self.get(self.fields, c, p) for c in range(3)])

    def weights(self, planes):
        for p in planes:
            for e in range(6):
                k = self.get(self.coeff, e, p)
                around = self.summed(self.coeff, e, p, self.entry(0, e))
                self.put(self.total, e, p, 64.0 * k + around)
                if e < 3:
                    self.put(self.scale, e, p, DAMPING / (MASS_SHIFT + 6.0 * k + 0.125 * around))

    def push(self, flux, p, v):
        pushed = times([self.get(self.coeff, e, p) for e in range(6)], v)
        for c in range(3):
            self.put(flux, c, p, pushed[c])

    def image(self, p, v_split, flux):
        v = [self.get(v_split, c, p) for c in range(3)]
        k = [self.get(self.coeff, e, p) for e in range(6)]
        m = [self.get(self.total, e, p) for e in range(6)]
        around = [self.summed(v_split, c, p) for c in range(3)]
        pushed = [self.summed(flux, c, p) for c in range(3)]
        mine, theirs = times(m, v), times(k, around)
        return v, [MASS_SHIFT * v[c] + 0.125 * (mine[c] - theirs[c] - pushed[c]) for c in range(3)]

    def sweep(self, planes, v_split, flux, to, to_flux, inside=None):
        for p in planes:
            keep = self.row_inside if p >= HALO else self.row_inside & (inside > 0.5)
            v, a = self.image(p, v_split, flux)
            new = []
            for c in range(3):
                value = v[c] + (self.right_side(c, p) - a[c]) * self.get(self.scale, c, p)
                value = jnp.where(keep, value, 0.0)
                self.put(to, c, p, value)
                new.append(value)
            self.push(to_flux, p, new)

    def remainder(self, p, v_split, flux):
        a = self.image(p, v_split, flux)[1]
        return [(self.right_side(c, p) - a[c])[:CY] for c in range(3)]


def near_part(
    stiffness, own, near,
    fields, coeff, total, scale, flux, first, flux_first, second, flux_second, table, last,
):
    sent = 1 - odd("gx")
    for c in range(3):
        for g in range(CX):
            fields[rows_of(c * PX + HALO + g, ROWS), :] = own[rows_of(c * CX + g, ROWS), :]
            fields[rows_of(RHS0 - 1 + c * PR + HALO + g, ROWS), :] = own[rows_of(OWN_RHS0 + c * CX + g, ROWS), :]
    for g in range(CX):
        fields[rows_of(LAB0 + HALO + g, ROWS), :] = own[rows_of(OWN_LAB0 + g, ROWS), :]
    for place, at, k in halo_planes():
        fields[rows_of(at + HALO + CX + k, ROWS), :] = near[sent, rows_of(place, ROWS), :]
    for m in range(LABELS):
        for e in range(6):
            table[pl.ds(m * 6 + e, 1), :] = jnp.full((1, NZ), stiffness[m, e], F32)

    def whole(ref):
        return Split(0, None, ref)

    grid = Stencil(
        lambda m, e: stiffness[m, e], whole(fields), whole(coeff), whole(total), whole(scale), whole(flux)
    )
    grid.coefficients(range(HALO, PX))
    grid.weights(range(HALO + 1, PX - 1))
    grid.sweep(range(HALO + 1, PX - 1), whole(fields), whole(flux), whole(first), whole(flux_first))
    grid.sweep(range(HALO + 2, PX - 2), whole(first), whole(flux_first), whole(second), whole(flux_second))
    remainder = grid.remainder(HALO + 3, whole(second), whole(flux_second))
    for c in range(3):
        last[rows_of(c, CY), :] = remainder[c]


def far_part(
    far, corner, ribbon,
    near_fields, near_coeff, near_total, near_scale, near_flux,
    near_first, near_flux_first, near_second, near_flux_second, table, last,
    smoothed, jumps, message,
    fields, coeff, total, scale, flux, first, flux_first, second, flux_second, coarse,
):
    inside = is_inside()
    flip = odd("gx")
    sign = jnp.where(flip == 1, -1.0, 1.0).astype(F32)
    for place, at, k in halo_planes():
        plane = (at + HALO - 1 - k) * ROWS
        fields[pl.ds(plane, CY), :] = inside * far[rows_of(place, CY), :]
        fields[pl.ds(plane + CY, TILE), :] = inside * corner[rows_of(place, TILE), :]
    v0, flux0 = Split(HALO, fields, near_fields), Split(HALO, flux, near_flux)
    v1, flux1 = Split(HALO + 1, first, near_first), Split(HALO + 1, flux_first, near_flux_first)
    v2, flux2 = Split(HALO + 2, second, near_second), Split(HALO + 2, flux_second, near_flux_second)
    grid = Stencil(
        lambda m, e: table[pl.ds(m * 6 + e, 1), :],
        v0,
        Split(HALO, coeff, near_coeff),
        Split(HALO + 1, total, near_total),
        Split(HALO + 1, scale, near_scale),
        flux0,
    )
    grid.coefficients(range(HALO))
    grid.weights(range(1, HALO + 1))
    grid.sweep(range(1, HALO + 1), v0, flux0, v1, flux1, inside)
    grid.sweep(range(2, HALO + 2), v1, flux1, v2, flux2, inside)
    remainders = [grid.remainder(HALO + g, v2, flux2) for g in range(CX - 1)]
    remainders.append([last[rows_of(c, CY), :] for c in range(3)])

    for c in range(3):
        planes = [grid.get(v2, c, HALO - 1 + i)[:CY] for i in range(CX + 2)]
        for g in range(CX):
            x = g + flip * (CX - 1 - 2 * g)
            smoothed[rows_of(c * CX + x, CY), :] = planes[1 + g]
        pushed = []
        for i in range(CX + 1):
            jump = sign * (planes[i] - planes[i + 1])
            jumps[c, rows_of(i, CY), :] = jump
            at = rows_of(i + flip, CY)
            pushed.append(jnp.where(ribbon[3, at, :] > 0.5, ribbon[c, at, :] + PENALTY * jump, 0.0))
        parts = [remainders[g][c] - sign * (pushed[g + 1] - pushed[g]) for g in range(CX)]
        for half in range(2):
            coarse[rows_of(half * 3 + c, CY), :] = parts[2 * half] + parts[2 * half + 1]

    out = jnp.zeros((3 * CY // 2, NZ), F32)
    lane_in = lax.broadcasted_iota(jnp.int32, (NZ, NZ), 0)
    lane_out = lax.broadcasted_iota(jnp.int32, (NZ, NZ), 1)
    for half in range(2):
        at = 3 * half * CY
        rows = coarse[pl.ds(at, 3 * CY // 2, stride=2), :] + coarse[pl.ds(at + 1, 3 * CY // 2, stride=2), :]
        x = half + flip * (1 - 2 * half)
        pick = jnp.where(lane_in // 2 + x * (NZ // 2) == lane_out, 1.0, 0.0).astype(BF16)
        for piece in pieces_of(rows):
            out = out + jnp.dot(piece, pick, preferred_element_type=F32)
    for s in range(N_GY):
        message[s] = out


def finish(
    cells, mult, jumps, smoothed, gathered,
    smoothed_out, updated_out, coarse_out,
    updated, coarse, done,
):
    copies = [
        pltpu.make_async_copy(smoothed, smoothed_out, done.at[0]),
        pltpu.make_async_copy(coarse, coarse_out, done.at[1]),
        pltpu.make_async_copy(updated, updated_out, done.at[2]),
    ]
    copies[0].start()
    for c in range(3):
        parts = [gathered[s, pl.ds(c * CY // 2, CY // 2), :] for s in range(N_GY)]
        coarse[c] = jnp.transpose(jnp.concatenate(parts, axis=0))
    copies[1].start()
    live = cells[...] >= 0
    column, depth = cells[...] // NZ, cells[...] % NZ
    block = CX * CY
    start = pl.multiple_of((1 - odd("gx")) * CY, CY)
    left = jnp.concatenate(
        [jnp.concatenate(pieces_of(jumps[c, pl.ds(start, block), :]), axis=1) for c in range(3)], axis=0
    )
    for j in range(SLOT_ROWS):
        at_depth = lax.broadcasted_iota(jnp.int32, (NZ, 128), 0) == depth[j : j + 1]
        right = jnp.where(at_depth, 1.0, 0.0).astype(BF16)
        picked = jnp.dot(left, jnp.concatenate([right] * 3, axis=0), preferred_element_type=F32)
        at_column = lax.broadcasted_iota(jnp.int32, (block, 128), 0) == column[j : j + 1]
        for c in range(3):
            jump = jnp.sum(
                jnp.where(at_column, picked[c * block : (c + 1) * block], 0.0), axis=0, keepdims=True
            )
            old = mult[c, j : j + 1, :]
            updated[c, j : j + 1, :] = jnp.where(live[j : j + 1], old + PENALTY * jump, old)
    copies[2].start()
    for copy in copies:
        copy.wait()


def in_hbm(array):
    return pltpu.with_memory_space_constraint(array, pltpu.HBM)


def call(kernel, outs, ins, out_specs=None, scratch=()):
    return pl.pallas_call(
        kernel,
        out_shape=outs,
        in_specs=ins,
        out_specs=out_specs or [VMEM] * len(outs),
        scratch_shapes=list(scratch),
        compiler_params=PARAMS,
        cost_estimate=pl.CostEstimate(flops=1000, bytes_accessed=1000, transcendentals=0),
    )


def pair(n):
    return [(i, i ^ 1) for i in range(n)]


def other(n):
    return [(i, (((i + 1) % n ^ 1) - 1) % n) for i in range(n)]


def body(displacement, rhs, labels, stiffness, rows, counts, multipliers):
    block = CX * CY
    copies = 2 + 7 * CX
    far, y_pair, y_other, own, cells, mult = call(
        pack_first,
        [
            f32(SIDE * CY + IFACE, NZ), f32(HALO, OWN, NZ), f32(HALO, OWN, NZ), f32(OWN * CY, NZ),
            jax.ShapeDtypeStruct((SLOT_ROWS, 128), jnp.int32), f32(3, SLOT_ROWS, 128),
        ],
        [SMEM] + [HBM] * 5,
        scratch=[
            pltpu.VMEM((block, NZ), jnp.int32),
            pltpu.VMEM((SLOT_ROWS, 128), jnp.int32),
            pltpu.SemaphoreType.DMA((copies,)),
        ],
    )(
        counts,
        in_hbm(displacement.reshape(3 * block, NZ)),
        in_hbm(rhs.reshape(3 * block, NZ)),
        in_hbm(labels.reshape(block, NZ)),
        in_hbm(rows.reshape(SLOT_ROWS, 128)),
        in_hbm(multipliers.reshape(3, SLOT_ROWS, 128)),
    )
    far = lax.ppermute(far, "gx", other(N_GX))
    y_other = lax.ppermute(y_other, "gy", other(N_GY))
    y_pair = lax.ppermute(y_pair, "gy", pair(N_GY))
    (dense,) = call(spread_own, [f32(4, block, NZ)], [VMEM] * 2)(cells, mult)
    near, corner, own = call(
        pack_second, [f32(2, SIDE * ROWS + IFACE, NZ), f32(SIDE * TILE, NZ), f32(OWN * ROWS, NZ)], [VMEM] * 6
    )(own, cells, mult, y_pair, y_other, dense)
    corner = lax.ppermute(corner, "gx", other(N_GX))
    near = lax.all_to_all(near, "gx", 0, 0, axis_index_groups=[[i, i + 1] for i in range(0, N_GX, 2)])
    three, six = f32(3 * PX * ROWS, NZ), f32(6 * PX * ROWS, NZ)
    arrays = [f32(FIELDS * ROWS, NZ), six, six] + [three] * 6
    half = call(
        near_part, arrays + [f32(LABELS * 6, NZ), f32(3 * CY, NZ)], [SMEM, VMEM, VMEM]
    )(stiffness, own, near)
    (ribbon,) = call(spread_before, [f32(4, (CX + 2) * CY, NZ)], [VMEM] * 4)(far, near, dense, half[-1])
    smoothed, jumps, message = call(
        far_part,
        [f32(3 * block, NZ), f32(3, (CX + 1) * CY, NZ), f32(N_GY, 3 * CY // 2, NZ)],
        [VMEM] * (3 + len(half)),
        scratch=[pltpu.VMEM(a.shape, F32) for a in arrays] + [pltpu.VMEM((6 * CY, NZ), F32)],
    )(far, corner, ribbon, *half)
    gathered = lax.all_to_all(message, "gy", 0, 0)
    smoothed, updated, coarse = call(
        finish,
        [pltpu.HBM(s, F32) for s in ((3 * block, NZ), (3, SLOT_ROWS, 128), (3, CX // 2 * NZ // 2, NY // 2))],
        [VMEM] * 5,
        out_specs=[HBM] * 3,
        scratch=[
            pltpu.VMEM((3, SLOT_ROWS, 128), F32),
            pltpu.VMEM((3, CX // 2 * NZ // 2, NY // 2), F32),
            pltpu.SemaphoreType.DMA((3,)),
        ],
    )(cells, mult, jumps, smoothed, gathered)
    coarse = jnp.swapaxes(coarse.reshape(3, CX // 2, NZ // 2, NY // 2), 2, 3)
    return (smoothed.reshape(3, CX, CY, NZ), coarse, updated.reshape(3, 1, 1, SLOTS))


def solution(mesh):
    return jax.shard_map(
        body,
        mesh=mesh,
        in_specs=(
            P(None, "gx", "gy", None),
            P(None, "gx", "gy", None),
            P("gx", "gy", None),
            P(),
            P("gx", "gy", None),
            P("gx", "gy"),
            P(None, "gx", "gy", None),
        ),
        out_specs=(P(None, "gx", "gy", None), P(None, "gx", None, None), P(None, "gx", "gy", None)),
        check_vma=False,
    )
```

time: 41 us -> 41.4 us (level)
  the two profiles are of different devices: /device:TPU:71 before, /device:TPU:1 now
where the time goes in v1:
time: 41.4 us; the launch traced here: 41.1 us
  blocking collectives  21.3 us (51%)
  starting transfers between devices  9.12 us (22%)
  Pallas kernels  8.4 us (20%)
  between operations  1.36 us (3%)
  waiting for transfers between devices  0.92 us (2%)
    all_to_all x1, blocking collectives, body(): lax.all_to_all(near, 'gx', 0, 0, axis_index_groups=[[i, i + 1] for i in r...  12.7 us
    all_to_all x1, blocking collectives, body(): gathered = lax.all_to_all(message, 'gy', 0, 0)  8.66 us
    ppermute x1, starting transfers between devices, body(): y_other = lax.ppermute(y_other, 'gy', other(N_GY))  3.25 us
    ppermute x1, starting transfers between devices, body(): far = lax.ppermute(far, 'gx', other(N_GX))  2.69 us
    pallas_call x1, Pallas kernels, body(): call(near_part, arrays + [f32(LABELS * 6, NZ), f32(3 * CY, NZ)], [SMEM, V...  2.63 us
    ppermute x1, starting transfers between devices, body(): corner = lax.ppermute(corner, 'gx', other(N_GX))  1.89 us
    pallas_call x1, Pallas kernels, body(): call(far_part, [f32(3 * block, NZ), f32(3, (CX + 1) * CY, NZ), f32(N_GY,...  1.69 us
    pallas_call x1, Pallas kernels, body(): call(finish, [pltpu.HBM(s, F32) for s in ((3 * block, NZ), (3, SLOT_ROWS,...  1.44 us
  transfers between devices with their start and end apart: 4, of which 1 were waited for; matrix products, arithmetic and copies ran while one was open for 0% of the time, Pallas kernels for 10%

profile of v1, /device:TPU:1, one launch (start us, length us, event | category | flops | bytes accessed | tf_op | source)
XLA Modules:
  0.0 41.1 jit_solution(11242662285585718236)
XLA Ops:
  1.3 1.3 %shard_map.94 = (f32[608,128]{1,0:T(8,128)S(1)}, f32[3,28,128]{2,1,0:T(8,128)S(1)}, f32[3,28,128]{2,1,0:T(8,128)S(1)}, f32[896,128]{1,0:T(8,128)S(1)}, s32[8,128]{1,0:T(8,128)S(1)}, /*index=5*/f32[3,8,128]{2,1,0:T(8,128)S(1)}) custom-call(s32[1,1]{1,0:T(1,128)S(6)} %copy.12.count, f32[384,128]{1,0:T(8,128)} %bitcast.10, f32[384,128]{1,0:T(8,128)} %bitcast.11, ...), custom_call_target="tpu_custom_call" | custom-call | flops 1000 | bytes 1000 | tf_op jit(solution)/shard_map/pallas_call | solution.py:458
  2.6 2.7 %collective-permute-start = (f32[608,128]{1,0:T(8,128)S(1)}, f32[608,128]{1,0:T(8,128)S(1)}, u32[]{:S(2)}, u32[]{:S(2)}) collective-permute-start(f32[608,128]{1,0:T(8,128)S(1)} %get-tuple-element.31), channel_id=1, source_target_pairs={{0,248},{8,16},{16,8},{24,32},{32,24},{40,48},{48,40},{56,64},{64,... | collective-permute-start | bytes 933896 | tf_op jit(solution)/shard_map/ppermute | solution.py:478
  5.3 1.3 %collective-permute-start.1 = (f32[3,28,128]{2,1,0:T(8,128)S(1)}, f32[3,28,128]{2,1,0:T(8,128)S(1)}, u32[]{:S(2)}, u32[]{:S(2)}) collective-permute-start(f32[3,28,128]{2,1,0:T(8,128)S(1)} %get-tuple-element.33), channel_id=1, source_target_pairs={{0,1},{1,0},{2,3},{3,2},{4,5},{5,4},{6,7},{7,6},{8,9},{9,8},{10,11... | collective-permute-start | bytes 129032 | tf_op jit(solution)/shard_map/ppermute | solution.py:480
  6.6 3.3 %collective-permute-start.2 = (f32[3,28,128]{2,1,0:T(8,128)S(1)}, f32[3,28,128]{2,1,0:T(8,128)S(1)}, u32[]{:S(2)}, u32[]{:S(2)}) collective-permute-start(f32[3,28,128]{2,1,0:T(8,128)S(1)} %get-tuple-element.34), channel_id=1, source_target_pairs={{0,7},{1,2},{2,1},{3,4},{4,3},{5,6},{6,5},{7,0},{8,15},{9,10},{10,... | collective-permute-start | bytes 129032 | tf_op jit(solution)/shard_map/ppermute | solution.py:479
  9.9 0.8 %shard_map.95.dense = f32[4,128,128]{2,1,0:T(8,128)S(1)} custom-call(s32[8,128]{1,0:T(8,128)S(1)} %get-tuple-element.29.cells, f32[3,8,128]{2,1,0:T(8,128)S(1)} %get-tuple-element.30.mult), custom_call_target="tpu_custom_call" | custom-call | flops 1000 | bytes 1000 | tf_op jit(solution)/shard_map/pallas_call | solution.py:481
  10.7 0.0 copy-start
  10.7 0.0 collective-permute-done.1.y_pair
  10.7 0.9 %collective-permute-done.2.y_other = f32[3,28,128]{2,1,0:T(8,128)S(1)} collective-permute-done((f32[3,28,128]{2,1,0:T(8,128)S(1)}, f32[3,28,128]{2,1,0:T(8,128)S(1)}, u32[]{:S(2)}, u32[]{:S(2)}) %collective-permute-start.2) | collective-permute-done | bytes 43040 | tf_op jit(solution)/shard_map/ppermute | solution.py:479
  11.7 0.1 shard_map.96
  11.7 1.9 %collective-permute-start.3 = (f32[144,128]{1,0:T(8,128)S(1)}, f32[144,128]{1,0:T(8,128)S(1)}, u32[]{:S(2)}, u32[]{:S(2)}) collective-permute-start(f32[144,128]{1,0:T(8,128)S(1)} %get-tuple-element.35), channel_id=1, source_target_pairs={{0,248},{8,16},{16,8},{24,32},{32,24},{40,48},{48,40},{56,64},{64,... | collective-permute-start | bytes 221192 | tf_op jit(solution)/shard_map/ppermute | solution.py:485
  13.6 12.7 %all_to_all.10.near = f32[2,752,128]{2,1,0:T(8,128)S(1)} all-to-all(f32[2,752,128]{2,1,0:T(8,128)S(1)} %get-tuple-element.36), channel_id=1, replica_groups={{0,8},{16,24},{32,40},{48,56},{64,72},{80,88},{96,104},{112,120},{128,1..., dimensions={0} | all-to-all | bytes 1540096 | tf_op jit(solution)/shard_map/all_to_all | solution.py:486
  26.3 0.0 copy-done
  26.3 2.6 %shard_map.97 = (f32[2560,128]{1,0:T(8,128)S(1)}, f32[2400,128]{1,0:T(8,128)S(1)}, f32[2400,128]{1,0:T(8,128)S(1)}, f32[1200,128]{1,0:T(8,128)S(1)}, f32[1200,12...) custom-call(f32[8,6]{1,0:T(8,128)S(1)} %copy-done, ...), custom_call_target="tpu_custom_call" | custom-call | flops 1000 | bytes 1000 | tf_op jit(solution)/shard_map/pallas_call | solution.py:489
  28.9 0.0 collective-permute-done.far
  28.9 0.4 shard_map.98.ribbon
  29.3 0.0 collective-permute-done.3.corner
  29.3 1.7 %shard_map.99 = (f32[384,128]{1,0:T(8,128)S(1)}, f32[3,160,128]{2,1,0:T(8,128)S(1)}, f32[8,48,128]{2,1,0:T(8,128)S(1)}) custom-call(f32[608,128]{1,0:T(8,128)S(1)} %collective-permute-done.far, f32[144,128]{1,0:T(8,128)S(1)} %collective-permute-done.3.corner, f32[4,192,128]{2,1,0:T(8,128)S(1)} %shard_map.98.ribbon, ...), custom_call_target="tpu_custom_call" | custom-call | flops 1000 | bytes 1000 | tf_op jit(solution)/shard_map/pallas_call | solution.py:493
  31.0 8.7 %all_to_all.11.gathered = f32[8,48,128]{2,1,0:T(8,128)S(1)} all-to-all(f32[8,48,128]{2,1,0:T(8,128)S(1)} %get-tuple-element.51), channel_id=1, replica_groups=mesh['gx'=32,'gy'=8] {'gy'}, dimensions={0} | all-to-all | bytes 393216 | tf_op jit(solution)/shard_map/all_to_all | solution.py:499
  39.7 1.4 %shard_map.100 = (f32[384,128]{1,0:T(8,128)}, f32[3,8,128]{2,1,0:T(8,128)}, f32[3,128,128]{2,1,0:T(8,128)}) custom-call(s32[8,128]{1,0:T(8,128)S(1)} %get-tuple-element.29.cells, f32[3,8,128]{2,1,0:T(8,128)S(1)} %get-tuple-element.30.mult, f32[3,160,128]{2,1,0:T(8,128)S(1)} %get-tuple-element.49.jumps, f32[384,128]{1,0:T(8,128)S(1)} %get-tuple-element.50.smoothed, ...), custom_call_target="tpu_custom_call" | custom-call | flops 1000 | bytes 1000 | tf_op jit(solution)/shard_map/pallas_call | solution.py:500
Async XLA Ops:
  2.6 26.3 %collective-permute-start = (f32[608,128]{1,0:T(8,128)S(1)}, f32[608,128]{1,0:T(8,128)S(1)}, u32[]{:S(2)}, u32[]{:S(2)}) collective-permute-start(f32[608,128]{1,0:T(8,128)S(1)} %get-tuple-element.31), channel_id=1, source_target_pairs={{0,248},{8,16},{16,8},{24,32},{32,24},{40,48},{48,40},{56,64},{64,... | collective-permute-start | bytes 933896 | tf_op jit(solution)/shard_map/ppermute | solution.py:478
  5.3 5.4 %collective-permute-start.1 = (f32[3,28,128]{2,1,0:T(8,128)S(1)}, f32[3,28,128]{2,1,0:T(8,128)S(1)}, u32[]{:S(2)}, u32[]{:S(2)}) collective-permute-start(f32[3,28,128]{2,1,0:T(8,128)S(1)} %get-tuple-element.33), channel_id=1, source_target_pairs={{0,1},{1,0},{2,3},{3,2},{4,5},{5,4},{6,7},{7,6},{8,9},{9,8},{10,11... | collective-permute-start | bytes 129032 | tf_op jit(solution)/shard_map/ppermute | solution.py:480
  6.6 5.0 %collective-permute-start.2 = (f32[3,28,128]{2,1,0:T(8,128)S(1)}, f32[3,28,128]{2,1,0:T(8,128)S(1)}, u32[]{:S(2)}, u32[]{:S(2)}) collective-permute-start(f32[3,28,128]{2,1,0:T(8,128)S(1)} %get-tuple-element.34), channel_id=1, source_target_pairs={{0,7},{1,2},{2,1},{3,4},{4,3},{5,6},{6,5},{7,0},{8,15},{9,10},{10,... | collective-permute-start | bytes 129032 | tf_op jit(solution)/shard_map/ppermute | solution.py:479
  10.7 15.6 %copy-start = (f32[8,6]{1,0:T(8,128)S(1)}, f32[8,6]{1,0:T(8,128)}, u32[]{:S(2)}) copy-start(f32[8,6]{1,0:T(8,128)} %stiffness.1) | copy-start | bytes 580
  11.7 17.6 %collective-permute-start.3 = (f32[144,128]{1,0:T(8,128)S(1)}, f32[144,128]{1,0:T(8,128)S(1)}, u32[]{:S(2)}, u32[]{:S(2)}) collective-permute-start(f32[144,128]{1,0:T(8,128)S(1)} %get-tuple-element.35), channel_id=1, source_target_pairs={{0,248},{8,16},{16,8},{24,32},{32,24},{40,48},{48,40},{56,64},{64,... | collective-permute-start | bytes 221192 | tf_op jit(solution)/shard_map/ppermute | solution.py:485

commit v2 on v1

--- a/solution.py
+++ b/solution.py
@@ -118,9 +118,8 @@
         y_other[k] = jnp.where(up, first, last)
 
 
-def pack_second(own, cells, mult, y_pair, y_other, dense, near, corner, wide):
+def pack_second(own, cells, mult, y_pair, y_other, near, corner, wide):
     here = lax.axis_index("gy")
-    to = 1 - odd("gx")
     up = odd("gy") == 0
     low = jnp.where(here > 0, 1.0, 0.0).astype(F32)
     high = jnp.where(here < N_GY - 1, 1.0, 0.0).astype(F32)
@@ -135,10 +134,10 @@
         wide[pl.ds(k, OWN, stride=ROWS), :] = jnp.zeros((OWN, NZ), F32)
     for place, first, k in sent_planes():
         corner[rows_of(place, TILE), :] = wide[pl.ds((first + k) * ROWS + CY, TILE), :]
-        near[to, rows_of(place, ROWS), :] = wide[rows_of(first + CX - 1 - k, ROWS), :]
-    near[to, pl.ds(SIDE * ROWS, SLOT_ROWS), :] = cells[...].astype(F32)
+        near[rows_of(place, ROWS), :] = wide[rows_of(first + CX - 1 - k, ROWS), :]
+    near[pl.ds(SIDE * ROWS, SLOT_ROWS), :] = cells[...].astype(F32)
     for c in range(3):
-        near[to, pl.ds(SIDE * ROWS + (1 + c) * SLOT_ROWS, SLOT_ROWS), :] = mult[c]
+        near[pl.ds(SIDE * ROWS + (1 + c) * SLOT_ROWS, SLOT_ROWS), :] = mult[c]
 
 
 def paired(array, j):
@@ -181,7 +180,7 @@
 
     def at(i):
         a = far[pl.ds(SIDE * CY + i * SLOT_ROWS, SLOT_ROWS), :]
-        b = near[0, pl.ds(SIDE * ROWS + i * SLOT_ROWS, SLOT_ROWS), :]
+        b = near[pl.ds(SIDE * ROWS + i * SLOT_ROWS, SLOT_ROWS), :]
         return jnp.where(flip == 1, b, a)
 
     values = spread(at(0).astype(jnp.int32), [at(1 + c) for c in range(3)], flip * (CX - 1) * CY, CY)
@@ -301,7 +300,6 @@
     stiffness, own, near,
     fields, coeff, total, scale, flux, first, flux_first, second, flux_second, table, last,
 ):
-    sent = 1 - odd("gx")
     for c in range(3):
         for g in range(CX):
             fields[rows_of(c * PX + HALO + g, ROWS), :] = own[rows_of(c * CX + g, ROWS), :]
@@ -309,7 +307,7 @@
     for g in range(CX):
         fields[rows_of(LAB0 + HALO + g, ROWS), :] = own[rows_of(OWN_LAB0 + g, ROWS), :]
     for place, at, k in halo_planes():
-        fields[rows_of(at + HALO + CX + k, ROWS), :] = near[sent, rows_of(place, ROWS), :]
+        fields[rows_of(at + HALO + CX + k, ROWS), :] = near[rows_of(place, ROWS), :]
     for m in range(LABELS):
         for e in range(6):
             table[pl.ds(m * 6 + e, 1), :] = jnp.full((1, NZ), stiffness[m, e], F32)
@@ -432,7 +430,7 @@
     return pltpu.with_memory_space_constraint(array, pltpu.HBM)
 
 
-def call(kernel, outs, ins, out_specs=None, scratch=()):
+def call(kernel, outs, ins, out_specs=None, scratch=(), flops=1000):
     return pl.pallas_call(
         kernel,
         out_shape=outs,
@@ -440,7 +438,7 @@
         out_specs=out_specs or [VMEM] * len(outs),
         scratch_shapes=list(scratch),
         compiler_params=PARAMS,
-        cost_estimate=pl.CostEstimate(flops=1000, bytes_accessed=1000, transcendentals=0),
+        cost_estimate=pl.CostEstimate(flops=flops, bytes_accessed=1000, transcendentals=0),
     )
 
 
@@ -478,12 +476,12 @@
     far = lax.ppermute(far, "gx", other(N_GX))
     y_other = lax.ppermute(y_other, "gy", other(N_GY))
     y_pair = lax.ppermute(y_pair, "gy", pair(N_GY))
-    (dense,) = call(spread_own, [f32(4, block, NZ)], [VMEM] * 2)(cells, mult)
+    (dense,) = call(spread_own, [f32(4, block, NZ)], [VMEM] * 2, flops=100000000000)(cells, mult)
     near, corner, own = call(
-        pack_second, [f32(2, SIDE * ROWS + IFACE, NZ), f32(SIDE * TILE, NZ), f32(OWN * ROWS, NZ)], [VMEM] * 6
-    )(own, cells, mult, y_pair, y_other, dense)
+        pack_second, [f32(SIDE * ROWS + IFACE, NZ), f32(SIDE * TILE, NZ), f32(OWN * ROWS, NZ)], [VMEM] * 5
+    )(own, cells, mult, y_pair, y_other)
     corner = lax.ppermute(corner, "gx", other(N_GX))
-    near = lax.all_to_all(near, "gx", 0, 0, axis_index_groups=[[i, i + 1] for i in range(0, N_GX, 2)])
+    near = lax.ppermute(near, "gx", pair(N_GX))
     three, six = f32(3 * PX * ROWS, NZ), f32(6 * PX * ROWS, NZ)
     arrays = [f32(FIELDS * ROWS, NZ), six, six] + [three] * 6
     half = call(

time: 41.4 us -> 36.6 us (0.88)
  the two profiles are of different devices: /device:TPU:1 before, /device:TPU:8 now
where the time goes in v2:
time: 36.6 us; the launch traced here: 36.4 us
  starting transfers between devices  13.7 us (37%)
  blocking collectives  11 us (30%)
  Pallas kernels  8.44 us (23%)
  waiting for transfers between devices  1.92 us (5%)
  between operations  1.36 us (4%)
    all_to_all x1, blocking collectives, body(): gathered = lax.all_to_all(message, 'gy', 0, 0)  11 us
    ppermute x1, starting transfers between devices, body(): far = lax.ppermute(far, 'gx', other(N_GX))  7.37 us
    ppermute x1, starting transfers between devices, body(): corner = lax.ppermute(corner, 'gx', other(N_GX))  3.27 us
    pallas_call x1, Pallas kernels, body(): call(near_part, arrays + [f32(LABELS * 6, NZ), f32(3 * CY, NZ)], [SMEM, V...  2.68 us
    ppermute x1, starting transfers between devices, body(): y_pair = lax.ppermute(y_pair, 'gy', pair(N_GY))  2.27 us
    pallas_call x1, Pallas kernels, body(): call(far_part, [f32(3 * block, NZ), f32(3, (CX + 1) * CY, NZ), f32(N_GY,...  1.69 us
    ppermute x1, waiting for transfers between devices, body(): far = lax.ppermute(far, 'gx', other(N_GX))  1.54 us
    pallas_call x1, Pallas kernels, body(): call(finish, [pltpu.HBM(s, F32) for s in ((3 * block, NZ), (3, SLOT_ROWS,...  1.44 us
  transfers between devices with their start and end apart: 5, of which 2 were waited for; matrix products, arithmetic and copies ran while one was open for 0% of the time, Pallas kernels for 11%

profile of v2, /device:TPU:8, one launch (start us, length us, event | category | flops | bytes accessed | tf_op | source)
XLA Modules:
  0.0 36.4 jit_solution(6110173811658927623)
XLA Ops:
  1.3 1.3 %shard_map.94 = (f32[608,128]{1,0:T(8,128)S(1)}, f32[3,28,128]{2,1,0:T(8,128)S(1)}, f32[3,28,128]{2,1,0:T(8,128)S(1)}, f32[896,128]{1,0:T(8,128)S(1)}, s32[8,128]{1,0:T(8,128)S(1)}, /*index=5*/f32[3,8,128]{2,1,0:T(8,128)S(1)}) custom-call(s32[1,1]{1,0:T(1,128)S(6)} %copy.12.count, f32[384,128]{1,0:T(8,128)} %bitcast.10, f32[384,128]{1,0:T(8,128)} %bitcast.11, ...), custom_call_target="tpu_custom_call" | custom-call | flops 1000 | bytes 1000 | tf_op jit(solution)/shard_map/pallas_call | solution.py:456
  2.6 2.3 %collective-permute-start.1 = (f32[3,28,128]{2,1,0:T(8,128)S(1)}, f32[3,28,128]{2,1,0:T(8,128)S(1)}, u32[]{:S(2)}, u32[]{:S(2)}) collective-permute-start(f32[3,28,128]{2,1,0:T(8,128)S(1)} %get-tuple-element.33), channel_id=1, source_target_pairs={{0,1},{1,0},{2,3},{3,2},{4,5},{5,4},{6,7},{7,6},{8,9},{9,8},{10,11... | collective-permute-start | bytes 129032 | tf_op jit(solution)/shard_map/ppermute | solution.py:478
  4.9 0.7 %collective-permute-start.2 = (f32[3,28,128]{2,1,0:T(8,128)S(1)}, f32[3,28,128]{2,1,0:T(8,128)S(1)}, u32[]{:S(2)}, u32[]{:S(2)}) collective-permute-start(f32[3,28,128]{2,1,0:T(8,128)S(1)} %get-tuple-element.34), channel_id=1, source_target_pairs={{0,7},{1,2},{2,1},{3,4},{4,3},{5,6},{6,5},{7,0},{8,15},{9,10},{10,... | collective-permute-start | bytes 129032 | tf_op jit(solution)/shard_map/ppermute | solution.py:477
  5.6 7.4 %collective-permute-start = (f32[608,128]{1,0:T(8,128)S(1)}, f32[608,128]{1,0:T(8,128)S(1)}, u32[]{:S(2)}, u32[]{:S(2)}) collective-permute-start(f32[608,128]{1,0:T(8,128)S(1)} %get-tuple-element.31), channel_id=1, source_target_pairs={{0,248},{8,16},{16,8},{24,32},{32,24},{40,48},{48,40},{56,64},{64,... | collective-permute-start | bytes 933896 | tf_op jit(solution)/shard_map/ppermute | solution.py:476
  12.9 0.0 collective-permute-done.1.y_pair
  12.9 0.0 collective-permute-done.2.y_other
  12.9 0.1 shard_map.95
  13.0 0.1 collective-permute-start.4
  13.1 0.0 copy-start
  13.1 3.3 %collective-permute-start.3 = (f32[144,128]{1,0:T(8,128)S(1)}, f32[144,128]{1,0:T(8,128)S(1)}, u32[]{:S(2)}, u32[]{:S(2)}) collective-permute-start(f32[144,128]{1,0:T(8,128)S(1)} %get-tuple-element.35), channel_id=1, source_target_pairs={{0,248},{8,16},{16,8},{24,32},{32,24},{40,48},{48,40},{56,64},{64,... | collective-permute-start | bytes 221192 | tf_op jit(solution)/shard_map/ppermute | solution.py:483
  16.4 0.8 %shard_map.96.dense = f32[4,128,128]{2,1,0:T(8,128)S(1)} custom-call(s32[8,128]{1,0:T(8,128)S(1)} %get-tuple-element.29.cells, f32[3,8,128]{2,1,0:T(8,128)S(1)} %get-tuple-element.30.mult), custom_call_target="tpu_custom_call" | custom-call | flops 99999997952 | bytes 1000 | tf_op jit(solution)/shard_map/pallas_call | solution.py:479
  17.3 0.0 collective-permute-done.4.near
  17.3 0.0 copy-done
  17.3 2.7 %shard_map.97 = (f32[2560,128]{1,0:T(8,128)S(1)}, f32[2400,128]{1,0:T(8,128)S(1)}, f32[2400,128]{1,0:T(8,128)S(1)}, f32[1200,128]{1,0:T(8,128)S(1)}, f32[1200,12...) custom-call(f32[8,6]{1,0:T(8,128)S(1)} %copy-done, ...), custom_call_target="tpu_custom_call" | custom-call | flops 1000 | bytes 1000 | tf_op jit(solution)/shard_map/pallas_call | solution.py:487
  20.0 1.5 %collective-permute-done.far = f32[608,128]{1,0:T(8,128)S(1)} collective-permute-done((f32[608,128]{1,0:T(8,128)S(1)}, f32[608,128]{1,0:T(8,128)S(1)}, u32[]{:S(2)}, u32[]{:S(2)}) %collective-permute-start) | collective-permute-done | bytes 311328 | tf_op jit(solution)/shard_map/ppermute | solution.py:476
  21.5 0.4 %shard_map.98.ribbon = f32[4,192,128]{2,1,0:T(8,128)S(1)} custom-call(f32[608,128]{1,0:T(8,128)S(1)} %collective-permute-done.far, f32[752,128]{1,0:T(8,128)S(1)} %collective-permute-done.4.near, f32[4,128,128]{2,1,0:T(8,128)S(1)} %shard_map.96.dense, f32[96,128]{1,0:T(8,128)S(1)} %get-tuple-element.38.last), custom_call_target="tpu_custom_call" | custom-call | flops 1000 | bytes 1000 | tf_op jit(solution)/shard_map/pallas_call | solution.py:490
  21.9 0.4 %collective-permute-done.3.corner = f32[144,128]{1,0:T(8,128)S(1)} collective-permute-done((f32[144,128]{1,0:T(8,128)S(1)}, f32[144,128]{1,0:T(8,128)S(1)}, u32[]{:S(2)}, u32[]{:S(2)}) %collective-permute-start.3) | collective-permute-done | bytes 73760 | tf_op jit(solution)/shard_map/ppermute | solution.py:483
  22.3 1.7 %shard_map.99 = (f32[384,128]{1,0:T(8,128)S(1)}, f32[3,160,128]{2,1,0:T(8,128)S(1)}, f32[8,48,128]{2,1,0:T(8,128)S(1)}) custom-call(f32[608,128]{1,0:T(8,128)S(1)} %collective-permute-done.far, f32[144,128]{1,0:T(8,128)S(1)} %collective-permute-done.3.corner, f32[4,192,128]{2,1,0:T(8,128)S(1)} %shard_map.98.ribbon, ...), custom_call_target="tpu_custom_call" | custom-call | flops 1000 | bytes 1000 | tf_op jit(solution)/shard_map/pallas_call | solution.py:491
  24.0 11.0 %all_to_all.5.gathered = f32[8,48,128]{2,1,0:T(8,128)S(1)} all-to-all(f32[8,48,128]{2,1,0:T(8,128)S(1)} %get-tuple-element.51), channel_id=1, replica_groups=mesh['gx'=32,'gy'=8] {'gy'}, dimensions={0} | all-to-all | bytes 393216 | tf_op jit(solution)/shard_map/all_to_all | solution.py:497
  34.9 1.4 %shard_map.100 = (f32[384,128]{1,0:T(8,128)}, f32[3,8,128]{2,1,0:T(8,128)}, f32[3,128,128]{2,1,0:T(8,128)}) custom-call(s32[8,128]{1,0:T(8,128)S(1)} %get-tuple-element.29.cells, f32[3,8,128]{2,1,0:T(8,128)S(1)} %get-tuple-element.30.mult, f32[3,160,128]{2,1,0:T(8,128)S(1)} %get-tuple-element.49.jumps, f32[384,128]{1,0:T(8,128)S(1)} %get-tuple-element.50.smoothed, ...), custom_call_target="tpu_custom_call" | custom-call | flops 1000 | bytes 1000 | tf_op jit(solution)/shard_map/pallas_call | solution.py:498
Async XLA Ops:
  2.6 10.3 %collective-permute-start.1 = (f32[3,28,128]{2,1,0:T(8,128)S(1)}, f32[3,28,128]{2,1,0:T(8,128)S(1)}, u32[]{:S(2)}, u32[]{:S(2)}) collective-permute-start(f32[3,28,128]{2,1,0:T(8,128)S(1)} %get-tuple-element.33), channel_id=1, source_target_pairs={{0,1},{1,0},{2,3},{3,2},{4,5},{5,4},{6,7},{7,6},{8,9},{9,8},{10,11... | collective-permute-start | bytes 129032 | tf_op jit(solution)/shard_map/ppermute | solution.py:478
  4.9 8.1 %collective-permute-start.2 = (f32[3,28,128]{2,1,0:T(8,128)S(1)}, f32[3,28,128]{2,1,0:T(8,128)S(1)}, u32[]{:S(2)}, u32[]{:S(2)}) collective-permute-start(f32[3,28,128]{2,1,0:T(8,128)S(1)} %get-tuple-element.34), channel_id=1, source_target_pairs={{0,7},{1,2},{2,1},{3,4},{4,3},{5,6},{6,5},{7,0},{8,15},{9,10},{10,... | collective-permute-start | bytes 129032 | tf_op jit(solution)/shard_map/ppermute | solution.py:477
  5.6 16.0 %collective-permute-start = (f32[608,128]{1,0:T(8,128)S(1)}, f32[608,128]{1,0:T(8,128)S(1)}, u32[]{:S(2)}, u32[]{:S(2)}) collective-permute-start(f32[608,128]{1,0:T(8,128)S(1)} %get-tuple-element.31), channel_id=1, source_target_pairs={{0,248},{8,16},{16,8},{24,32},{32,24},{40,48},{48,40},{56,64},{64,... | collective-permute-start | bytes 933896 | tf_op jit(solution)/shard_map/ppermute | solution.py:476
  13.0 4.2 %collective-permute-start.4 = (f32[752,128]{1,0:T(8,128)S(1)}, f32[752,128]{1,0:T(8,128)S(1)}, u32[]{:S(2)}, u32[]{:S(2)}) collective-permute-start(f32[752,128]{1,0:T(8,128)S(1)} %get-tuple-element.36), channel_id=1, source_target_pairs={{0,8},{8,0},{16,24},{24,16},{32,40},{40,32},{48,56},{56,48},{64,72... | collective-permute-start | bytes 1155080 | tf_op jit(solution)/shard_map/ppermute | solution.py:484
  13.1 4.2 %copy-start = (f32[8,6]{1,0:T(8,128)S(1)}, f32[8,6]{1,0:T(8,128)}, u32[]{:S(2)}) copy-start(f32[8,6]{1,0:T(8,128)} %stiffness.1) | copy-start | bytes 580
  13.1 9.1 %collective-permute-start.3 = (f32[144,128]{1,0:T(8,128)S(1)}, f32[144,128]{1,0:T(8,128)S(1)}, u32[]{:S(2)}, u32[]{:S(2)}) collective-permute-start(f32[144,128]{1,0:T(8,128)S(1)} %get-tuple-element.35), channel_id=1, source_target_pairs={{0,248},{8,16},{16,8},{24,32},{32,24},{40,48},{48,40},{56,64},{64,... | collective-permute-start | bytes 221192 | tf_op jit(solution)/shard_map/ppermute | solution.py:483

commit v3 on v2

--- a/solution.py
+++ b/solution.py
@@ -18,7 +18,6 @@
 PX = CX + 2 * HALO
 PR = PX - 2
 ROWS = 40
-TILE = ROWS - CY
 LAB0 = 3 * PX
 RHS0 = LAB0 + PX
 FIELDS = RHS0 + 3 * PR
@@ -133,7 +132,8 @@
     for k in range(CY + HALO, ROWS - HALO):
         wide[pl.ds(k, OWN, stride=ROWS), :] = jnp.zeros((OWN, NZ), F32)
     for place, first, k in sent_planes():
-        corner[rows_of(place, TILE), :] = wide[pl.ds((first + k) * ROWS + CY, TILE), :]
+        for i, y in enumerate((CY, ROWS - HALO)):
+            corner[pl.ds(place * 2 * HALO + i * HALO, HALO), :] = wide[pl.ds((first + k) * ROWS + y, HALO), :]
         near[rows_of(place, ROWS), :] = wide[rows_of(first + CX - 1 - k, ROWS), :]
     near[pl.ds(SIDE * ROWS, SLOT_ROWS), :] = cells[...].astype(F32)
     for c in range(3):
@@ -331,16 +331,19 @@
     far, corner, ribbon,
     near_fields, near_coeff, near_total, near_scale, near_flux,
     near_first, near_flux_first, near_second, near_flux_second, table, last,
-    smoothed, jumps, message,
-    fields, coeff, total, scale, flux, first, flux_first, second, flux_second, coarse,
+    message, second,
+    fields, coeff, total, scale, flux, first, flux_first, flux_second, coarse,
 ):
     inside = is_inside()
     flip = odd("gx")
     sign = jnp.where(flip == 1, -1.0, 1.0).astype(F32)
+    for y in range(CY + HALO, ROWS - HALO):
+        fields[pl.ds(y, FIELDS, stride=ROWS), :] = jnp.zeros((FIELDS, NZ), F32)
     for place, at, k in halo_planes():
         plane = (at + HALO - 1 - k) * ROWS
         fields[pl.ds(plane, CY), :] = inside * far[rows_of(place, CY), :]
-        fields[pl.ds(plane + CY, TILE), :] = inside * corner[rows_of(place, TILE), :]
+        for i, y in enumerate((CY, ROWS - HALO)):
+            fields[pl.ds(plane + y, HALO), :] = inside * corner[pl.ds(place * 2 * HALO + i * HALO, HALO), :]
     v0, flux0 = Split(HALO, fields, near_fields), Split(HALO, flux, near_flux)
     v1, flux1 = Split(HALO + 1, first, near_first), Split(HALO + 1, flux_first, near_flux_first)
     v2, flux2 = Split(HALO + 2, second, near_second), Split(HALO + 2, flux_second, near_flux_second)
@@ -361,13 +364,9 @@
 
     for c in range(3):
         planes = [grid.get(v2, c, HALO - 1 + i)[:CY] for i in range(CX + 2)]
-        for g in range(CX):
-            x = g + flip * (CX - 1 - 2 * g)
-            smoothed[rows_of(c * CX + x, CY), :] = planes[1 + g]
         pushed = []
         for i in range(CX + 1):
             jump = sign * (planes[i] - planes[i + 1])
-            jumps[c, rows_of(i, CY), :] = jump
             at = rows_of(i + flip, CY)
             pushed.append(jnp.where(ribbon[3, at, :] > 0.5, ribbon[c, at, :] + PENALTY * jump, 0.0))
         parts = [remainders[g][c] - sign * (pushed[g + 1] - pushed[g]) for g in range(CX)]
@@ -388,28 +387,38 @@
         message[s] = out
 
 
-def finish(
-    cells, mult, jumps, smoothed, gathered,
-    smoothed_out, updated_out, coarse_out,
-    updated, coarse, done,
+def finish_slots(
+    cells, mult, low, high,
+    smoothed_out, updated_out,
+    updated, done,
 ):
-    copies = [
-        pltpu.make_async_copy(smoothed, smoothed_out, done.at[0]),
-        pltpu.make_async_copy(coarse, coarse_out, done.at[1]),
-        pltpu.make_async_copy(updated, updated_out, done.at[2]),
-    ]
-    copies[0].start()
-    for c in range(3):
-        parts = [gathered[s, pl.ds(c * CY // 2, CY // 2), :] for s in range(N_GY)]
-        coarse[c] = jnp.transpose(jnp.concatenate(parts, axis=0))
-    copies[1].start()
+    flip = odd("gx")
+    split = Split(HALO + 2, low, high)
+
+    def plane(c, p):
+        ref, at = split.of(c, p)
+        return ref.at[pl.ds(at.start, CY), :]
+
+    copies = [pltpu.make_async_copy(updated, updated_out, done.at[3 * CX])]
+    for c in range(3):
+        for g in range(CX):
+            x = g + flip * (CX - 1 - 2 * g)
+            copies.append(
+                pltpu.make_async_copy(
+                    plane(c, HALO + g), smoothed_out.at[rows_of(c * CX + x, CY), :], done.at[c * CX + g]
+                )
+            )
+    for copy in copies[1:]:
+        copy.start()
     live = cells[...] >= 0
     column, depth = cells[...] // NZ, cells[...] % NZ
     block = CX * CY
-    start = pl.multiple_of((1 - odd("gx")) * CY, CY)
-    left = jnp.concatenate(
-        [jnp.concatenate(pieces_of(jumps[c, pl.ds(start, block), :]), axis=1) for c in range(3)], axis=0
-    )
+    left = []
+    for c in range(3):
+        v = [plane(c, HALO - 1 + i)[...] for i in range(CX + 2)]
+        jumps = [v[1 + g] - jnp.where(flip == 1, v[g], v[2 + g]) for g in range(CX)]
+        left.append(jnp.concatenate(pieces_of(jnp.concatenate(jumps, axis=0)), axis=1))
+    left = jnp.concatenate(left, axis=0)
     for j in range(SLOT_ROWS):
         at_depth = lax.broadcasted_iota(jnp.int32, (NZ, 128), 0) == depth[j : j + 1]
         right = jnp.where(at_depth, 1.0, 0.0).astype(BF16)
@@ -421,7 +430,18 @@
             )
             old = mult[c, j : j + 1, :]
             updated[c, j : j + 1, :] = jnp.where(live[j : j + 1], old + PENALTY * jump, old)
-    copies[2].start()
+    copies[0].start()
+    for copy in copies:
+        copy.wait()
+
+
+def finish_coarse(gathered, coarse_out, coarse, done):
+    copies = []
+    for c in range(3):
+        parts = [gathered[s, pl.ds(c * CY // 2, CY // 2), :] for s in range(N_GY)]
+        coarse[c] = jnp.transpose(jnp.concatenate(parts, axis=0))
+        copies.append(pltpu.make_async_copy(coarse.at[c], coarse_out.at[c], done.at[c]))
+        copies[c].start()
     for copy in copies:
         copy.wait()
 
@@ -447,7 +467,7 @@
 
 
 def other(n):
-    return [(i, (((i + 1) % n ^ 1) - 1) % n) for i in range(n)]
+    return [(i, i if i in (0, n - 1) else ((i + 1) ^ 1) - 1) for i in range(n)]
 
 
 def body(displacement, rhs, labels, stiffness, rows, counts, multipliers):
@@ -478,7 +498,7 @@
     y_pair = lax.ppermute(y_pair, "gy", pair(N_GY))
     (dense,) = call(spread_own, [f32(4, block, NZ)], [VMEM] * 2, flops=100000000000)(cells, mult)
     near, corner, own = call(
-        pack_second, [f32(SIDE * ROWS + IFACE, NZ), f32(SIDE * TILE, NZ), f32(OWN * ROWS, NZ)], [VMEM] * 5
+        pack_second, [f32(SIDE * ROWS + IFACE, NZ), f32(SIDE * 2 * HALO + 4, NZ), f32(OWN * ROWS, NZ)], [VMEM] * 5
     )(own, cells, mult, y_pair, y_other)
     corner = lax.ppermute(corner, "gx", other(N_GX))
     near = lax.ppermute(near, "gx", pair(N_GX))
@@ -488,24 +508,28 @@
         near_part, arrays + [f32(LABELS * 6, NZ), f32(3 * CY, NZ)], [SMEM, VMEM, VMEM]
     )(stiffness, own, near)
     (ribbon,) = call(spread_before, [f32(4, (CX + 2) * CY, NZ)], [VMEM] * 4)(far, near, dense, half[-1])
-    smoothed, jumps, message = call(
+    message, low = call(
         far_part,
-        [f32(3 * block, NZ), f32(3, (CX + 1) * CY, NZ), f32(N_GY, 3 * CY // 2, NZ)],
+        [f32(N_GY, 3 * CY // 2, NZ), three],
         [VMEM] * (3 + len(half)),
-        scratch=[pltpu.VMEM(a.shape, F32) for a in arrays] + [pltpu.VMEM((6 * CY, NZ), F32)],
+        scratch=[pltpu.VMEM(a.shape, F32) for a in arrays[:-1]] + [pltpu.VMEM((6 * CY, NZ), F32)],
     )(far, corner, ribbon, *half)
     gathered = lax.all_to_all(message, "gy", 0, 0)
-    smoothed, updated, coarse = call(
-        finish,
-        [pltpu.HBM(s, F32) for s in ((3 * block, NZ), (3, SLOT_ROWS, 128), (3, CX // 2 * NZ // 2, NY // 2))],
-        [VMEM] * 5,
-        out_specs=[HBM] * 3,
-        scratch=[
-            pltpu.VMEM((3, SLOT_ROWS, 128), F32),
-            pltpu.VMEM((3, CX // 2 * NZ // 2, NY // 2), F32),
-            pltpu.SemaphoreType.DMA((3,)),
-        ],
-    )(cells, mult, jumps, smoothed, gathered)
+    smoothed, updated = call(
+        finish_slots,
+        [pltpu.HBM((3 * block, NZ), F32), pltpu.HBM((3, SLOT_ROWS, 128), F32)],
+        [VMEM] * 4,
+        out_specs=[HBM] * 2,
+        scratch=[pltpu.VMEM((3, SLOT_ROWS, 128), F32), pltpu.SemaphoreType.DMA((3 * CX + 1,))],
+        flops=10**10,
+    )(cells, mult, low, half[7])
+    (coarse,) = call(
+        finish_coarse,
+        [pltpu.HBM((3, CX // 2 * NZ // 2, NY // 2), F32)],
+        [VMEM],
+        out_specs=[HBM],
+        scratch=[pltpu.VMEM((3, CX // 2 * NZ // 2, NY // 2), F32), pltpu.SemaphoreType.DMA((3,))],
+    )(gathered)
     coarse = jnp.swapaxes(coarse.reshape(3, CX // 2, NZ // 2, NY // 2), 2, 3)
     return (smoothed.reshape(3, CX, CY, NZ), coarse, updated.reshape(3, 1, 1, SLOTS))
 

time: 36.6 us -> 38.7 us (1.057)
  the two profiles are of different devices: /device:TPU:8 before, /device:TPU:71 now
where the time goes in v3:
time: 38.7 us; the launch traced here: 38.4 us
  starting transfers between devices  18.2 us (47%)
  Pallas kernels  10 us (26%)
  waiting for transfers between devices  8.74 us (23%)
  between operations  1.39 us (4%)
    ppermute x1, starting transfers between devices, body(): far = lax.ppermute(far, 'gx', other(N_GX))  6.87 us
    all_to_all x1, starting transfers between devices, body(): gathered = lax.all_to_all(message, 'gy', 0, 0)  5.61 us
    all_to_all x1, waiting for transfers between devices, body(): gathered = lax.all_to_all(message, 'gy', 0, 0)  4.25 us
    ppermute x1, waiting for transfers between devices, body(): corner = lax.ppermute(corner, 'gx', other(N_GX))  4.11 us
    ppermute x1, starting transfers between devices, body(): corner = lax.ppermute(corner, 'gx', other(N_GX))  3.61 us
    pallas_call x1, Pallas kernels, body(): call(near_part, arrays + [f32(LABELS * 6, NZ), f32(3 * CY, NZ)], [SMEM, V...  2.67 us
    pallas_call x1, Pallas kernels, body(): call(far_part, [f32(N_GY, 3 * CY // 2, NZ), three], [VMEM] * (3 + len(hal...  2.42 us
    pallas_call x1, Pallas kernels, body(): call(finish_slots, [pltpu.HBM((3 * block, NZ), F32), pltpu.HBM((3, SLOT_R...  1.52 us
  transfers between devices with their start and end apart: 6, of which 3 were waited for; matrix products, arithmetic and copies ran while one was open for 0% of the time, Pallas kernels for 14%

profile of v3, /device:TPU:71, one launch (start us, length us, event | category | flops | bytes accessed | tf_op | source)
XLA Modules:
  0.0 38.4 jit_solution(12943866313534506276)
XLA Ops:
  1.3 1.3 %shard_map.94 = (f32[608,128]{1,0:T(8,128)S(1)}, f32[3,28,128]{2,1,0:T(8,128)S(1)}, f32[3,28,128]{2,1,0:T(8,128)S(1)}, f32[896,128]{1,0:T(8,128)S(1)}, s32[8,128]{1,0:T(8,128)S(1)}, /*index=5*/f32[3,8,128]{2,1,0:T(8,128)S(1)}) custom-call(s32[1,1]{1,0:T(1,128)S(6)} %copy.12.count, f32[384,128]{1,0:T(8,128)} %bitcast.10, f32[384,128]{1,0:T(8,128)} %bitcast.11, ...), custom_call_target="tpu_custom_call" | custom-call | flops 1000 | bytes 1000 | tf_op jit(solution)/shard_map/pallas_call | solution.py:476
  2.6 1.4 %collective-permute-start.1 = (f32[3,28,128]{2,1,0:T(8,128)S(1)}, f32[3,28,128]{2,1,0:T(8,128)S(1)}, u32[]{:S(2)}, u32[]{:S(2)}) collective-permute-start(f32[3,28,128]{2,1,0:T(8,128)S(1)} %get-tuple-element.31), channel_id=1, source_target_pairs={{0,1},{1,0},{2,3},{3,2},{4,5},{5,4},{6,7},{7,6},{8,9},{9,8},{10,11... | collective-permute-start | bytes 129032 | tf_op jit(solution)/shard_map/ppermute | solution.py:498
  4.0 0.7 %collective-permute-start.2 = (f32[3,28,128]{2,1,0:T(8,128)S(1)}, f32[3,28,128]{2,1,0:T(8,128)S(1)}, u32[]{:S(2)}, u32[]{:S(2)}) collective-permute-start(f32[3,28,128]{2,1,0:T(8,128)S(1)} %get-tuple-element.32), channel_id=1, source_target_pairs={{0,0},{1,2},{2,1},{3,4},{4,3},{5,6},{6,5},{7,7},{8,8},{9,10},{10,9... | collective-permute-start | bytes 129032 | tf_op jit(solution)/shard_map/ppermute | solution.py:497
  4.7 6.9 %collective-permute-start = (f32[608,128]{1,0:T(8,128)S(1)}, f32[608,128]{1,0:T(8,128)S(1)}, u32[]{:S(2)}, u32[]{:S(2)}) collective-permute-start(f32[608,128]{1,0:T(8,128)S(1)} %get-tuple-element.29), channel_id=1, source_target_pairs={{0,0},{8,16},{16,8},{24,32},{32,24},{40,48},{48,40},{56,64},{64,56... | collective-permute-start | bytes 933896 | tf_op jit(solution)/shard_map/ppermute | solution.py:496
  11.5 0.0 collective-permute-done.1.y_pair
  11.5 0.0 collective-permute-done.2.y_other
  11.6 0.1 shard_map.95
  11.6 0.1 collective-permute-start.4
  11.7 0.0 copy-start
  11.8 3.6 %collective-permute-start.3 = (f32[112,128]{1,0:T(8,128)S(1)}, f32[112,128]{1,0:T(8,128)S(1)}, u32[]{:S(2)}, u32[]{:S(2)}) collective-permute-start(f32[112,128]{1,0:T(8,128)S(1)} %get-tuple-element.33), channel_id=1, source_target_pairs={{0,0},{8,16},{16,8},{24,32},{32,24},{40,48},{48,40},{56,64},{64,56... | collective-permute-start | bytes 172040 | tf_op jit(solution)/shard_map/ppermute | solution.py:503
  15.4 0.8 %shard_map.96.dense = f32[4,128,128]{2,1,0:T(8,128)S(1)} custom-call(s32[8,128]{1,0:T(8,128)S(1)} %get-tuple-element.27.cells, f32[3,8,128]{2,1,0:T(8,128)S(1)} %get-tuple-element.28.mult), custom_call_target="tpu_custom_call" | custom-call | flops 99999997952 | bytes 1000 | tf_op jit(solution)/shard_map/pallas_call | solution.py:499
  16.2 0.0 collective-permute-done.4.near
  16.2 0.0 copy-done
  16.3 2.7 %shard_map.97 = (f32[2560,128]{1,0:T(8,128)S(1)}, f32[2400,128]{1,0:T(8,128)S(1)}, f32[2400,128]{1,0:T(8,128)S(1)}, f32[1200,128]{1,0:T(8,128)S(1)}, f32[1200,12...) custom-call(f32[8,6]{1,0:T(8,128)S(1)} %copy-done, ...), custom_call_target="tpu_custom_call" | custom-call | flops 1000 | bytes 1000 | tf_op jit(solution)/shard_map/pallas_call | solution.py:507
  18.9 0.4 collective-permute-done.far
  19.3 0.4 shard_map.98.ribbon
  19.7 4.1 %collective-permute-done.3.corner = f32[112,128]{1,0:T(8,128)S(1)} collective-permute-done((f32[112,128]{1,0:T(8,128)S(1)}, f32[112,128]{1,0:T(8,128)S(1)}, u32[]{:S(2)}, u32[]{:S(2)}) %collective-permute-start.3) | collective-permute-done | bytes 57376 | tf_op jit(solution)/shard_map/ppermute | solution.py:503
  23.8 2.4 %shard_map.99 = (f32[8,48,128]{2,1,0:T(8,128)}, f32[1200,128]{1,0:T(8,128)S(1)}) custom-call(f32[608,128]{1,0:T(8,128)S(1)} %collective-permute-done.far, f32[112,128]{1,0:T(8,128)S(1)} %collective-permute-done.3.corner, f32[4,192,128]{2,1,0:T(8,128)S(1)} %shard_map.98.ribbon, f32[2560,128]{1,0:T(8,128)S(1)} %get-tuple-element.37.near_fields, ...), custom_call_target="tpu_custom_call" | custom-call | flops 1000 | bytes 1000 | tf_op jit(solution)/shard_map/pallas_call | solution.py:511
  26.2 5.6 %all-to-all-start = ((f32[8,48,128]{2,1,0:T(8,128)}), f32[8,48,128]{2,1,0:T(8,128)S(1)}, u32[]{:S(2)}, u32[]{:S(2)}) async-start(f32[8,48,128]{2,1,0:T(8,128)} %get-tuple-element.49), calls=%async_computation | async-start | bytes 393216 | tf_op jit(solution)/shard_map/all_to_all | solution.py:517
  31.8 1.5 %shard_map.100 = (f32[384,128]{1,0:T(8,128)}, f32[3,8,128]{2,1,0:T(8,128)}) custom-call(s32[8,128]{1,0:T(8,128)S(1)} %get-tuple-element.27.cells, f32[3,8,128]{2,1,0:T(8,128)S(1)} %get-tuple-element.28.mult, f32[1200,128]{1,0:T(8,128)S(1)} %get-tuple-element.47.low, f32[1200,128]{1,0:T(8,128)S(1)} %get-tuple-element.44.near_second.high), custom_call_target="tpu_custom_call" | custom-call | flops 10000000000 | bytes 1000 | tf_op jit(solution)/shard_map/pallas_call | solution.py:518
  33.3 4.3 %all-to-all-done.gathered = f32[8,48,128]{2,1,0:T(8,128)S(1)} async-done(((f32[8,48,128]{2,1,0:T(8,128)}), f32[8,48,128]{2,1,0:T(8,128)S(1)}, u32[]{:S(2)}, u32[]{:S(2)}) %all-to-all-start) | async-done | bytes 196640 | tf_op jit(solution)/shard_map/all_to_all | solution.py:517
  37.6 0.8 %shard_map.101 = f32[3,128,128]{2,1,0:T(8,128)} custom-call(f32[8,48,128]{2,1,0:T(8,128)S(1)} %all-to-all-done.gathered), custom_call_target="tpu_custom_call" | custom-call | flops 1000 | bytes 1000 | tf_op jit(solution)/shard_map/pallas_call | solution.py:526
Async XLA Ops:
  2.6 8.9 %collective-permute-start.1 = (f32[3,28,128]{2,1,0:T(8,128)S(1)}, f32[3,28,128]{2,1,0:T(8,128)S(1)}, u32[]{:S(2)}, u32[]{:S(2)}) collective-permute-start(f32[3,28,128]{2,1,0:T(8,128)S(1)} %get-tuple-element.31), channel_id=1, source_target_pairs={{0,1},{1,0},{2,3},{3,2},{4,5},{5,4},{6,7},{7,6},{8,9},{9,8},{10,11... | collective-permute-start | bytes 129032 | tf_op jit(solution)/shard_map/ppermute | solution.py:498
  4.0 7.5 %collective-permute-start.2 = (f32[3,28,128]{2,1,0:T(8,128)S(1)}, f32[3,28,128]{2,1,0:T(8,128)S(1)}, u32[]{:S(2)}, u32[]{:S(2)}) collective-permute-start(f32[3,28,128]{2,1,0:T(8,128)S(1)} %get-tuple-element.32), channel_id=1, source_target_pairs={{0,0},{1,2},{2,1},{3,4},{4,3},{5,6},{6,5},{7,7},{8,8},{9,10},{10,9... | collective-permute-start | bytes 129032 | tf_op jit(solution)/shard_map/ppermute | solution.py:497
  4.7 14.6 %collective-permute-start = (f32[608,128]{1,0:T(8,128)S(1)}, f32[608,128]{1,0:T(8,128)S(1)}, u32[]{:S(2)}, u32[]{:S(2)}) collective-permute-start(f32[608,128]{1,0:T(8,128)S(1)} %get-tuple-element.29), channel_id=1, source_target_pairs={{0,0},{8,16},{16,8},{24,32},{32,24},{40,48},{48,40},{56,64},{64,56... | collective-permute-start | bytes 933896 | tf_op jit(solution)/shard_map/ppermute | solution.py:496
  11.6 4.6 %collective-permute-start.4 = (f32[752,128]{1,0:T(8,128)S(1)}, f32[752,128]{1,0:T(8,128)S(1)}, u32[]{:S(2)}, u32[]{:S(2)}) collective-permute-start(f32[752,128]{1,0:T(8,128)S(1)} %get-tuple-element.34), channel_id=1, source_target_pairs={{0,8},{8,0},{16,24},{24,16},{32,40},{40,32},{48,56},{56,48},{64,72... | collective-permute-start | bytes 1155080 | tf_op jit(solution)/shard_map/ppermute | solution.py:504
  11.7 4.5 %copy-start = (f32[8,6]{1,0:T(8,128)S(1)}, f32[8,6]{1,0:T(8,128)}, u32[]{:S(2)}) copy-start(f32[8,6]{1,0:T(8,128)} %stiffness.1) | copy-start | bytes 580
  11.8 12.0 %collective-permute-start.3 = (f32[112,128]{1,0:T(8,128)S(1)}, f32[112,128]{1,0:T(8,128)S(1)}, u32[]{:S(2)}, u32[]{:S(2)}) collective-permute-start(f32[112,128]{1,0:T(8,128)S(1)} %get-tuple-element.33), channel_id=1, source_target_pairs={{0,0},{8,16},{16,8},{24,32},{32,24},{40,48},{48,40},{56,64},{64,56... | collective-permute-start | bytes 172040 | tf_op jit(solution)/shard_map/ppermute | solution.py:503
  26.2 11.4 %all-to-all-start = ((f32[8,48,128]{2,1,0:T(8,128)}), f32[8,48,128]{2,1,0:T(8,128)S(1)}, u32[]{:S(2)}, u32[]{:S(2)}) async-start(f32[8,48,128]{2,1,0:T(8,128)} %get-tuple-element.49), calls=%async_computation | async-start | bytes 393216 | tf_op jit(solution)/shard_map/all_to_all | solution.py:517

commit v4 on v2

--- a/solution.py
+++ b/solution.py
@@ -18,7 +18,6 @@
 PX = CX + 2 * HALO
 PR = PX - 2
 ROWS = 40
-TILE = ROWS - CY
 LAB0 = 3 * PX
 RHS0 = LAB0 + PX
 FIELDS = RHS0 + 3 * PR
@@ -118,7 +117,7 @@
         y_other[k] = jnp.where(up, first, last)
 
 
-def pack_second(own, cells, mult, y_pair, y_other, near, corner, wide):
+def pack_second(y_other, y_pair, own, cells, mult, corner, near, wide):
     here = lax.axis_index("gy")
     up = odd("gy") == 0
     low = jnp.where(here > 0, 1.0, 0.0).astype(F32)
@@ -133,7 +132,8 @@
     for k in range(CY + HALO, ROWS - HALO):
         wide[pl.ds(k, OWN, stride=ROWS), :] = jnp.zeros((OWN, NZ), F32)
     for place, first, k in sent_planes():
-        corner[rows_of(place, TILE), :] = wide[pl.ds((first + k) * ROWS + CY, TILE), :]
+        for i, y in enumerate((CY, ROWS - HALO)):
+            corner[pl.ds(place * 2 * HALO + i * HALO, HALO), :] = wide[pl.ds((first + k) * ROWS + y, HALO), :]
         near[rows_of(place, ROWS), :] = wide[rows_of(first + CX - 1 - k, ROWS), :]
     near[pl.ds(SIDE * ROWS, SLOT_ROWS), :] = cells[...].astype(F32)
     for c in range(3):
@@ -337,10 +337,13 @@
     inside = is_inside()
     flip = odd("gx")
     sign = jnp.where(flip == 1, -1.0, 1.0).astype(F32)
+    for y in range(CY + HALO, ROWS - HALO):
+        fields[pl.ds(y, FIELDS, stride=ROWS), :] = jnp.zeros((FIELDS, NZ), F32)
     for place, at, k in halo_planes():
         plane = (at + HALO - 1 - k) * ROWS
         fields[pl.ds(plane, CY), :] = inside * far[rows_of(place, CY), :]
-        fields[pl.ds(plane + CY, TILE), :] = inside * corner[rows_of(place, TILE), :]
+        for i, y in enumerate((CY, ROWS - HALO)):
+            fields[pl.ds(plane + y, HALO), :] = inside * corner[pl.ds(place * 2 * HALO + i * HALO, HALO), :]
     v0, flux0 = Split(HALO, fields, near_fields), Split(HALO, flux, near_flux)
     v1, flux1 = Split(HALO + 1, first, near_first), Split(HALO + 1, flux_first, near_flux_first)
     v2, flux2 = Split(HALO + 2, second, near_second), Split(HALO + 2, flux_second, near_flux_second)
@@ -410,17 +413,20 @@
     left = jnp.concatenate(
         [jnp.concatenate(pieces_of(jumps[c, pl.ds(start, block), :]), axis=1) for c in range(3)], axis=0
     )
-    for j in range(SLOT_ROWS):
-        at_depth = lax.broadcasted_iota(jnp.int32, (NZ, 128), 0) == depth[j : j + 1]
+    for j in range(SLOT_ROWS // 2):
+        at_depth = lax.broadcasted_iota(jnp.int32, (NZ, 256), 0) == paired(depth, j)
         right = jnp.where(at_depth, 1.0, 0.0).astype(BF16)
         picked = jnp.dot(left, jnp.concatenate([right] * 3, axis=0), preferred_element_type=F32)
-        at_column = lax.broadcasted_iota(jnp.int32, (block, 128), 0) == column[j : j + 1]
+        at_column = lax.broadcasted_iota(jnp.int32, (block, 256), 0) == paired(column, j)
         for c in range(3):
             jump = jnp.sum(
                 jnp.where(at_column, picked[c * block : (c + 1) * block], 0.0), axis=0, keepdims=True
             )
-            old = mult[c, j : j + 1, :]
-            updated[c, j : j + 1, :] = jnp.where(live[j : j + 1], old + PENALTY * jump, old)
+            for i in range(2):
+                at = 2 * j + i
+                old = mult[c, at : at + 1, :]
+                new = old + PENALTY * jump[:, i * 128 : (i + 1) * 128]
+                updated[c, at : at + 1, :] = jnp.where(live[at : at + 1], new, old)
     copies[2].start()
     for copy in copies:
         copy.wait()
@@ -446,8 +452,22 @@
     return [(i, i ^ 1) for i in range(n)]
 
 
-def other(n):
-    return [(i, (((i + 1) % n ^ 1) - 1) % n) for i in range(n)]
+def other_x():
+    out = []
+    for i in range(N_GX):
+        for j in range(N_GY):
+            partner = (i, j ^ 1) if i in (0, N_GX - 1) else (((i + 1) ^ 1) - 1, j)
+            out.append((i * N_GY + j, partner[0] * N_GY + partner[1]))
+    return out
+
+
+def other_y():
+    out = []
+    for i in range(N_GX):
+        for j in range(N_GY):
+            partner = (i ^ 1, j) if j in (0, N_GY - 1) else (i, ((j + 1) ^ 1) - 1)
+            out.append((i * N_GY + j, partner[0] * N_GY + partner[1]))
+    return out
 
 
 def body(displacement, rhs, labels, stiffness, rows, counts, multipliers):
@@ -473,14 +493,14 @@
         in_hbm(rows.reshape(SLOT_ROWS, 128)),
         in_hbm(multipliers.reshape(3, SLOT_ROWS, 128)),
     )
-    far = lax.ppermute(far, "gx", other(N_GX))
-    y_other = lax.ppermute(y_other, "gy", other(N_GY))
+    far = lax.ppermute(far, ("gx", "gy"), other_x())
     y_pair = lax.ppermute(y_pair, "gy", pair(N_GY))
+    y_other = lax.ppermute(y_other, ("gx", "gy"), other_y())
     (dense,) = call(spread_own, [f32(4, block, NZ)], [VMEM] * 2, flops=100000000000)(cells, mult)
-    near, corner, own = call(
-        pack_second, [f32(SIDE * ROWS + IFACE, NZ), f32(SIDE * TILE, NZ), f32(OWN * ROWS, NZ)], [VMEM] * 5
-    )(own, cells, mult, y_pair, y_other)
-    corner = lax.ppermute(corner, "gx", other(N_GX))
+    corner, near, own = call(
+        pack_second, [f32(SIDE * 2 * HALO + 4, NZ), f32(SIDE * ROWS + IFACE, NZ), f32(OWN * ROWS, NZ)], [VMEM] * 5
+    )(y_other, y_pair, own, cells, mult)
+    corner = lax.ppermute(corner, ("gx", "gy"), other_x())
     near = lax.ppermute(near, "gx", pair(N_GX))
     three, six = f32(3 * PX * ROWS, NZ), f32(6 * PX * ROWS, NZ)
     arrays = [f32(FIELDS * ROWS, NZ), six, six] + [three] * 6

time: 36.6 us -> 33.9 us (0.926)
  the two profiles are of different devices: /device:TPU:8 before, /device:TPU:128 now
where the time goes in v4:
time: 33.9 us; the launch traced here: 33.4 us
  blocking collectives  9.51 us (28%)
  Pallas kernels  8.29 us (24%)
  starting transfers between devices  8.05 us (24%)
  waiting for transfers between devices  6.19 us (18%)
  between operations  1.36 us (4%)
    all_to_all x1, blocking collectives, body(): gathered = lax.all_to_all(message, 'gy', 0, 0)  9.51 us
    ppermute x1, waiting for transfers between devices, body(): far = lax.ppermute(far, ('gx', 'gy'), other_x())  4.62 us
    ppermute x1, starting transfers between devices, body(): corner = lax.ppermute(corner, ('gx', 'gy'), other_x())  3.99 us
    ppermute x1, starting transfers between devices, body(): y_pair = lax.ppermute(y_pair, 'gy', pair(N_GY))  3.14 us
    pallas_call x1, Pallas kernels, body(): call(near_part, arrays + [f32(LABELS * 6, NZ), f32(3 * CY, NZ)], [SMEM, V...  2.68 us
    pallas_call x1, Pallas kernels, body(): call(far_part, [f32(3 * block, NZ), f32(3, (CX + 1) * CY, NZ), f32(N_GY,...  1.71 us
    ppermute x1, waiting for transfers between devices, body(): y_pair = lax.ppermute(y_pair, 'gy', pair(N_GY))  1.34 us
    pallas_call x1, Pallas kernels, body(): call(pack_first, [f32(SIDE * CY + IFACE, NZ), f32(HALO, OWN, NZ), f32(HAL...  1.33 us
  transfers between devices with their start and end apart: 5, of which 3 were waited for; matrix products, arithmetic and copies ran while one was open for 0% of the time, Pallas kernels for 12%

profile of v4, /device:TPU:128, one launch (start us, length us, event | category | flops | bytes accessed | tf_op | source)
XLA Modules:
  0.0 33.4 jit_solution(2788578270287767194)
XLA Ops:
  1.3 1.3 %shard_map.94 = (f32[608,128]{1,0:T(8,128)S(1)}, f32[3,28,128]{2,1,0:T(8,128)S(1)}, f32[3,28,128]{2,1,0:T(8,128)S(1)}, f32[896,128]{1,0:T(8,128)S(1)}, s32[8,128]{1,0:T(8,128)S(1)}, /*index=5*/f32[3,8,128]{2,1,0:T(8,128)S(1)}) custom-call(s32[1,1]{1,0:T(1,128)S(6)} %copy.12.count, f32[384,128]{1,0:T(8,128)} %bitcast.10, f32[384,128]{1,0:T(8,128)} %bitcast.11, ...), custom_call_target="tpu_custom_call" | custom-call | flops 1000 | bytes 1000 | tf_op jit(solution)/shard_map/pallas_call | solution.py:476
  2.6 0.1 collective-permute-start.1
  2.7 3.1 %collective-permute-start.2 = (f32[3,28,128]{2,1,0:T(8,128)S(1)}, f32[3,28,128]{2,1,0:T(8,128)S(1)}, u32[]{:S(2)}, u32[]{:S(2)}) collective-permute-start(f32[3,28,128]{2,1,0:T(8,128)S(1)} %get-tuple-element.33), channel_id=1, source_target_pairs={{0,1},{1,0},{2,3},{3,2},{4,5},{5,4},{6,7},{7,6},{8,9},{9,8},{10,11... | collective-permute-start | bytes 129032 | tf_op jit(solution)/shard_map/ppermute | solution.py:497
  5.9 0.7 %collective-permute-start = (f32[608,128]{1,0:T(8,128)S(1)}, f32[608,128]{1,0:T(8,128)S(1)}, u32[]{:S(2)}, u32[]{:S(2)}) collective-permute-start(f32[608,128]{1,0:T(8,128)S(1)} %get-tuple-element.31), channel_id=1, source_target_pairs={{0,1},{1,0},{2,3},{3,2},{4,5},{5,4},{6,7},{7,6},{8,16},{9,17},{10,... | collective-permute-start | bytes 933896 | tf_op jit(solution)/shard_map/ppermute | solution.py:496
  6.6 0.0 collective-permute-done.1.y_other
  6.6 1.3 %collective-permute-done.2.y_pair = f32[3,28,128]{2,1,0:T(8,128)S(1)} collective-permute-done((f32[3,28,128]{2,1,0:T(8,128)S(1)}, f32[3,28,128]{2,1,0:T(8,128)S(1)}, u32[]{:S(2)}, u32[]{:S(2)}) %collective-permute-start.2) | collective-permute-done | bytes 43040 | tf_op jit(solution)/shard_map/ppermute | solution.py:497
  7.9 0.1 shard_map.95
  8.0 0.1 collective-permute-start.4
  8.1 0.0 copy-start
  8.1 4.0 %collective-permute-start.3 = (f32[112,128]{1,0:T(8,128)S(1)}, f32[112,128]{1,0:T(8,128)S(1)}, u32[]{:S(2)}, u32[]{:S(2)}) collective-permute-start(f32[112,128]{1,0:T(8,128)S(1)} %get-tuple-element.35), channel_id=1, source_target_pairs={{0,1},{1,0},{2,3},{3,2},{4,5},{5,4},{6,7},{7,6},{8,16},{9,17},{10,... | collective-permute-start | bytes 172040 | tf_op jit(solution)/shard_map/ppermute | solution.py:503
  12.1 0.8 %shard_map.96.dense = f32[4,128,128]{2,1,0:T(8,128)S(1)} custom-call(s32[8,128]{1,0:T(8,128)S(1)} %get-tuple-element.29.cells, f32[3,8,128]{2,1,0:T(8,128)S(1)} %get-tuple-element.30.mult), custom_call_target="tpu_custom_call" | custom-call | flops 99999997952 | bytes 1000 | tf_op jit(solution)/shard_map/pallas_call | solution.py:499
  13.0 0.0 collective-permute-done.4.near
  13.0 0.0 copy-done
  13.0 2.7 %shard_map.97 = (f32[2560,128]{1,0:T(8,128)S(1)}, f32[2400,128]{1,0:T(8,128)S(1)}, f32[2400,128]{1,0:T(8,128)S(1)}, f32[1200,128]{1,0:T(8,128)S(1)}, f32[1200,12...) custom-call(f32[8,6]{1,0:T(8,128)S(1)} %copy-done, ...), custom_call_target="tpu_custom_call" | custom-call | flops 1000 | bytes 1000 | tf_op jit(solution)/shard_map/pallas_call | solution.py:507
  15.7 4.6 %collective-permute-done.far = f32[608,128]{1,0:T(8,128)S(1)} collective-permute-done((f32[608,128]{1,0:T(8,128)S(1)}, f32[608,128]{1,0:T(8,128)S(1)}, u32[]{:S(2)}, u32[]{:S(2)}) %collective-permute-start) | collective-permute-done | bytes 311328 | tf_op jit(solution)/shard_map/ppermute | solution.py:496
  20.3 0.4 %shard_map.98.ribbon = f32[4,192,128]{2,1,0:T(8,128)S(1)} custom-call(f32[608,128]{1,0:T(8,128)S(1)} %collective-permute-done.far, f32[752,128]{1,0:T(8,128)S(1)} %collective-permute-done.4.near, f32[4,128,128]{2,1,0:T(8,128)S(1)} %shard_map.96.dense, f32[96,128]{1,0:T(8,128)S(1)} %get-tuple-element.38.last), custom_call_target="tpu_custom_call" | custom-call | flops 1000 | bytes 1000 | tf_op jit(solution)/shard_map/pallas_call | solution.py:510
  20.7 0.2 collective-permute-done.3.corner
  20.9 1.7 %shard_map.99 = (f32[384,128]{1,0:T(8,128)S(1)}, f32[3,160,128]{2,1,0:T(8,128)S(1)}, f32[8,48,128]{2,1,0:T(8,128)S(1)}) custom-call(f32[608,128]{1,0:T(8,128)S(1)} %collective-permute-done.far, f32[112,128]{1,0:T(8,128)S(1)} %collective-permute-done.3.corner, f32[4,192,128]{2,1,0:T(8,128)S(1)} %shard_map.98.ribbon, ...), custom_call_target="tpu_custom_call" | custom-call | flops 1000 | bytes 1000 | tf_op jit(solution)/shard_map/pallas_call | solution.py:511
  22.6 9.5 %all_to_all.5.gathered = f32[8,48,128]{2,1,0:T(8,128)S(1)} all-to-all(f32[8,48,128]{2,1,0:T(8,128)S(1)} %get-tuple-element.51), channel_id=1, replica_groups=mesh['gx'=32,'gy'=8] {'gy'}, dimensions={0} | all-to-all | bytes 393216 | tf_op jit(solution)/shard_map/all_to_all | solution.py:517
  32.1 1.3 %shard_map.100 = (f32[384,128]{1,0:T(8,128)}, f32[3,8,128]{2,1,0:T(8,128)}, f32[3,128,128]{2,1,0:T(8,128)}) custom-call(s32[8,128]{1,0:T(8,128)S(1)} %get-tuple-element.29.cells, f32[3,8,128]{2,1,0:T(8,128)S(1)} %get-tuple-element.30.mult, f32[3,160,128]{2,1,0:T(8,128)S(1)} %get-tuple-element.49.jumps, f32[384,128]{1,0:T(8,128)S(1)} %get-tuple-element.50.smoothed, ...), custom_call_target="tpu_custom_call" | custom-call | flops 1000 | bytes 1000 | tf_op jit(solution)/shard_map/pallas_call | solution.py:518
Async XLA Ops:
  2.6 4.0 %collective-permute-start.1 = (f32[3,28,128]{2,1,0:T(8,128)S(1)}, f32[3,28,128]{2,1,0:T(8,128)S(1)}, u32[]{:S(2)}, u32[]{:S(2)}) collective-permute-start(f32[3,28,128]{2,1,0:T(8,128)S(1)} %get-tuple-element.32), channel_id=1, source_target_pairs={{0,8},{1,2},{2,1},{3,4},{4,3},{5,6},{6,5},{7,15},{8,0},{9,10},{10,... | collective-permute-start | bytes 129032 | tf_op jit(solution)/shard_map/ppermute | solution.py:498
  2.7 5.2 %collective-permute-start.2 = (f32[3,28,128]{2,1,0:T(8,128)S(1)}, f32[3,28,128]{2,1,0:T(8,128)S(1)}, u32[]{:S(2)}, u32[]{:S(2)}) collective-permute-start(f32[3,28,128]{2,1,0:T(8,128)S(1)} %get-tuple-element.33), channel_id=1, source_target_pairs={{0,1},{1,0},{2,3},{3,2},{4,5},{5,4},{6,7},{7,6},{8,9},{9,8},{10,11... | collective-permute-start | bytes 129032 | tf_op jit(solution)/shard_map/ppermute | solution.py:497
  5.9 14.4 %collective-permute-start = (f32[608,128]{1,0:T(8,128)S(1)}, f32[608,128]{1,0:T(8,128)S(1)}, u32[]{:S(2)}, u32[]{:S(2)}) collective-permute-start(f32[608,128]{1,0:T(8,128)S(1)} %get-tuple-element.31), channel_id=1, source_target_pairs={{0,1},{1,0},{2,3},{3,2},{4,5},{5,4},{6,7},{7,6},{8,16},{9,17},{10,... | collective-permute-start | bytes 933896 | tf_op jit(solution)/shard_map/ppermute | solution.py:496
  8.0 5.0 %collective-permute-start.4 = (f32[752,128]{1,0:T(8,128)S(1)}, f32[752,128]{1,0:T(8,128)S(1)}, u32[]{:S(2)}, u32[]{:S(2)}) collective-permute-start(f32[752,128]{1,0:T(8,128)S(1)} %get-tuple-element.36), channel_id=1, source_target_pairs={{0,8},{8,0},{16,24},{24,16},{32,40},{40,32},{48,56},{56,48},{64,72... | collective-permute-start | bytes 1155080 | tf_op jit(solution)/shard_map/ppermute | solution.py:504
  8.1 4.9 %copy-start = (f32[8,6]{1,0:T(8,128)S(1)}, f32[8,6]{1,0:T(8,128)}, u32[]{:S(2)}) copy-start(f32[8,6]{1,0:T(8,128)} %stiffness.1) | copy-start | bytes 580
  8.1 12.8 %collective-permute-start.3 = (f32[112,128]{1,0:T(8,128)S(1)}, f32[112,128]{1,0:T(8,128)S(1)}, u32[]{:S(2)}, u32[]{:S(2)}) collective-permute-start(f32[112,128]{1,0:T(8,128)S(1)} %get-tuple-element.35), channel_id=1, source_target_pairs={{0,1},{1,0},{2,3},{3,2},{4,5},{5,4},{6,7},{7,6},{8,16},{9,17},{10,... | collective-permute-start | bytes 172040 | tf_op jit(solution)/shard_map/ppermute | solution.py:503

commit v5 on v4

--- a/solution.py
+++ b/solution.py
@@ -82,39 +82,44 @@
 
 
 def pack_first(
-    count, disp, rhs, labels, cells_in, mult_in,
-    far, y_pair, y_other, own, cells, mult,
-    raw_labels, raw_cells, arrived,
+    disp, rhs, labels, cells_in, mult_in,
+    y_other, y_pair, own, cells, mult,
+    raw_labels, arrived,
 ):
     flip = odd("gx")
-    pairs = [(cells_in, raw_cells), (mult_in, mult)]
+    pairs = []
     for g in range(CX):
         x = g + flip * (CX - 1 - 2 * g)
         pairs.append((labels.at[rows_of(x, CY)], raw_labels.at[rows_of(g, CY)]))
         for c in range(3):
             pairs.append((disp.at[rows_of(c * CX + x, CY)], own.at[rows_of(c * CX + g, CY)]))
             pairs.append((rhs.at[rows_of(c * CX + x, CY)], own.at[rows_of(OWN_RHS0 + c * CX + g, CY)]))
+    pairs += [(cells_in, cells), (mult_in, mult)]
     copies = [pltpu.make_async_copy(a, b, arrived.at[i]) for i, (a, b) in enumerate(pairs)]
     for copy in copies:
         copy.start()
     for copy in copies:
         copy.wait()
-    block_plane = raw_cells[...] // (CY * NZ)
-    turned = raw_cells[...] + flip * (CX - 1 - 2 * block_plane) * (CY * NZ)
-    live_cells = jnp.where(slot_number() < count[0, 0], turned, -1)
-    cells[...] = live_cells
     own[pl.ds(OWN_LAB0 * CY, CX * CY), :] = raw_labels[...].astype(F32)
-    for place, first, k in sent_planes():
-        far[rows_of(place, CY), :] = own[rows_of(first + k, CY), :]
-    far[pl.ds(SIDE * CY, SLOT_ROWS), :] = live_cells.astype(F32)
-    for c in range(3):
-        far[pl.ds(SIDE * CY + (1 + c) * SLOT_ROWS, SLOT_ROWS), :] = mult[c]
     up = odd("gy") == 0
     for k in range(HALO):
         first = own[pl.ds(k, OWN, stride=CY), :]
         last = own[pl.ds(CY - HALO + k, OWN, stride=CY), :]
         y_pair[k] = jnp.where(up, last, first)
         y_other[k] = jnp.where(up, first, last)
+
+
+def pack_far(count, own, raw_cells, mult, far, cells):
+    flip = odd("gx")
+    block_plane = raw_cells[...] // (CY * NZ)
+    turned = raw_cells[...] + flip * (CX - 1 - 2 * block_plane) * (CY * NZ)
+    live_cells = jnp.where(slot_number() < count[0, 0], turned, -1)
+    cells[...] = live_cells
+    for place, first, k in sent_planes():
+        far[rows_of(place, CY), :] = own[rows_of(first + k, CY), :]
+    far[pl.ds(SIDE * CY, SLOT_ROWS), :] = live_cells.astype(F32)
+    for c in range(3):
+        far[pl.ds(SIDE * CY + (1 + c) * SLOT_ROWS, SLOT_ROWS), :] = mult[c]
 
 
 def pack_second(y_other, y_pair, own, cells, mult, corner, near, wide):
@@ -473,25 +478,21 @@
 def body(displacement, rhs, labels, stiffness, rows, counts, multipliers):
     block = CX * CY
     copies = 2 + 7 * CX
-    far, y_pair, y_other, own, cells, mult = call(
+    slots = jax.ShapeDtypeStruct((SLOT_ROWS, 128), jnp.int32)
+    y_other, y_pair, own, raw_cells, mult = call(
         pack_first,
-        [
-            f32(SIDE * CY + IFACE, NZ), f32(HALO, OWN, NZ), f32(HALO, OWN, NZ), f32(OWN * CY, NZ),
-            jax.ShapeDtypeStruct((SLOT_ROWS, 128), jnp.int32), f32(3, SLOT_ROWS, 128),
-        ],
-        [SMEM] + [HBM] * 5,
-        scratch=[
-            pltpu.VMEM((block, NZ), jnp.int32),
-            pltpu.VMEM((SLOT_ROWS, 128), jnp.int32),
-            pltpu.SemaphoreType.DMA((copies,)),
-        ],
+        [f32(HALO, OWN, NZ), f32(HALO, OWN, NZ), f32(OWN * CY, NZ), slots, f32(3, SLOT_ROWS, 128)],
+        [HBM] * 5,
+        scratch=[pltpu.VMEM((block, NZ), jnp.int32), pltpu.SemaphoreType.DMA((copies,))],
     )(
-        counts,
         in_hbm(displacement.reshape(3 * block, NZ)),
         in_hbm(rhs.reshape(3 * block, NZ)),
         in_hbm(labels.reshape(block, NZ)),
         in_hbm(rows.reshape(SLOT_ROWS, 128)),
         in_hbm(multipliers.reshape(3, SLOT_ROWS, 128)),
+    )
+    far, cells = call(pack_far, [f32(SIDE * CY + IFACE, NZ), slots], [SMEM] + [VMEM] * 3)(
+        counts, own, raw_cells, mult
     )
     far = lax.ppermute(far, ("gx", "gy"), other_x())
     y_pair = lax.ppermute(y_pair, "gy", pair(N_GY))

time: 33.9 us -> 34 us (level)
  starting transfers between devices: 8.05 us -> 8.92 us
  waiting for transfers between devices: 6.19 us -> 5.42 us
    ppermute x1, waiting for transfers between devices: 1.34 us -> 0.56 us  [body(): y_pair = lax.ppermute(y_pair, 'gy', pair(N_GY))]
    ppermute x1, starting transfers between devices: 3.99 us -> 4.47 us  [body(): corner = lax.ppermute(corner, ('gx', 'gy'), other_x())]
    pallas_call x1 -> x2, Pallas kernels: 1.33 us -> 1.33 us  [the longest x1 1.3 us: body(): call(pack_first, [f32(HALO, OWN, NZ), f32(HALO, OWN, NZ), f32(OWN * CY, N...]
where the time goes in v5:
time: 34 us; the launch traced here: 33.3 us
  blocking collectives  9.34 us (27%)
  starting transfers between devices  8.92 us (26%)
  Pallas kernels  8.3 us (24%)
  waiting for transfers between devices  5.42 us (16%)
  between operations  1.36 us (4%)
    all_to_all x1, blocking collectives, body(): gathered = lax.all_to_all(message, 'gy', 0, 0)  9.34 us
    ppermute x1, waiting for transfers between devices, body(): far = lax.ppermute(far, ('gx', 'gy'), other_x())  4.62 us
    ppermute x1, starting transfers between devices, body(): corner = lax.ppermute(corner, ('gx', 'gy'), other_x())  4.47 us
    ppermute x1, starting transfers between devices, body(): y_pair = lax.ppermute(y_pair, 'gy', pair(N_GY))  3.14 us
    pallas_call x1, Pallas kernels, body(): call(near_part, arrays + [f32(LABELS * 6, NZ), f32(3 * CY, NZ)], [SMEM, V...  2.68 us
    pallas_call x1, Pallas kernels, body(): call(far_part, [f32(3 * block, NZ), f32(3, (CX + 1) * CY, NZ), f32(N_GY,...  1.71 us
    pallas_call x1, Pallas kernels, body(): call(pack_first, [f32(HALO, OWN, NZ), f32(HALO, OWN, NZ), f32(OWN * CY, N...  1.3 us
    pallas_call x1, Pallas kernels, body(): call(finish, [pltpu.HBM(s, F32) for s in ((3 * block, NZ), (3, SLOT_ROWS,...  1.27 us
  transfers between devices with their start and end apart: 5, of which 3 were waited for; matrix products, arithmetic and copies ran while one was open for 0% of the time, Pallas kernels for 12%

profile of v5, /device:TPU:128, one launch (start us, length us, event | category | flops | bytes accessed | tf_op | source)
XLA Modules:
  0.0 33.3 jit_solution(5120628181900411627)
XLA Ops:
  0.6 1.3 %shard_map.94 = (f32[3,28,128]{2,1,0:T(8,128)S(1)}, f32[3,28,128]{2,1,0:T(8,128)S(1)}, f32[896,128]{1,0:T(8,128)S(1)}, s32[8,128]{1,0:T(8,128)S(1)}, f32[3,8,128]{2,1,0:T(8,128)S(1)}) custom-call(f32[384,128]{1,0:T(8,128)} %bitcast.10, f32[384,128]{1,0:T(8,128)} %bitcast.11, s32[128,128]{1,0:T(8,128)} %bitcast.12, s32[8,128]{1,0:T(8,128)} %bitcast.14, ...), custom_call_target="tpu_custom_call" | custom-call | flops 1000 | bytes 1000 | tf_op jit(solution)/shard_map/pallas_call | solution.py:482
  1.9 0.1 collective-permute-start.1
  2.0 3.1 %collective-permute-start.2 = (f32[3,28,128]{2,1,0:T(8,128)S(1)}, f32[3,28,128]{2,1,0:T(8,128)S(1)}, u32[]{:S(2)}, u32[]{:S(2)}) collective-permute-start(f32[3,28,128]{2,1,0:T(8,128)S(1)} %get-tuple-element.36), channel_id=1, source_target_pairs={{0,1},{1,0},{2,3},{3,2},{4,5},{5,4},{6,7},{7,6},{8,9},{9,8},{10,11... | collective-permute-start | bytes 129032 | tf_op jit(solution)/shard_map/ppermute | solution.py:498
  5.9 0.8 %collective-permute-start = (f32[608,128]{1,0:T(8,128)S(1)}, f32[608,128]{1,0:T(8,128)S(1)}, u32[]{:S(2)}, u32[]{:S(2)}) collective-permute-start(f32[608,128]{1,0:T(8,128)S(1)} %get-tuple-element.34), channel_id=1, source_target_pairs={{0,1},{1,0},{2,3},{3,2},{4,5},{5,4},{6,7},{7,6},{8,16},{9,17},{10,... | collective-permute-start | bytes 933896 | tf_op jit(solution)/shard_map/ppermute | solution.py:497
  6.7 0.0 collective-permute-done.1.y_other
  6.7 0.6 %collective-permute-done.2.y_pair = f32[3,28,128]{2,1,0:T(8,128)S(1)} collective-permute-done((f32[3,28,128]{2,1,0:T(8,128)S(1)}, f32[3,28,128]{2,1,0:T(8,128)S(1)}, u32[]{:S(2)}, u32[]{:S(2)}) %collective-permute-start.2) | collective-permute-done | bytes 43040 | tf_op jit(solution)/shard_map/ppermute | solution.py:498
  7.3 0.1 shard_map.96
  7.3 0.4 %collective-permute-start.4 = (f32[752,128]{1,0:T(8,128)S(1)}, f32[752,128]{1,0:T(8,128)S(1)}, u32[]{:S(2)}, u32[]{:S(2)}) collective-permute-start(f32[752,128]{1,0:T(8,128)S(1)} %get-tuple-element.38), channel_id=1, source_target_pairs={{0,8},{8,0},{16,24},{24,16},{32,40},{40,32},{48,56},{56,48},{64,72... | collective-permute-start | bytes 1155080 | tf_op jit(solution)/shard_map/ppermute | solution.py:505
  7.7 0.0 copy-start
  7.7 4.5 %collective-permute-start.3 = (f32[112,128]{1,0:T(8,128)S(1)}, f32[112,128]{1,0:T(8,128)S(1)}, u32[]{:S(2)}, u32[]{:S(2)}) collective-permute-start(f32[112,128]{1,0:T(8,128)S(1)} %get-tuple-element.37), channel_id=1, source_target_pairs={{0,1},{1,0},{2,3},{3,2},{4,5},{5,4},{6,7},{7,6},{8,16},{9,17},{10,... | collective-permute-start | bytes 172040 | tf_op jit(solution)/shard_map/ppermute | solution.py:504
  12.2 0.8 %shard_map.97.dense = f32[4,128,128]{2,1,0:T(8,128)S(1)} custom-call(s32[8,128]{1,0:T(8,128)S(1)} %get-tuple-element.33.cells, f32[3,8,128]{2,1,0:T(8,128)S(1)} %get-tuple-element.32.mult), custom_call_target="tpu_custom_call" | custom-call | flops 99999997952 | bytes 1000 | tf_op jit(solution)/shard_map/pallas_call | solution.py:500
  13.1 0.0 collective-permute-done.4.near
  13.1 0.0 copy-done
  13.1 2.7 %shard_map.98 = (f32[2560,128]{1,0:T(8,128)S(1)}, f32[2400,128]{1,0:T(8,128)S(1)}, f32[2400,128]{1,0:T(8,128)S(1)}, f32[1200,128]{1,0:T(8,128)S(1)}, f32[1200,12...) custom-call(f32[8,6]{1,0:T(8,128)S(1)} %copy-done, ...), custom_call_target="tpu_custom_call" | custom-call | flops 1000 | bytes 1000 | tf_op jit(solution)/shard_map/pallas_call | solution.py:508
  15.8 4.6 %collective-permute-done.far = f32[608,128]{1,0:T(8,128)S(1)} collective-permute-done((f32[608,128]{1,0:T(8,128)S(1)}, f32[608,128]{1,0:T(8,128)S(1)}, u32[]{:S(2)}, u32[]{:S(2)}) %collective-permute-start) | collective-permute-done | bytes 311328 | tf_op jit(solution)/shard_map/ppermute | solution.py:497
  20.4 0.4 %shard_map.99.ribbon = f32[4,192,128]{2,1,0:T(8,128)S(1)} custom-call(f32[608,128]{1,0:T(8,128)S(1)} %collective-permute-done.far, f32[752,128]{1,0:T(8,128)S(1)} %collective-permute-done.4.near, f32[4,128,128]{2,1,0:T(8,128)S(1)} %shard_map.97.dense, f32[96,128]{1,0:T(8,128)S(1)} %get-tuple-element.40.last), custom_call_target="tpu_custom_call" | custom-call | flops 1000 | bytes 1000 | tf_op jit(solution)/shard_map/pallas_call | solution.py:511
  20.8 0.2 collective-permute-done.3.corner
  21.0 1.7 %shard_map.100 = (f32[384,128]{1,0:T(8,128)S(1)}, f32[3,160,128]{2,1,0:T(8,128)S(1)}, f32[8,48,128]{2,1,0:T(8,128)S(1)}) custom-call(f32[608,128]{1,0:T(8,128)S(1)} %collective-permute-done.far, f32[112,128]{1,0:T(8,128)S(1)} %collective-permute-done.3.corner, f32[4,192,128]{2,1,0:T(8,128)S(1)} %shard_map.99.ribbon, ...), custom_call_target="tpu_custom_call" | custom-call | flops 1000 | bytes 1000 | tf_op jit(solution)/shard_map/pallas_call | solution.py:512
  22.7 9.3 %all_to_all.5.gathered = f32[8,48,128]{2,1,0:T(8,128)S(1)} all-to-all(f32[8,48,128]{2,1,0:T(8,128)S(1)} %get-tuple-element.53), channel_id=1, replica_groups=mesh['gx'=32,'gy'=8] {'gy'}, dimensions={0} | all-to-all | bytes 393216 | tf_op jit(solution)/shard_map/all_to_all | solution.py:518
  32.1 1.3 %shard_map.101 = (f32[384,128]{1,0:T(8,128)}, f32[3,8,128]{2,1,0:T(8,128)}, f32[3,128,128]{2,1,0:T(8,128)}) custom-call(s32[8,128]{1,0:T(8,128)S(1)} %get-tuple-element.33.cells, f32[3,8,128]{2,1,0:T(8,128)S(1)} %get-tuple-element.32.mult, f32[3,160,128]{2,1,0:T(8,128)S(1)} %get-tuple-element.51.jumps, f32[384,128]{1,0:T(8,128)S(1)} %get-tuple-element.52.smoothed, ...), custom_call_target="tpu_custom_call" | custom-call | flops 1000 | bytes 1000 | tf_op jit(solution)/shard_map/pallas_call | solution.py:519
  (1 shorter events, 0.0 us)
Async XLA Ops:
  1.9 4.7 %collective-permute-start.1 = (f32[3,28,128]{2,1,0:T(8,128)S(1)}, f32[3,28,128]{2,1,0:T(8,128)S(1)}, u32[]{:S(2)}, u32[]{:S(2)}) collective-permute-start(f32[3,28,128]{2,1,0:T(8,128)S(1)} %get-tuple-element.35), channel_id=1, source_target_pairs={{0,8},{1,2},{2,1},{3,4},{4,3},{5,6},{6,5},{7,15},{8,0},{9,10},{10,... | collective-permute-start | bytes 129032 | tf_op jit(solution)/shard_map/ppermute | solution.py:499
  2.0 5.2 %collective-permute-start.2 = (f32[3,28,128]{2,1,0:T(8,128)S(1)}, f32[3,28,128]{2,1,0:T(8,128)S(1)}, u32[]{:S(2)}, u32[]{:S(2)}) collective-permute-start(f32[3,28,128]{2,1,0:T(8,128)S(1)} %get-tuple-element.36), channel_id=1, source_target_pairs={{0,1},{1,0},{2,3},{3,2},{4,5},{5,4},{6,7},{7,6},{8,9},{9,8},{10,11... | collective-permute-start | bytes 129032 | tf_op jit(solution)/shard_map/ppermute | solution.py:498
  5.9 14.5 %collective-permute-start = (f32[608,128]{1,0:T(8,128)S(1)}, f32[608,128]{1,0:T(8,128)S(1)}, u32[]{:S(2)}, u32[]{:S(2)}) collective-permute-start(f32[608,128]{1,0:T(8,128)S(1)} %get-tuple-element.34), channel_id=1, source_target_pairs={{0,1},{1,0},{2,3},{3,2},{4,5},{5,4},{6,7},{7,6},{8,16},{9,17},{10,... | collective-permute-start | bytes 933896 | tf_op jit(solution)/shard_map/ppermute | solution.py:497
  7.3 5.7 %collective-permute-start.4 = (f32[752,128]{1,0:T(8,128)S(1)}, f32[752,128]{1,0:T(8,128)S(1)}, u32[]{:S(2)}, u32[]{:S(2)}) collective-permute-start(f32[752,128]{1,0:T(8,128)S(1)} %get-tuple-element.38), channel_id=1, source_target_pairs={{0,8},{8,0},{16,24},{24,16},{32,40},{40,32},{48,56},{56,48},{64,72... | collective-permute-start | bytes 1155080 | tf_op jit(solution)/shard_map/ppermute | solution.py:505
  7.7 5.3 %copy-start = (f32[8,6]{1,0:T(8,128)S(1)}, f32[8,6]{1,0:T(8,128)}, u32[]{:S(2)}) copy-start(f32[8,6]{1,0:T(8,128)} %stiffness.1) | copy-start | bytes 580
  7.7 13.3 %collective-permute-start.3 = (f32[112,128]{1,0:T(8,128)S(1)}, f32[112,128]{1,0:T(8,128)S(1)}, u32[]{:S(2)}, u32[]{:S(2)}) collective-permute-start(f32[112,128]{1,0:T(8,128)S(1)} %get-tuple-element.37), channel_id=1, source_target_pairs={{0,1},{1,0},{2,3},{3,2},{4,5},{5,4},{6,7},{7,6},{8,16},{9,17},{10,... | collective-permute-start | bytes 172040 | tf_op jit(solution)/shard_map/ppermute | solution.py:504

commit v6 on v5

--- a/solution.py
+++ b/solution.py
@@ -26,6 +26,7 @@
 OWN = OWN_RHS0 + 3 * CX
 SIDE = 3 * HALO + HALO + 3 * (HALO - 1)
 SLOT_ROWS = SLOTS // 128
+CORNER = 112
 IFACE = 4 * SLOT_ROWS
 VMEM = pl.BlockSpec(memory_space=pltpu.VMEM)
 SMEM = pl.BlockSpec(memory_space=pltpu.SMEM)
@@ -109,20 +110,19 @@
         y_other[k] = jnp.where(up, first, last)
 
 
-def pack_far(count, own, raw_cells, mult, far, cells):
+def pack_far(own, raw_cells, mult, far, cells):
     flip = odd("gx")
     block_plane = raw_cells[...] // (CY * NZ)
     turned = raw_cells[...] + flip * (CX - 1 - 2 * block_plane) * (CY * NZ)
-    live_cells = jnp.where(slot_number() < count[0, 0], turned, -1)
-    cells[...] = live_cells
+    cells[...] = turned
     for place, first, k in sent_planes():
         far[rows_of(place, CY), :] = own[rows_of(first + k, CY), :]
-    far[pl.ds(SIDE * CY, SLOT_ROWS), :] = live_cells.astype(F32)
+    far[pl.ds(SIDE * CY, SLOT_ROWS), :] = turned.astype(F32)
     for c in range(3):
         far[pl.ds(SIDE * CY + (1 + c) * SLOT_ROWS, SLOT_ROWS), :] = mult[c]
 
 
-def pack_second(y_other, y_pair, own, cells, mult, corner, near, wide):
+def pack_second(y_other, y_pair, count, own, cells, mult, corner, near, wide, limit):
     here = lax.axis_index("gy")
     up = odd("gy") == 0
     low = jnp.where(here > 0, 1.0, 0.0).astype(F32)
@@ -140,6 +140,10 @@
         for i, y in enumerate((CY, ROWS - HALO)):
             corner[pl.ds(place * 2 * HALO + i * HALO, HALO), :] = wide[pl.ds((first + k) * ROWS + y, HALO), :]
         near[rows_of(place, ROWS), :] = wide[rows_of(first + CX - 1 - k, ROWS), :]
+    live = jnp.full((SLOT_ROWS, 128), count[0, 0].astype(F32), F32)
+    limit[...] = live
+    corner[pl.ds(CORNER, SLOT_ROWS), :] = live
+    near[pl.ds(SIDE * ROWS + IFACE, SLOT_ROWS), :] = live
     near[pl.ds(SIDE * ROWS, SLOT_ROWS), :] = cells[...].astype(F32)
     for c in range(3):
         near[pl.ds(SIDE * ROWS + (1 + c) * SLOT_ROWS, SLOT_ROWS), :] = mult[c]
@@ -150,23 +154,23 @@
 
 
 def spread(cells, mult, first, columns):
-    column = jnp.where(cells < 0, -1, cells // NZ - first)
+    column = cells // NZ - first
     depth = cells % NZ
-    total = jnp.zeros((10 * columns, NZ), F32)
+    total = jnp.zeros((11 * columns, NZ), F32)
     parts = [piece for c in range(3) for piece in pieces_of(mult[c])]
+    parts += pieces_of((slot_number() + 1).astype(F32))[:2]
     for j in range(SLOT_ROWS // 2):
         at_column = lax.broadcasted_iota(jnp.int32, (columns, 256), 0) == paired(column, j)
         at_depth = lax.broadcasted_iota(jnp.int32, (NZ, 256), 0) == paired(depth, j)
         left = [jnp.where(at_column, paired(piece.astype(F32), j), 0.0).astype(BF16) for piece in parts]
-        left.append(jnp.where(at_column, 1.0, 0.0).astype(BF16))
         total = total + lax.dot_general(
             jnp.concatenate(left, axis=0),
             jnp.where(at_depth, 1.0, 0.0).astype(BF16),
             (((1,), (1,)), ((), ())),
             preferred_element_type=F32,
         )
-    part = [total[i * columns : (i + 1) * columns] for i in range(10)]
-    return [part[3 * c] + part[3 * c + 1] + part[3 * c + 2] for c in range(3)] + [part[9]]
+    part = [total[i * columns : (i + 1) * columns] for i in range(11)]
+    return [part[3 * c] + part[3 * c + 1] + part[3 * c + 2] for c in range(3)] + [part[9] + part[10]]
 
 
 def spread_own(cells, mult, dense):
@@ -333,7 +337,7 @@
 
 
 def far_part(
-    far, corner, ribbon,
+    far, corner, near, limit, ribbon,
     near_fields, near_coeff, near_total, near_scale, near_flux,
     near_first, near_flux_first, near_second, near_flux_second, table, last,
     smoothed, jumps, message,
@@ -367,6 +371,18 @@
     remainders = [grid.remainder(HALO + g, v2, flux2) for g in range(CX - 1)]
     remainders.append([last[rows_of(c, CY), :] for c in range(3)])
 
+    mine = limit[:1]
+    theirs = jnp.where(flip == 1, near[pl.ds(SIDE * ROWS + IFACE, 1), :], corner[pl.ds(CORNER, 1), :])
+    live = []
+    for i in range(CX + 1):
+        if i == 0:
+            top = jnp.where(flip == 1, mine, theirs)
+        elif i == CX:
+            top = jnp.where(flip == 1, theirs, mine)
+        else:
+            top = mine
+        number = ribbon[3, rows_of(i + flip, CY), :]
+        live.append((number > 0.5) & (number < top + 0.5))
     for c in range(3):
         planes = [grid.get(v2, c, HALO - 1 + i)[:CY] for i in range(CX + 2)]
         for g in range(CX):
@@ -377,7 +393,7 @@
             jump = sign * (planes[i] - planes[i + 1])
             jumps[c, rows_of(i, CY), :] = jump
             at = rows_of(i + flip, CY)
-            pushed.append(jnp.where(ribbon[3, at, :] > 0.5, ribbon[c, at, :] + PENALTY * jump, 0.0))
+            pushed.append(jnp.where(live[i], ribbon[c, at, :] + PENALTY * jump, 0.0))
         parts = [remainders[g][c] - sign * (pushed[g + 1] - pushed[g]) for g in range(CX)]
         for half in range(2):
             coarse[rows_of(half * 3 + c, CY), :] = parts[2 * half] + parts[2 * half + 1]
@@ -397,7 +413,7 @@
 
 
 def finish(
-    cells, mult, jumps, smoothed, gathered,
+    limit, cells, mult, jumps, smoothed, gathered,
     smoothed_out, updated_out, coarse_out,
     updated, coarse, done,
 ):
@@ -411,7 +427,7 @@
         parts = [gathered[s, pl.ds(c * CY // 2, CY // 2), :] for s in range(N_GY)]
         coarse[c] = jnp.transpose(jnp.concatenate(parts, axis=0))
     copies[1].start()
-    live = cells[...] >= 0
+    live = slot_number().astype(F32) < limit[...] - 0.5
     column, depth = cells[...] // NZ, cells[...] % NZ
     block = CX * CY
     start = pl.multiple_of((1 - odd("gx")) * CY, CY)
@@ -491,16 +507,19 @@
         in_hbm(rows.reshape(SLOT_ROWS, 128)),
         in_hbm(multipliers.reshape(3, SLOT_ROWS, 128)),
     )
-    far, cells = call(pack_far, [f32(SIDE * CY + IFACE, NZ), slots], [SMEM] + [VMEM] * 3)(
-        counts, own, raw_cells, mult
-    )
+    far, cells = call(pack_far, [f32(SIDE * CY + IFACE, NZ), slots], [VMEM] * 3)(own, raw_cells, mult)
     far = lax.ppermute(far, ("gx", "gy"), other_x())
     y_pair = lax.ppermute(y_pair, "gy", pair(N_GY))
     y_other = lax.ppermute(y_other, ("gx", "gy"), other_y())
     (dense,) = call(spread_own, [f32(4, block, NZ)], [VMEM] * 2, flops=100000000000)(cells, mult)
-    corner, near, own = call(
-        pack_second, [f32(SIDE * 2 * HALO + 4, NZ), f32(SIDE * ROWS + IFACE, NZ), f32(OWN * ROWS, NZ)], [VMEM] * 5
-    )(y_other, y_pair, own, cells, mult)
+    corner, near, own, limit = call(
+        pack_second,
+        [
+            f32(CORNER + SLOT_ROWS, NZ), f32(SIDE * ROWS + IFACE + SLOT_ROWS, NZ), f32(OWN * ROWS, NZ),
+            f32(SLOT_ROWS, NZ),
+        ],
+        [VMEM, VMEM, SMEM, VMEM, VMEM, VMEM],
+    )(y_other, y_pair, counts, own, cells, mult)
     corner = lax.ppermute(corner, ("gx", "gy"), other_x())
     near = lax.ppermute(near, "gx", pair(N_GX))
     three, six = f32(3 * PX * ROWS, NZ), f32(6 * PX * ROWS, NZ)
@@ -512,21 +531,21 @@
     smoothed, jumps, message = call(
         far_part,
         [f32(3 * block, NZ), f32(3, (CX + 1) * CY, NZ), f32(N_GY, 3 * CY // 2, NZ)],
-        [VMEM] * (3 + len(half)),
+        [VMEM] * (5 + len(half)),
         scratch=[pltpu.VMEM(a.shape, F32) for a in arrays] + [pltpu.VMEM((6 * CY, NZ), F32)],
-    )(far, corner, ribbon, *half)
+    )(far, corner, near, limit, ribbon, *half)
     gathered = lax.all_to_all(message, "gy", 0, 0)
     smoothed, updated, coarse = call(
         finish,
         [pltpu.HBM(s, F32) for s in ((3 * block, NZ), (3, SLOT_ROWS, 128), (3, CX // 2 * NZ // 2, NY // 2))],
-        [VMEM] * 5,
+        [VMEM] * 6,
         out_specs=[HBM] * 3,
         scratch=[
             pltpu.VMEM((3, SLOT_ROWS, 128), F32),
             pltpu.VMEM((3, CX // 2 * NZ // 2, NY // 2), F32),
             pltpu.SemaphoreType.DMA((3,)),
         ],
-    )(cells, mult, jumps, smoothed, gathered)
+    )(limit, cells, mult, jumps, smoothed, gathered)
     coarse = jnp.swapaxes(coarse.reshape(3, CX // 2, NZ // 2, NY // 2), 2, 3)
     return (smoothed.reshape(3, CX, CY, NZ), coarse, updated.reshape(3, 1, 1, SLOTS))
 

time: 34 us -> 33.5 us (0.985)
  waiting for transfers between devices: 5.42 us -> 4.89 us
    ppermute x1, waiting for transfers between devices: 4.62 us -> 3.25 us  [body(): far = lax.ppermute(far, ('gx', 'gy'), other_x())]
    ppermute x1, waiting for transfers between devices: 0.01 us -> 0.8 us  [body(): near = lax.ppermute(near, 'gx', pair(N_GX))]
    ppermute x1, starting transfers between devices: 0.41 us -> 0.01 us  [body(): near = lax.ppermute(near, 'gx', pair(N_GX))]
  transfers between devices with their start and end apart: 5 -> 5, of which waited for: 3 -> 4; matrix products, arithmetic and copies ran while one was open for 0% -> 0% of each run, Pallas kernels for 12% -> 12%
where the time goes in v6:
time: 33.5 us; the launch traced here: 33 us
  blocking collectives  9.51 us (28%)
  starting transfers between devices  8.82 us (26%)
  Pallas kernels  8.38 us (25%)
  waiting for transfers between devices  4.89 us (15%)
  between operations  1.35 us (4%)
    all_to_all x1, blocking collectives, body(): gathered = lax.all_to_all(message, 'gy', 0, 0)  9.51 us
    ppermute x1, starting transfers between devices, body(): corner = lax.ppermute(corner, ('gx', 'gy'), other_x())  4.77 us
    ppermute x1, waiting for transfers between devices, body(): far = lax.ppermute(far, ('gx', 'gy'), other_x())  3.25 us
    ppermute x1, starting transfers between devices, body(): y_pair = lax.ppermute(y_pair, 'gy', pair(N_GY))  3.14 us
    pallas_call x1, Pallas kernels, body(): call(near_part, arrays + [f32(LABELS * 6, NZ), f32(3 * CY, NZ)], [SMEM, V...  2.68 us
    pallas_call x1, Pallas kernels, body(): call(far_part, [f32(3 * block, NZ), f32(3, (CX + 1) * CY, NZ), f32(N_GY,...  1.73 us
    pallas_call x1, Pallas kernels, body(): call(pack_first, [f32(HALO, OWN, NZ), f32(HALO, OWN, NZ), f32(OWN * CY, N...  1.3 us
    pallas_call x1, Pallas kernels, body(): call(finish, [pltpu.HBM(s, F32) for s in ((3 * block, NZ), (3, SLOT_ROWS,...  1.27 us
  transfers between devices with their start and end apart: 5, of which 4 were waited for; matrix products, arithmetic and copies ran while one was open for 0% of the time, Pallas kernels for 12%

profile of v6, /device:TPU:128, one launch (start us, length us, event | category | flops | bytes accessed | tf_op | source)
XLA Modules:
  0.0 33.0 jit_solution(12644237941165422552)
XLA Ops:
  0.6 1.3 %shard_map.94 = (f32[3,28,128]{2,1,0:T(8,128)S(1)}, f32[3,28,128]{2,1,0:T(8,128)S(1)}, f32[896,128]{1,0:T(8,128)S(1)}, s32[8,128]{1,0:T(8,128)S(1)}, f32[3,8,128]{2,1,0:T(8,128)S(1)}) custom-call(f32[384,128]{1,0:T(8,128)} %bitcast.10, f32[384,128]{1,0:T(8,128)} %bitcast.11, s32[128,128]{1,0:T(8,128)} %bitcast.12, s32[8,128]{1,0:T(8,128)} %bitcast.14, ...), custom_call_target="tpu_custom_call" | custom-call | flops 1000 | bytes 1000 | tf_op jit(solution)/shard_map/pallas_call | solution.py:498
  1.9 0.1 collective-permute-start
  2.0 3.1 %collective-permute-start.1 = (f32[3,28,128]{2,1,0:T(8,128)S(1)}, f32[3,28,128]{2,1,0:T(8,128)S(1)}, u32[]{:S(2)}, u32[]{:S(2)}) collective-permute-start(f32[3,28,128]{2,1,0:T(8,128)S(1)} %get-tuple-element.32), channel_id=1, source_target_pairs={{0,1},{1,0},{2,3},{3,2},{4,5},{5,4},{6,7},{7,6},{8,9},{9,8},{10,11... | collective-permute-start | bytes 129032 | tf_op jit(solution)/shard_map/ppermute | solution.py:512
  5.2 0.8 %collective-permute-start.2 = (f32[608,128]{1,0:T(8,128)S(1)}, f32[608,128]{1,0:T(8,128)S(1)}, u32[]{:S(2)}, u32[]{:S(2)}) collective-permute-start(f32[608,128]{1,0:T(8,128)S(1)} %get-tuple-element.38), channel_id=1, source_target_pairs={{0,1},{1,0},{2,3},{3,2},{4,5},{5,4},{6,7},{7,6},{8,16},{9,17},{10,... | collective-permute-start | bytes 933896 | tf_op jit(solution)/shard_map/ppermute | solution.py:511
  6.7 0.0 collective-permute-done.y_other
  6.7 0.6 %collective-permute-done.1.y_pair = f32[3,28,128]{2,1,0:T(8,128)S(1)} collective-permute-done((f32[3,28,128]{2,1,0:T(8,128)S(1)}, f32[3,28,128]{2,1,0:T(8,128)S(1)}, u32[]{:S(2)}, u32[]{:S(2)}) %collective-permute-start.1) | collective-permute-done | bytes 43040 | tf_op jit(solution)/shard_map/ppermute | solution.py:512
  7.3 0.1 shard_map.96
  7.3 4.8 %collective-permute-start.3 = (f32[120,128]{1,0:T(8,128)S(1)}, f32[120,128]{1,0:T(8,128)S(1)}, u32[]{:S(2)}, u32[]{:S(2)}) collective-permute-start(f32[120,128]{1,0:T(8,128)S(1)} %get-tuple-element.39), channel_id=1, source_target_pairs={{0,1},{1,0},{2,3},{3,2},{4,5},{5,4},{6,7},{7,6},{8,16},{9,17},{10,... | collective-permute-start | bytes 184328 | tf_op jit(solution)/shard_map/ppermute | solution.py:523
  12.1 0.0 copy-start
  12.1 0.0 collective-permute-start.4
  12.1 0.9 %shard_map.97.dense = f32[4,128,128]{2,1,0:T(8,128)S(1)} custom-call(s32[8,128]{1,0:T(8,128)S(1)} %get-tuple-element.36.cells, f32[3,8,128]{2,1,0:T(8,128)S(1)} %get-tuple-element.35.mult), custom_call_target="tpu_custom_call" | custom-call | flops 99999997952 | bytes 1000 | tf_op jit(solution)/shard_map/pallas_call | solution.py:514
  13.0 0.8 %collective-permute-done.4.near = f32[760,128]{1,0:T(8,128)S(1)} collective-permute-done((f32[760,128]{1,0:T(8,128)S(1)}, f32[760,128]{1,0:T(8,128)S(1)}, u32[]{:S(2)}, u32[]{:S(2)}) %collective-permute-start.4) | collective-permute-done | bytes 389152 | tf_op jit(solution)/shard_map/ppermute | solution.py:524
  13.8 0.0 copy-done
  13.8 2.7 %shard_map.98 = (f32[2560,128]{1,0:T(8,128)S(1)}, f32[2400,128]{1,0:T(8,128)S(1)}, f32[2400,128]{1,0:T(8,128)S(1)}, f32[1200,128]{1,0:T(8,128)S(1)}, f32[1200,12...) custom-call(f32[8,6]{1,0:T(8,128)S(1)} %copy-done, ...), custom_call_target="tpu_custom_call" | custom-call | flops 1000 | bytes 1000 | tf_op jit(solution)/shard_map/pallas_call | solution.py:527
  16.5 3.3 %collective-permute-done.2.far = f32[608,128]{1,0:T(8,128)S(1)} collective-permute-done((f32[608,128]{1,0:T(8,128)S(1)}, f32[608,128]{1,0:T(8,128)S(1)}, u32[]{:S(2)}, u32[]{:S(2)}) %collective-permute-start.2) | collective-permute-done | bytes 311328 | tf_op jit(solution)/shard_map/ppermute | solution.py:511
  19.8 0.4 %shard_map.99.ribbon = f32[4,192,128]{2,1,0:T(8,128)S(1)} custom-call(f32[608,128]{1,0:T(8,128)S(1)} %collective-permute-done.2.far, f32[760,128]{1,0:T(8,128)S(1)} %collective-permute-done.4.near, f32[4,128,128]{2,1,0:T(8,128)S(1)} %shard_map.97.dense, f32[96,128]{1,0:T(8,128)S(1)} %get-tuple-element.42.last), custom_call_target="tpu_custom_call" | custom-call | flops 1000 | bytes 1000 | tf_op jit(solution)/shard_map/pallas_call | solution.py:530
  20.2 0.3 collective-permute-done.3.corner
  20.4 1.7 %shard_map.100 = (f32[384,128]{1,0:T(8,128)S(1)}, f32[3,160,128]{2,1,0:T(8,128)S(1)}, f32[8,48,128]{2,1,0:T(8,128)S(1)}) custom-call(f32[608,128]{1,0:T(8,128)S(1)} %collective-permute-done.2.far, f32[120,128]{1,0:T(8,128)S(1)} %collective-permute-done.3.corner, f32[760,128]{1,0:T(8,128)S(1)} %collective-permute-done.4.near, ...), custom_call_target="tpu_custom_call" | custom-call | flops 1000 | bytes 1000 | tf_op jit(solution)/shard_map/pallas_call | solution.py:531
  22.2 9.5 %all_to_all.5.gathered = f32[8,48,128]{2,1,0:T(8,128)S(1)} all-to-all(f32[8,48,128]{2,1,0:T(8,128)S(1)} %get-tuple-element.55), channel_id=1, replica_groups=mesh['gx'=32,'gy'=8] {'gy'}, dimensions={0} | all-to-all | bytes 393216 | tf_op jit(solution)/shard_map/all_to_all | solution.py:537
  31.7 1.3 %shard_map.101 = (f32[384,128]{1,0:T(8,128)}, f32[3,8,128]{2,1,0:T(8,128)}, f32[3,128,128]{2,1,0:T(8,128)}) custom-call(f32[8,128]{1,0:T(8,128)S(1)} %get-tuple-element.37.limit, s32[8,128]{1,0:T(8,128)S(1)} %get-tuple-element.36.cells, f32[3,8,128]{2,1,0:T(8,128)S(1)} %get-tuple-element.35.mult, f32[3,160,128]{2,1,0:T(8,128)S(1)} %get-tuple-element.53.jumps, ...), custom_call_target="tpu_custom_call" | custom-call | flops 1000 | bytes 1000 | tf_op jit(solution)/shard_map/pallas_call | solution.py:538
  (1 shorter events, 0.0 us)
Async XLA Ops:
  1.9 4.7 %collective-permute-start = (f32[3,28,128]{2,1,0:T(8,128)S(1)}, f32[3,28,128]{2,1,0:T(8,128)S(1)}, u32[]{:S(2)}, u32[]{:S(2)}) collective-permute-start(f32[3,28,128]{2,1,0:T(8,128)S(1)} %get-tuple-element.31), channel_id=1, source_target_pairs={{0,8},{1,2},{2,1},{3,4},{4,3},{5,6},{6,5},{7,15},{8,0},{9,10},{10,... | collective-permute-start | bytes 129032 | tf_op jit(solution)/shard_map/ppermute | solution.py:513
  2.0 5.2 %collective-permute-start.1 = (f32[3,28,128]{2,1,0:T(8,128)S(1)}, f32[3,28,128]{2,1,0:T(8,128)S(1)}, u32[]{:S(2)}, u32[]{:S(2)}) collective-permute-start(f32[3,28,128]{2,1,0:T(8,128)S(1)} %get-tuple-element.32), channel_id=1, source_target_pairs={{0,1},{1,0},{2,3},{3,2},{4,5},{5,4},{6,7},{7,6},{8,9},{9,8},{10,11... | collective-permute-start | bytes 129032 | tf_op jit(solution)/shard_map/ppermute | solution.py:512
  5.2 14.6 %collective-permute-start.2 = (f32[608,128]{1,0:T(8,128)S(1)}, f32[608,128]{1,0:T(8,128)S(1)}, u32[]{:S(2)}, u32[]{:S(2)}) collective-permute-start(f32[608,128]{1,0:T(8,128)S(1)} %get-tuple-element.38), channel_id=1, source_target_pairs={{0,1},{1,0},{2,3},{3,2},{4,5},{5,4},{6,7},{7,6},{8,16},{9,17},{10,... | collective-permute-start | bytes 933896 | tf_op jit(solution)/shard_map/ppermute | solution.py:511
  7.3 13.1 %collective-permute-start.3 = (f32[120,128]{1,0:T(8,128)S(1)}, f32[120,128]{1,0:T(8,128)S(1)}, u32[]{:S(2)}, u32[]{:S(2)}) collective-permute-start(f32[120,128]{1,0:T(8,128)S(1)} %get-tuple-element.39), channel_id=1, source_target_pairs={{0,1},{1,0},{2,3},{3,2},{4,5},{5,4},{6,7},{7,6},{8,16},{9,17},{10,... | collective-permute-start | bytes 184328 | tf_op jit(solution)/shard_map/ppermute | solution.py:523
  12.1 1.7 %copy-start = (f32[8,6]{1,0:T(8,128)S(1)}, f32[8,6]{1,0:T(8,128)}, u32[]{:S(2)}) copy-start(f32[8,6]{1,0:T(8,128)} %stiffness.1) | copy-start | bytes 580
  12.1 1.7 %collective-permute-start.4 = (f32[760,128]{1,0:T(8,128)S(1)}, f32[760,128]{1,0:T(8,128)S(1)}, u32[]{:S(2)}, u32[]{:S(2)}) collective-permute-start(f32[760,128]{1,0:T(8,128)S(1)} %get-tuple-element.40), channel_id=1, source_target_pairs={{0,8},{8,0},{16,24},{24,16},{32,40},{40,32},{48,56},{56,48},{64,72... | collective-permute-start | bytes 1167368 | tf_op jit(solution)/shard_map/ppermute | solution.py:524

commit v7 on v6

--- a/solution.py
+++ b/solution.py
@@ -173,7 +173,11 @@
     return [part[3 * c] + part[3 * c + 1] + part[3 * c + 2] for c in range(3)] + [part[9] + part[10]]
 
 
-def spread_own(cells, mult, dense):
+def spread_own(cells, mult, dense, at_depth):
+    depth = cells[...] % NZ
+    for j in range(SLOT_ROWS // 2):
+        hit = lax.broadcasted_iota(jnp.int32, (NZ, 256), 0) == paired(depth, j)
+        at_depth[:, pl.ds(256 * j, 256)] = jnp.where(hit, 1.0, 0.0).astype(BF16)
     values = spread(cells[...], [mult[c] for c in range(3)], 0, CX * CY)
     for i in range(4):
         dense[i] = values[i]
@@ -252,7 +256,7 @@
         f = f + (pltpu.roll(f, 1, 1) * self.not_first + pltpu.roll(f, NZ - 1, 1) * self.not_last)
         if edge is not None:
             f = f + self.ends * (0.5 * edge)
-        return f + f
+        return f
 
     def coefficients(self, planes):
         for p in planes:
@@ -270,9 +274,9 @@
             for e in range(6):
                 k = self.get(self.coeff, e, p)
                 around = self.summed(self.coeff, e, p, self.entry(0, e))
-                self.put(self.total, e, p, 64.0 * k + around)
+                self.put(self.total, e, p, 32.0 * k + around)
                 if e < 3:
-                    self.put(self.scale, e, p, DAMPING / (MASS_SHIFT + 6.0 * k + 0.125 * around))
+                    self.put(self.scale, e, p, DAMPING / (MASS_SHIFT + 6.0 * k + 0.25 * around))
 
     def push(self, flux, p, v):
         pushed = times([self.get(self.coeff, e, p) for e in range(6)], v)
@@ -286,7 +290,7 @@
         around = [self.summed(v_split, c, p) for c in range(3)]
         pushed = [self.summed(flux, c, p) for c in range(3)]
         mine, theirs = times(m, v), times(k, around)
-        return v, [MASS_SHIFT * v[c] + 0.125 * (mine[c] - theirs[c] - pushed[c]) for c in range(3)]
+        return v, [MASS_SHIFT * v[c] + 0.25 * (mine[c] - theirs[c] - pushed[c]) for c in range(3)]
 
     def sweep(self, planes, v_split, flux, to, to_flux, inside=None):
         for p in planes:
@@ -337,11 +341,11 @@
 
 
 def far_part(
-    far, corner, near, limit, ribbon,
+    far, corner, near, limit, ribbon, cells, mult, at_depth,
     near_fields, near_coeff, near_total, near_scale, near_flux,
     near_first, near_flux_first, near_second, near_flux_second, table, last,
-    smoothed, jumps, message,
-    fields, coeff, total, scale, flux, first, flux_first, second, flux_second, coarse,
+    message, second, updated,
+    fields, coeff, total, scale, flux, first, flux_first, flux_second, coarse,
 ):
     inside = is_inside()
     flip = odd("gx")
@@ -368,6 +372,28 @@
     grid.weights(range(1, HALO + 1))
     grid.sweep(range(1, HALO + 1), v0, flux0, v1, flux1, inside)
     grid.sweep(range(2, HALO + 2), v1, flux1, v2, flux2, inside)
+    used = slot_number().astype(F32) < limit[...] - 0.5
+    column = cells[...] // NZ
+    block = CX * CY
+    left = []
+    for c in range(3):
+        v = [grid.get(v2, c, HALO - 1 + i)[:CY] for i in range(CX + 2)]
+        jumps = [v[1 + g] - jnp.where(flip == 1, v[g], v[2 + g]) for g in range(CX)]
+        left.append(jnp.concatenate(pieces_of(jnp.concatenate(jumps, axis=0)), axis=1))
+    left = jnp.concatenate(left, axis=0)
+    for j in range(SLOT_ROWS // 2):
+        right = at_depth[:, pl.ds(256 * j, 256)]
+        picked = jnp.dot(left, jnp.concatenate([right] * 3, axis=0), preferred_element_type=F32)
+        at_column = lax.broadcasted_iota(jnp.int32, (block, 256), 0) == paired(column, j)
+        for c in range(3):
+            jump = jnp.sum(
+                jnp.where(at_column, picked[c * block : (c + 1) * block], 0.0), axis=0, keepdims=True
+            )
+            for i in range(2):
+                at = 2 * j + i
+                old = mult[c, at : at + 1, :]
+                new = old + PENALTY * jump[:, i * 128 : (i + 1) * 128]
+                updated[c, at : at + 1, :] = jnp.where(used[at : at + 1], new, old)
     remainders = [grid.remainder(HALO + g, v2, flux2) for g in range(CX - 1)]
     remainders.append([last[rows_of(c, CY), :] for c in range(3)])
 
@@ -385,70 +411,55 @@
         live.append((number > 0.5) & (number < top + 0.5))
     for c in range(3):
         planes = [grid.get(v2, c, HALO - 1 + i)[:CY] for i in range(CX + 2)]
-        for g in range(CX):
-            x = g + flip * (CX - 1 - 2 * g)
-            smoothed[rows_of(c * CX + x, CY), :] = planes[1 + g]
         pushed = []
         for i in range(CX + 1):
             jump = sign * (planes[i] - planes[i + 1])
-            jumps[c, rows_of(i, CY), :] = jump
             at = rows_of(i + flip, CY)
             pushed.append(jnp.where(live[i], ribbon[c, at, :] + PENALTY * jump, 0.0))
         parts = [remainders[g][c] - sign * (pushed[g + 1] - pushed[g]) for g in range(CX)]
         for half in range(2):
             coarse[rows_of(half * 3 + c, CY), :] = parts[2 * half] + parts[2 * half + 1]
 
-    out = jnp.zeros((3 * CY // 2, NZ), F32)
-    lane_in = lax.broadcasted_iota(jnp.int32, (NZ, NZ), 0)
-    lane_out = lax.broadcasted_iota(jnp.int32, (NZ, NZ), 1)
+    pairs = []
     for half in range(2):
         at = 3 * half * CY
         rows = coarse[pl.ds(at, 3 * CY // 2, stride=2), :] + coarse[pl.ds(at + 1, 3 * CY // 2, stride=2), :]
-        x = half + flip * (1 - 2 * half)
-        pick = jnp.where(lane_in // 2 + x * (NZ // 2) == lane_out, 1.0, 0.0).astype(BF16)
-        for piece in pieces_of(rows):
-            out = out + jnp.dot(piece, pick, preferred_element_type=F32)
+        pairs.append(rows)
+    low_x = jnp.where(flip == 1, pairs[1], pairs[0])
+    high_x = jnp.where(flip == 1, pairs[0], pairs[1])
+    even_lane = lax.rem(lax.broadcasted_iota(jnp.int32, (1, NZ), 1), 2) == 0
+    out = jnp.where(even_lane, low_x + pltpu.roll(low_x, NZ - 1, 1), high_x + pltpu.roll(high_x, 1, 1))
     for s in range(N_GY):
         message[s] = out
 
 
 def finish(
-    limit, cells, mult, jumps, smoothed, gathered,
+    updated, low, high, gathered,
     smoothed_out, updated_out, coarse_out,
-    updated, coarse, done,
+    coarse, turned, done,
 ):
-    copies = [
-        pltpu.make_async_copy(smoothed, smoothed_out, done.at[0]),
-        pltpu.make_async_copy(coarse, coarse_out, done.at[1]),
-        pltpu.make_async_copy(updated, updated_out, done.at[2]),
-    ]
-    copies[0].start()
+    flip = odd("gx")
+    split = Split(HALO + 2, low, high)
+    copies = [pltpu.make_async_copy(updated, updated_out, done.at[0])]
+    for c in range(3):
+        for g in range(CX):
+            x = g + flip * (CX - 1 - 2 * g)
+            ref, at = split.of(c, HALO + g)
+            copies.append(
+                pltpu.make_async_copy(
+                    ref.at[pl.ds(at.start, CY), :], smoothed_out.at[rows_of(c * CX + x, CY), :],
+                    done.at[1 + c * CX + g],
+                )
+            )
+    for copy in copies:
+        copy.start()
     for c in range(3):
         parts = [gathered[s, pl.ds(c * CY // 2, CY // 2), :] for s in range(N_GY)]
-        coarse[c] = jnp.transpose(jnp.concatenate(parts, axis=0))
-    copies[1].start()
-    live = slot_number().astype(F32) < limit[...] - 0.5
-    column, depth = cells[...] // NZ, cells[...] % NZ
-    block = CX * CY
-    start = pl.multiple_of((1 - odd("gx")) * CY, CY)
-    left = jnp.concatenate(
-        [jnp.concatenate(pieces_of(jumps[c, pl.ds(start, block), :]), axis=1) for c in range(3)], axis=0
-    )
-    for j in range(SLOT_ROWS // 2):
-        at_depth = lax.broadcasted_iota(jnp.int32, (NZ, 256), 0) == paired(depth, j)
-        right = jnp.where(at_depth, 1.0, 0.0).astype(BF16)
-        picked = jnp.dot(left, jnp.concatenate([right] * 3, axis=0), preferred_element_type=F32)
-        at_column = lax.broadcasted_iota(jnp.int32, (block, 256), 0) == paired(column, j)
-        for c in range(3):
-            jump = jnp.sum(
-                jnp.where(at_column, picked[c * block : (c + 1) * block], 0.0), axis=0, keepdims=True
-            )
-            for i in range(2):
-                at = 2 * j + i
-                old = mult[c, at : at + 1, :]
-                new = old + PENALTY * jump[:, i * 128 : (i + 1) * 128]
-                updated[c, at : at + 1, :] = jnp.where(live[at : at + 1], new, old)
-    copies[2].start()
+        turned[c] = jnp.transpose(jnp.concatenate(parts, axis=0))
+        for x in range(CX // 2):
+            coarse[c, pl.ds(x * NZ // 2, NZ // 2), :] = turned[c, pl.ds(x, NZ // 2, stride=2), :]
+        copies.append(pltpu.make_async_copy(coarse.at[c], coarse_out.at[c], done.at[1 + 3 * CX + c]))
+        copies[-1].start()
     for copy in copies:
         copy.wait()
 
@@ -511,7 +522,9 @@
     far = lax.ppermute(far, ("gx", "gy"), other_x())
     y_pair = lax.ppermute(y_pair, "gy", pair(N_GY))
     y_other = lax.ppermute(y_other, ("gx", "gy"), other_y())
-    (dense,) = call(spread_own, [f32(4, block, NZ)], [VMEM] * 2, flops=100000000000)(cells, mult)
+    dense, at_depth = call(
+        spread_own, [f32(4, block, NZ), jax.ShapeDtypeStruct((NZ, 8 * 128), BF16)], [VMEM] * 2, flops=10**11
+    )(cells, mult)
     corner, near, own, limit = call(
         pack_second,
         [
@@ -528,24 +541,24 @@
         near_part, arrays + [f32(LABELS * 6, NZ), f32(3 * CY, NZ)], [SMEM, VMEM, VMEM]
     )(stiffness, own, near)
     (ribbon,) = call(spread_before, [f32(4, (CX + 2) * CY, NZ)], [VMEM] * 4)(far, near, dense, half[-1])
-    smoothed, jumps, message = call(
+    message, low, updated = call(
         far_part,
-        [f32(3 * block, NZ), f32(3, (CX + 1) * CY, NZ), f32(N_GY, 3 * CY // 2, NZ)],
-        [VMEM] * (5 + len(half)),
-        scratch=[pltpu.VMEM(a.shape, F32) for a in arrays] + [pltpu.VMEM((6 * CY, NZ), F32)],
-    )(far, corner, near, limit, ribbon, *half)
+        [f32(N_GY, 3 * CY // 2, NZ), three, f32(3, SLOT_ROWS, 128)],
+        [VMEM] * (8 + len(half)),
+        scratch=[pltpu.VMEM(a.shape, F32) for a in arrays[:-1]] + [pltpu.VMEM((6 * CY, NZ), F32)],
+    )(far, corner, near, limit, ribbon, cells, mult, at_depth, *half)
     gathered = lax.all_to_all(message, "gy", 0, 0)
     smoothed, updated, coarse = call(
         finish,
         [pltpu.HBM(s, F32) for s in ((3 * block, NZ), (3, SLOT_ROWS, 128), (3, CX // 2 * NZ // 2, NY // 2))],
-        [VMEM] * 6,
+        [VMEM] * 4,
         out_specs=[HBM] * 3,
         scratch=[
-            pltpu.VMEM((3, SLOT_ROWS, 128), F32),
             pltpu.VMEM((3, CX // 2 * NZ // 2, NY // 2), F32),
-            pltpu.SemaphoreType.DMA((3,)),
+            pltpu.VMEM((3, NZ, NY // 2), F32),
+            pltpu.SemaphoreType.DMA((4 + 3 * CX,)),
         ],
-    )(limit, cells, mult, jumps, smoothed, gathered)
+    )(updated, low, half[7], gathered)
     coarse = jnp.swapaxes(coarse.reshape(3, CX // 2, NZ // 2, NY // 2), 2, 3)
     return (smoothed.reshape(3, CX, CY, NZ), coarse, updated.reshape(3, 1, 1, SLOTS))
 

time: 33.5 us -> 33.4 us (level)
  no operation moved by 1% of the time
where the time goes in v7:
time: 33.4 us; the launch traced here: 32.8 us
  blocking collectives  9.51 us (28%)
  starting transfers between devices  8.82 us (26%)
  Pallas kernels  8.27 us (25%)
  waiting for transfers between devices  4.9 us (15%)
  between operations  1.35 us (4%)
    all_to_all x1, blocking collectives, body(): gathered = lax.all_to_all(message, 'gy', 0, 0)  9.51 us
    ppermute x1, starting transfers between devices, body(): corner = lax.ppermute(corner, ('gx', 'gy'), other_x())  4.77 us
    ppermute x1, waiting for transfers between devices, body(): far = lax.ppermute(far, ('gx', 'gy'), other_x())  3.31 us
    ppermute x1, starting transfers between devices, body(): y_pair = lax.ppermute(y_pair, 'gy', pair(N_GY))  3.14 us
    pallas_call x1, Pallas kernels, body(): call(near_part, arrays + [f32(LABELS * 6, NZ), f32(3 * CY, NZ)], [SMEM, V...  2.63 us
    pallas_call x1, Pallas kernels, body(): call(far_part, [f32(N_GY, 3 * CY // 2, NZ), three, f32(3, SLOT_ROWS, 128)...  1.96 us
    pallas_call x1, Pallas kernels, body(): call(pack_first, [f32(HALO, OWN, NZ), f32(HALO, OWN, NZ), f32(OWN * CY, N...  1.3 us
    pallas_call x1, Pallas kernels, body(): call(spread_own, [f32(4, block, NZ), jax.ShapeDtypeStruct((NZ, 8 * 128),...  0.95 us
  transfers between devices with their start and end apart: 5, of which 4 were waited for; matrix products, arithmetic and copies ran while one was open for 0% of the time, Pallas kernels for 12%

profile of v7, /device:TPU:128, one launch (start us, length us, event | category | flops | bytes accessed | tf_op | source)
XLA Modules:
  0.0 32.8 jit_solution(15006486563403751120)
XLA Ops:
  0.6 1.3 %shard_map.94 = (f32[3,28,128]{2,1,0:T(8,128)S(1)}, f32[3,28,128]{2,1,0:T(8,128)S(1)}, f32[896,128]{1,0:T(8,128)S(1)}, s32[8,128]{1,0:T(8,128)S(1)}, f32[3,8,128]{2,1,0:T(8,128)S(1)}) custom-call(f32[384,128]{1,0:T(8,128)} %bitcast.10, f32[384,128]{1,0:T(8,128)} %bitcast.11, s32[128,128]{1,0:T(8,128)} %bitcast.12, s32[8,128]{1,0:T(8,128)} %bitcast.14, ...), custom_call_target="tpu_custom_call" | custom-call | flops 1000 | bytes 1000 | tf_op jit(solution)/shard_map/pallas_call | solution.py:509
  1.9 0.1 collective-permute-start.1
  2.0 3.1 %collective-permute-start.2 = (f32[3,28,128]{2,1,0:T(8,128)S(1)}, f32[3,28,128]{2,1,0:T(8,128)S(1)}, u32[]{:S(2)}, u32[]{:S(2)}) collective-permute-start(f32[3,28,128]{2,1,0:T(8,128)S(1)} %get-tuple-element.38), channel_id=1, source_target_pairs={{0,1},{1,0},{2,3},{3,2},{4,5},{5,4},{6,7},{7,6},{8,9},{9,8},{10,11... | collective-permute-start | bytes 129032 | tf_op jit(solution)/shard_map/ppermute | solution.py:523
  5.2 0.8 %collective-permute-start = (f32[608,128]{1,0:T(8,128)S(1)}, f32[608,128]{1,0:T(8,128)S(1)}, u32[]{:S(2)}, u32[]{:S(2)}) collective-permute-start(f32[608,128]{1,0:T(8,128)S(1)} %get-tuple-element.36), channel_id=1, source_target_pairs={{0,1},{1,0},{2,3},{3,2},{4,5},{5,4},{6,7},{7,6},{8,16},{9,17},{10,... | collective-permute-start | bytes 933896 | tf_op jit(solution)/shard_map/ppermute | solution.py:522
  6.7 0.0 collective-permute-done.1.y_other
  6.7 0.6 %collective-permute-done.2.y_pair = f32[3,28,128]{2,1,0:T(8,128)S(1)} collective-permute-done((f32[3,28,128]{2,1,0:T(8,128)S(1)}, f32[3,28,128]{2,1,0:T(8,128)S(1)}, u32[]{:S(2)}, u32[]{:S(2)}) %collective-permute-start.2) | collective-permute-done | bytes 43040 | tf_op jit(solution)/shard_map/ppermute | solution.py:523
  7.3 0.1 shard_map.96
  7.3 4.8 %collective-permute-start.3 = (f32[120,128]{1,0:T(8,128)S(1)}, f32[120,128]{1,0:T(8,128)S(1)}, u32[]{:S(2)}, u32[]{:S(2)}) collective-permute-start(f32[120,128]{1,0:T(8,128)S(1)} %get-tuple-element.40), channel_id=1, source_target_pairs={{0,1},{1,0},{2,3},{3,2},{4,5},{5,4},{6,7},{7,6},{8,16},{9,17},{10,... | collective-permute-start | bytes 184328 | tf_op jit(solution)/shard_map/ppermute | solution.py:536
  12.1 0.0 copy-start
  12.1 0.0 collective-permute-start.4
  12.1 1.0 %shard_map.97 = (f32[4,128,128]{2,1,0:T(8,128)S(1)}, bf16[128,1024]{1,0:T(8,128)(2,1)S(1)}) custom-call(s32[8,128]{1,0:T(8,128)S(1)} %get-tuple-element.39.cells, f32[3,8,128]{2,1,0:T(8,128)S(1)} %get-tuple-element.35.mult), custom_call_target="tpu_custom_call" | custom-call | flops 99999997952 | bytes 1000 | tf_op jit(solution)/shard_map/pallas_call | solution.py:525
  13.1 0.8 %collective-permute-done.4.near = f32[760,128]{1,0:T(8,128)S(1)} collective-permute-done((f32[760,128]{1,0:T(8,128)S(1)}, f32[760,128]{1,0:T(8,128)S(1)}, u32[]{:S(2)}, u32[]{:S(2)}) %collective-permute-start.4) | collective-permute-done | bytes 389152 | tf_op jit(solution)/shard_map/ppermute | solution.py:537
  13.8 0.0 copy-done
  13.8 2.6 %shard_map.98 = (f32[2560,128]{1,0:T(8,128)S(1)}, f32[2400,128]{1,0:T(8,128)S(1)}, f32[2400,128]{1,0:T(8,128)S(1)}, f32[1200,128]{1,0:T(8,128)S(1)}, f32[1200,12...) custom-call(f32[8,6]{1,0:T(8,128)S(1)} %copy-done, ...), custom_call_target="tpu_custom_call" | custom-call | flops 1000 | bytes 1000 | tf_op jit(solution)/shard_map/pallas_call | solution.py:540
  16.5 3.3 %collective-permute-done.far = f32[608,128]{1,0:T(8,128)S(1)} collective-permute-done((f32[608,128]{1,0:T(8,128)S(1)}, f32[608,128]{1,0:T(8,128)S(1)}, u32[]{:S(2)}, u32[]{:S(2)}) %collective-permute-start) | collective-permute-done | bytes 311328 | tf_op jit(solution)/shard_map/ppermute | solution.py:522
  19.8 0.4 %shard_map.99.ribbon = f32[4,192,128]{2,1,0:T(8,128)S(1)} custom-call(f32[608,128]{1,0:T(8,128)S(1)} %collective-permute-done.far, f32[760,128]{1,0:T(8,128)S(1)} %collective-permute-done.4.near, f32[4,128,128]{2,1,0:T(8,128)S(1)} %get-tuple-element.43.dense, f32[96,128]{1,0:T(8,128)S(1)} %get-tuple-element.45.last), custom_call_target="tpu_custom_call" | custom-call | flops 1000 | bytes 1000 | tf_op jit(solution)/shard_map/pallas_call | solution.py:543
  20.2 0.3 collective-permute-done.3.corner
  20.4 2.0 %shard_map.100 = (f32[8,48,128]{2,1,0:T(8,128)S(1)}, f32[1200,128]{1,0:T(8,128)S(1)}, f32[3,8,128]{2,1,0:T(8,128)S(1)}) custom-call(f32[608,128]{1,0:T(8,128)S(1)} %collective-permute-done.far, f32[120,128]{1,0:T(8,128)S(1)} %collective-permute-done.3.corner, f32[760,128]{1,0:T(8,128)S(1)} %collective-permute-done.4.near, ...), custom_call_target="tpu_custom_call" | custom-call | flops 1000 | bytes 1000 | tf_op jit(solution)/shard_map/pallas_call | solution.py:544
  22.4 9.5 %all_to_all.5.gathered = f32[8,48,128]{2,1,0:T(8,128)S(1)} all-to-all(f32[8,48,128]{2,1,0:T(8,128)S(1)} %get-tuple-element.59), channel_id=1, replica_groups=mesh['gx'=32,'gy'=8] {'gy'}, dimensions={0} | all-to-all | bytes 393216 | tf_op jit(solution)/shard_map/all_to_all | solution.py:550
  31.9 0.9 %shard_map.101 = (f32[384,128]{1,0:T(8,128)}, f32[3,8,128]{2,1,0:T(8,128)}, f32[3,128,128]{2,1,0:T(8,128)}) custom-call(f32[3,8,128]{2,1,0:T(8,128)S(1)} %get-tuple-element.57.updated, f32[1200,128]{1,0:T(8,128)S(1)} %get-tuple-element.58.low, f32[1200,128]{1,0:T(8,128)S(1)} %get-tuple-element.54.near_second.high, f32[8,48,128]{2,1,0:T(8,128)S(1)} %all_to_all.5.gathered), custom_call_target="tpu_custom_call" | custom-call | flops 1000 | bytes 1000 | tf_op jit(solution)/shard_map/pallas_call | solution.py:551
  (1 shorter events, 0.0 us)
Async XLA Ops:
  1.9 4.7 %collective-permute-start.1 = (f32[3,28,128]{2,1,0:T(8,128)S(1)}, f32[3,28,128]{2,1,0:T(8,128)S(1)}, u32[]{:S(2)}, u32[]{:S(2)}) collective-permute-start(f32[3,28,128]{2,1,0:T(8,128)S(1)} %get-tuple-element.37), channel_id=1, source_target_pairs={{0,8},{1,2},{2,1},{3,4},{4,3},{5,6},{6,5},{7,15},{8,0},{9,10},{10,... | collective-permute-start | bytes 129032 | tf_op jit(solution)/shard_map/ppermute | solution.py:524
  2.0 5.2 %collective-permute-start.2 = (f32[3,28,128]{2,1,0:T(8,128)S(1)}, f32[3,28,128]{2,1,0:T(8,128)S(1)}, u32[]{:S(2)}, u32[]{:S(2)}) collective-permute-start(f32[3,28,128]{2,1,0:T(8,128)S(1)} %get-tuple-element.38), channel_id=1, source_target_pairs={{0,1},{1,0},{2,3},{3,2},{4,5},{5,4},{6,7},{7,6},{8,9},{9,8},{10,11... | collective-permute-start | bytes 129032 | tf_op jit(solution)/shard_map/ppermute | solution.py:523
  5.2 14.6 %collective-permute-start = (f32[608,128]{1,0:T(8,128)S(1)}, f32[608,128]{1,0:T(8,128)S(1)}, u32[]{:S(2)}, u32[]{:S(2)}) collective-permute-start(f32[608,128]{1,0:T(8,128)S(1)} %get-tuple-element.36), channel_id=1, source_target_pairs={{0,1},{1,0},{2,3},{3,2},{4,5},{5,4},{6,7},{7,6},{8,16},{9,17},{10,... | collective-permute-start | bytes 933896 | tf_op jit(solution)/shard_map/ppermute | solution.py:522
  7.3 13.1 %collective-permute-start.3 = (f32[120,128]{1,0:T(8,128)S(1)}, f32[120,128]{1,0:T(8,128)S(1)}, u32[]{:S(2)}, u32[]{:S(2)}) collective-permute-start(f32[120,128]{1,0:T(8,128)S(1)} %get-tuple-element.40), channel_id=1, source_target_pairs={{0,1},{1,0},{2,3},{3,2},{4,5},{5,4},{6,7},{7,6},{8,16},{9,17},{10,... | collective-permute-start | bytes 184328 | tf_op jit(solution)/shard_map/ppermute | solution.py:536
  12.1 1.7 %copy-start = (f32[8,6]{1,0:T(8,128)S(1)}, f32[8,6]{1,0:T(8,128)}, u32[]{:S(2)}) copy-start(f32[8,6]{1,0:T(8,128)} %stiffness.1) | copy-start | bytes 580
  12.1 1.7 %collective-permute-start.4 = (f32[760,128]{1,0:T(8,128)S(1)}, f32[760,128]{1,0:T(8,128)S(1)}, u32[]{:S(2)}, u32[]{:S(2)}) collective-permute-start(f32[760,128]{1,0:T(8,128)S(1)} %get-tuple-element.41), channel_id=1, source_target_pairs={{0,8},{8,0},{16,24},{24,16},{32,40},{40,32},{48,56},{56,48},{64,72... | collective-permute-start | bytes 1167368 | tf_op jit(solution)/shard_map/ppermute | solution.py:537

commit v8 on v7

--- a/solution.py
+++ b/solution.py
@@ -26,8 +26,8 @@
 OWN = OWN_RHS0 + 3 * CX
 SIDE = 3 * HALO + HALO + 3 * (HALO - 1)
 SLOT_ROWS = SLOTS // 128
-CORNER = 112
 IFACE = 4 * SLOT_ROWS
+CORNER = 2 * (4 * HALO * HALO + 3 * (HALO - 1) ** 2)
 VMEM = pl.BlockSpec(memory_space=pltpu.VMEM)
 SMEM = pl.BlockSpec(memory_space=pltpu.SMEM)
 HBM = pl.BlockSpec(memory_space=pltpu.HBM)
@@ -54,6 +54,14 @@
 
 def rows_of(j, height):
     return pl.ds(j * height if isinstance(j, int) else pl.multiple_of(j * height, height), height)
+
+
+def corner_rows():
+    at = 0
+    for place in range(SIDE):
+        depth = HALO if place < 4 * HALO else HALO - 1
+        yield place, at, depth
+        at += 2 * depth
 
 
 def sent_planes():
@@ -84,7 +92,7 @@
 
 def pack_first(
     disp, rhs, labels, cells_in, mult_in,
-    y_other, y_pair, own, cells, mult,
+    y_other, own, cells, mult,
     raw_labels, arrived,
 ):
     flip = odd("gx")
@@ -106,47 +114,62 @@
     for k in range(HALO):
         first = own[pl.ds(k, OWN, stride=CY), :]
         last = own[pl.ds(CY - HALO + k, OWN, stride=CY), :]
-        y_pair[k] = jnp.where(up, last, first)
         y_other[k] = jnp.where(up, first, last)
 
 
-def pack_far(own, raw_cells, mult, far, cells):
+def pack_sides(own, raw_cells, mult, far, near, cells):
     flip = odd("gx")
     block_plane = raw_cells[...] // (CY * NZ)
     turned = raw_cells[...] + flip * (CX - 1 - 2 * block_plane) * (CY * NZ)
     cells[...] = turned
     for place, first, k in sent_planes():
         far[rows_of(place, CY), :] = own[rows_of(first + k, CY), :]
-    far[pl.ds(SIDE * CY, SLOT_ROWS), :] = turned.astype(F32)
-    for c in range(3):
-        far[pl.ds(SIDE * CY + (1 + c) * SLOT_ROWS, SLOT_ROWS), :] = mult[c]
-
-
-def pack_second(y_other, y_pair, count, own, cells, mult, corner, near, wide, limit):
+        near[rows_of(place, CY), :] = own[rows_of(first + CX - 1 - k, CY), :]
+    for side in (far, near):
+        side[pl.ds(SIDE * CY, SLOT_ROWS), :] = turned.astype(F32)
+        for c in range(3):
+            side[pl.ds(SIDE * CY + (1 + c) * SLOT_ROWS, SLOT_ROWS), :] = mult[c]
+
+
+def pack_pair(own, near, y_pair):
+    up = odd("gy") == 0
+    for k in range(HALO):
+        first = own[pl.ds(k, OWN, stride=CY), :]
+        last = own[pl.ds(CY - HALO + k, OWN, stride=CY), :]
+        y_pair[k] = jnp.where(up, last, first)
+
+
+def reach():
     here = lax.axis_index("gy")
-    up = odd("gy") == 0
-    low = jnp.where(here > 0, 1.0, 0.0).astype(F32)
-    high = jnp.where(here < N_GY - 1, 1.0, 0.0).astype(F32)
+    return (
+        jnp.where(here > 0, 1.0, 0.0).astype(F32),
+        jnp.where(here < N_GY - 1, 1.0, 0.0).astype(F32),
+    )
+
+
+def pack_wide(own, wide):
     for j in range(OWN):
         wide[pl.ds(j * ROWS, CY), :] = own[rows_of(j, CY), :]
+        wide[pl.ds(j * ROWS + CY, ROWS - CY), :] = jnp.zeros((ROWS - CY, NZ), F32)
+
+
+def pack_second(y_other, y_pair, count, inner, corner_far, corner_near, wide, limit):
+    low, high = reach()
+    up = odd("gy") == 0
+    wide[...] = inner[...]
     for k in range(HALO):
-        after = jnp.where(up, y_pair[k], y_other[k])
-        before = jnp.where(up, y_other[k], y_pair[k])
-        wide[pl.ds(CY + k, OWN, stride=ROWS), :] = high * after
-        wide[pl.ds(ROWS - HALO + k, OWN, stride=ROWS), :] = low * before
-    for k in range(CY + HALO, ROWS - HALO):
-        wide[pl.ds(k, OWN, stride=ROWS), :] = jnp.zeros((OWN, NZ), F32)
-    for place, first, k in sent_planes():
-        for i, y in enumerate((CY, ROWS - HALO)):
-            corner[pl.ds(place * 2 * HALO + i * HALO, HALO), :] = wide[pl.ds((first + k) * ROWS + y, HALO), :]
-        near[rows_of(place, ROWS), :] = wide[rows_of(first + CX - 1 - k, ROWS), :]
+        wide[pl.ds(CY + k, OWN, stride=ROWS), :] = high * jnp.where(up, y_pair[k], y_other[k])
+        wide[pl.ds(ROWS - HALO + k, OWN, stride=ROWS), :] = low * jnp.where(up, y_other[k], y_pair[k])
     live = jnp.full((SLOT_ROWS, 128), count[0, 0].astype(F32), F32)
     limit[...] = live
-    corner[pl.ds(CORNER, SLOT_ROWS), :] = live
-    near[pl.ds(SIDE * ROWS + IFACE, SLOT_ROWS), :] = live
-    near[pl.ds(SIDE * ROWS, SLOT_ROWS), :] = cells[...].astype(F32)
-    for c in range(3):
-        near[pl.ds(SIDE * ROWS + (1 + c) * SLOT_ROWS, SLOT_ROWS), :] = mult[c]
+    planes = list(sent_planes())
+    for corner, turn in ((corner_far, False), (corner_near, True)):
+        for place, at, depth in corner_rows():
+            first, k = planes[place][1:]
+            base = (first + (CX - 1 - k if turn else k)) * ROWS
+            corner[pl.ds(at, depth), :] = wide[pl.ds(base + CY, depth), :]
+            corner[pl.ds(at + depth, depth), :] = wide[pl.ds(base + ROWS - depth, depth), :]
+        corner[pl.ds(CORNER, SLOT_ROWS), :] = live
 
 
 def paired(array, j):
@@ -193,7 +216,7 @@
 
     def at(i):
         a = far[pl.ds(SIDE * CY + i * SLOT_ROWS, SLOT_ROWS), :]
-        b = near[pl.ds(SIDE * ROWS + i * SLOT_ROWS, SLOT_ROWS), :]
+        b = near[pl.ds(SIDE * CY + i * SLOT_ROWS, SLOT_ROWS), :]
         return jnp.where(flip == 1, b, a)
 
     values = spread(at(0).astype(jnp.int32), [at(1 + c) for c in range(3)], flip * (CX - 1) * CY, CY)
@@ -309,8 +332,19 @@
         return [(self.right_side(c, p) - a[c])[:CY] for c in range(3)]
 
 
+def fill_halo(fields, side, corner, plane_of, inside):
+    tiles = {place: (at, depth) for place, at, depth in corner_rows()}
+    for place, base, k in halo_planes():
+        plane = (base + plane_of(k)) * ROWS
+        at, depth = tiles[place]
+        fields[pl.ds(plane, CY), :] = inside * side[rows_of(place, CY), :]
+        fields[pl.ds(plane + CY, ROWS - CY), :] = jnp.zeros((ROWS - CY, NZ), F32)
+        fields[pl.ds(plane + CY, depth), :] = inside * corner[pl.ds(at, depth), :]
+        fields[pl.ds(plane + ROWS - depth, depth), :] = inside * corner[pl.ds(at + depth, depth), :]
+
+
 def near_part(
-    stiffness, own, near,
+    stiffness, own, near, corner_near,
     fields, coeff, total, scale, flux, first, flux_first, second, flux_second, table, last,
 ):
     for c in range(3):
@@ -319,8 +353,7 @@
             fields[rows_of(RHS0 - 1 + c * PR + HALO + g, ROWS), :] = own[rows_of(OWN_RHS0 + c * CX + g, ROWS), :]
     for g in range(CX):
         fields[rows_of(LAB0 + HALO + g, ROWS), :] = own[rows_of(OWN_LAB0 + g, ROWS), :]
-    for place, at, k in halo_planes():
-        fields[rows_of(at + HALO + CX + k, ROWS), :] = near[rows_of(place, ROWS), :]
+    fill_halo(fields, near, corner_near, lambda k: HALO + CX + k, 1.0)
     for m in range(LABELS):
         for e in range(6):
             table[pl.ds(m * 6 + e, 1), :] = jnp.full((1, NZ), stiffness[m, e], F32)
@@ -341,7 +374,7 @@
 
 
 def far_part(
-    far, corner, near, limit, ribbon, cells, mult, at_depth,
+    far, corner, corner_near, limit, ribbon, cells, mult, at_depth,
     near_fields, near_coeff, near_total, near_scale, near_flux,
     near_first, near_flux_first, near_second, near_flux_second, table, last,
     message, second, updated,
@@ -350,13 +383,7 @@
     inside = is_inside()
     flip = odd("gx")
     sign = jnp.where(flip == 1, -1.0, 1.0).astype(F32)
-    for y in range(CY + HALO, ROWS - HALO):
-        fields[pl.ds(y, FIELDS, stride=ROWS), :] = jnp.zeros((FIELDS, NZ), F32)
-    for place, at, k in halo_planes():
-        plane = (at + HALO - 1 - k) * ROWS
-        fields[pl.ds(plane, CY), :] = inside * far[rows_of(place, CY), :]
-        for i, y in enumerate((CY, ROWS - HALO)):
-            fields[pl.ds(plane + y, HALO), :] = inside * corner[pl.ds(place * 2 * HALO + i * HALO, HALO), :]
+    fill_halo(fields, far, corner, lambda k: HALO - 1 - k, inside)
     v0, flux0 = Split(HALO, fields, near_fields), Split(HALO, flux, near_flux)
     v1, flux1 = Split(HALO + 1, first, near_first), Split(HALO + 1, flux_first, near_flux_first)
     v2, flux2 = Split(HALO + 2, second, near_second), Split(HALO + 2, flux_second, near_flux_second)
@@ -398,7 +425,7 @@
     remainders.append([last[rows_of(c, CY), :] for c in range(3)])
 
     mine = limit[:1]
-    theirs = jnp.where(flip == 1, near[pl.ds(SIDE * ROWS + IFACE, 1), :], corner[pl.ds(CORNER, 1), :])
+    theirs = jnp.where(flip == 1, corner_near[pl.ds(CORNER, 1), :], corner[pl.ds(CORNER, 1), :])
     live = []
     for i in range(CX + 1):
         if i == 0:
@@ -506,9 +533,9 @@
     block = CX * CY
     copies = 2 + 7 * CX
     slots = jax.ShapeDtypeStruct((SLOT_ROWS, 128), jnp.int32)
-    y_other, y_pair, own, raw_cells, mult = call(
+    y_other, own, raw_cells, mult = call(
         pack_first,
-        [f32(HALO, OWN, NZ), f32(HALO, OWN, NZ), f32(OWN * CY, NZ), slots, f32(3, SLOT_ROWS, 128)],
+        [f32(HALO, OWN, NZ), f32(OWN * CY, NZ), slots, f32(3, SLOT_ROWS, 128)],
         [HBM] * 5,
         scratch=[pltpu.VMEM((block, NZ), jnp.int32), pltpu.SemaphoreType.DMA((copies,))],
     )(
@@ -518,35 +545,35 @@
         in_hbm(rows.reshape(SLOT_ROWS, 128)),
         in_hbm(multipliers.reshape(3, SLOT_ROWS, 128)),
     )
-    far, cells = call(pack_far, [f32(SIDE * CY + IFACE, NZ), slots], [VMEM] * 3)(own, raw_cells, mult)
+    y_other = lax.ppermute(y_other, ("gx", "gy"), other_y())
+    side = f32(SIDE * CY + IFACE, NZ)
+    far, near, cells = call(pack_sides, [side, side, slots], [VMEM] * 3)(own, raw_cells, mult)
+    near = lax.ppermute(near, "gx", pair(N_GX))
     far = lax.ppermute(far, ("gx", "gy"), other_x())
+    (y_pair,) = call(pack_pair, [f32(HALO, OWN, NZ)], [VMEM] * 2)(own, near)
     y_pair = lax.ppermute(y_pair, "gy", pair(N_GY))
-    y_other = lax.ppermute(y_other, ("gx", "gy"), other_y())
     dense, at_depth = call(
-        spread_own, [f32(4, block, NZ), jax.ShapeDtypeStruct((NZ, 8 * 128), BF16)], [VMEM] * 2, flops=10**11
+        spread_own, [f32(4, block, NZ), jax.ShapeDtypeStruct((NZ, 8 * 128), BF16)], [VMEM] * 2, flops=5 * 10**9
     )(cells, mult)
-    corner, near, own, limit = call(
-        pack_second,
-        [
-            f32(CORNER + SLOT_ROWS, NZ), f32(SIDE * ROWS + IFACE + SLOT_ROWS, NZ), f32(OWN * ROWS, NZ),
-            f32(SLOT_ROWS, NZ),
-        ],
-        [VMEM, VMEM, SMEM, VMEM, VMEM, VMEM],
-    )(y_other, y_pair, counts, own, cells, mult)
+    (inner,) = call(pack_wide, [f32(OWN * ROWS, NZ)], [VMEM], flops=5 * 10**9)(own)
+    tile = f32(CORNER + SLOT_ROWS, NZ)
+    corner, corner_near, own, limit = call(
+        pack_second, [tile, tile, f32(OWN * ROWS, NZ), f32(SLOT_ROWS, NZ)], [VMEM, VMEM, SMEM, VMEM]
+    )(y_other, y_pair, counts, inner)
     corner = lax.ppermute(corner, ("gx", "gy"), other_x())
-    near = lax.ppermute(near, "gx", pair(N_GX))
+    corner_near = lax.ppermute(corner_near, "gx", pair(N_GX))
     three, six = f32(3 * PX * ROWS, NZ), f32(6 * PX * ROWS, NZ)
     arrays = [f32(FIELDS * ROWS, NZ), six, six] + [three] * 6
     half = call(
-        near_part, arrays + [f32(LABELS * 6, NZ), f32(3 * CY, NZ)], [SMEM, VMEM, VMEM]
-    )(stiffness, own, near)
+        near_part, arrays + [f32(LABELS * 6, NZ), f32(3 * CY, NZ)], [SMEM, VMEM, VMEM, VMEM]
+    )(stiffness, own, near, corner_near)
     (ribbon,) = call(spread_before, [f32(4, (CX + 2) * CY, NZ)], [VMEM] * 4)(far, near, dense, half[-1])
     message, low, updated = call(
         far_part,
         [f32(N_GY, 3 * CY // 2, NZ), three, f32(3, SLOT_ROWS, 128)],
         [VMEM] * (8 + len(half)),
         scratch=[pltpu.VMEM(a.shape, F32) for a in arrays[:-1]] + [pltpu.VMEM((6 * CY, NZ), F32)],
-    )(far, corner, near, limit, ribbon, cells, mult, at_depth, *half)
+    )(far, corner, corner_near, limit, ribbon, cells, mult, at_depth, *half)
     gathered = lax.all_to_all(message, "gy", 0, 0)
     smoothed, updated, coarse = call(
         finish,

time: 33.4 us -> 33.4 us (level)
  blocking collectives: 9.51 us -> 12.6 us
  waiting for transfers between devices: 4.9 us -> 1.96 us
    ppermute x1, waiting for transfers between devices: 3.31 us -> 0.12 us  [body(): far = lax.ppermute(far, ('gx', 'gy'), other_x())]
    all_to_all x1, blocking collectives: 9.51 us -> 12.6 us  [body(): gathered = lax.all_to_all(message, 'gy', 0, 0)]
    ppermute x1, starting transfers between devices: 4.77 us -> 3.88 us  [body(): corner = lax.ppermute(corner, ('gx', 'gy'), other_x())]
    ppermute x1, waiting for transfers between devices: 0.56 us -> 1.37 us  [body(): y_pair = lax.ppermute(y_pair, 'gy', pair(N_GY))]
    ppermute x1, waiting for transfers between devices: 0.75 us -> 0.01 us  [body(): near = lax.ppermute(near, 'gx', pair(N_GX))]
    ppermute x1, starting transfers between devices: 0.81 us -> 1.55 us  [body(): far = lax.ppermute(far, ('gx', 'gy'), other_x())]
    ppermute x1, starting transfers between devices: 0.09 us -> 0.5 us  [body(): y_other = lax.ppermute(y_other, ('gx', 'gy'), other_y())]
    pallas_call x3 -> x5, Pallas kernels: 1.41 us -> 1.51 us  [the longest x1 1.3 us: body(): call(pack_first, [f32(HALO, OWN, NZ), f32(OWN * CY, NZ), slots, f32(3, SL...]
  transfers between devices with their start and end apart: 5 -> 6, of which waited for: 4 -> 4; matrix products, arithmetic and copies ran while one was open for 0% -> 0% of each run, Pallas kernels for 12% -> 12%
where the time goes in v8:
time: 33.4 us; the launch traced here: 33.1 us
  blocking collectives  12.6 us (38%)
  starting transfers between devices  8.9 us (27%)
  Pallas kernels  8.3 us (25%)
  waiting for transfers between devices  1.96 us (6%)
  between operations  1.36 us (4%)
    all_to_all x1, blocking collectives, body(): gathered = lax.all_to_all(message, 'gy', 0, 0)  12.6 us
    ppermute x1, starting transfers between devices, body(): corner = lax.ppermute(corner, ('gx', 'gy'), other_x())  3.88 us
    ppermute x1, starting transfers between devices, body(): y_pair = lax.ppermute(y_pair, 'gy', pair(N_GY))  2.88 us
    pallas_call x1, Pallas kernels, body(): call(near_part, arrays + [f32(LABELS * 6, NZ), f32(3 * CY, NZ)], [SMEM, V...  2.61 us
    pallas_call x1, Pallas kernels, body(): call(far_part, [f32(N_GY, 3 * CY // 2, NZ), three, f32(3, SLOT_ROWS, 128)...  1.92 us
    ppermute x1, starting transfers between devices, body(): far = lax.ppermute(far, ('gx', 'gy'), other_x())  1.55 us
    ppermute x1, waiting for transfers between devices, body(): y_pair = lax.ppermute(y_pair, 'gy', pair(N_GY))  1.37 us
    pallas_call x1, Pallas kernels, body(): call(pack_first, [f32(HALO, OWN, NZ), f32(OWN * CY, NZ), slots, f32(3, SL...  1.3 us
  transfers between devices with their start and end apart: 6, of which 4 were waited for; matrix products, arithmetic and copies ran while one was open for 0% of the time, Pallas kernels for 12%

profile of v8, /device:TPU:128, one launch (start us, length us, event | category | flops | bytes accessed | tf_op | source)
XLA Modules:
  0.0 33.1 jit_solution(17524641292559582908)
XLA Ops:
  0.6 1.3 %shard_map.94 = (f32[3,28,128]{2,1,0:T(8,128)S(1)}, f32[896,128]{1,0:T(8,128)S(1)}, s32[8,128]{1,0:T(8,128)S(1)}, f32[3,8,128]{2,1,0:T(8,128)S(1)}) custom-call(f32[384,128]{1,0:T(8,128)} %bitcast.10, f32[384,128]{1,0:T(8,128)} %bitcast.11, s32[128,128]{1,0:T(8,128)} %bitcast.12, s32[8,128]{1,0:T(8,128)} %bitcast.14, f32[3,8,128]{2,1,0:T(8,128)} %bitcast.13), custom_call_target="tpu_custom_call" | custom-call | flops 1000 | bytes 1000 | tf_op jit(solution)/shard_map/pallas_call | solution.py:536
  2.0 0.1 collective-permute-start.2
  2.1 0.5 %collective-permute-start.1 = (f32[3,28,128]{2,1,0:T(8,128)S(1)}, f32[3,28,128]{2,1,0:T(8,128)S(1)}, u32[]{:S(2)}, u32[]{:S(2)}) collective-permute-start(f32[3,28,128]{2,1,0:T(8,128)S(1)} %get-tuple-element.37), channel_id=1, source_target_pairs={{0,8},{1,2},{2,1},{3,4},{4,3},{5,6},{6,5},{7,15},{8,0},{9,10},{10,... | collective-permute-start | bytes 129032 | tf_op jit(solution)/shard_map/ppermute | solution.py:548
  2.6 1.6 %collective-permute-start = (f32[608,128]{1,0:T(8,128)S(1)}, f32[608,128]{1,0:T(8,128)S(1)}, u32[]{:S(2)}, u32[]{:S(2)}) collective-permute-start(f32[608,128]{1,0:T(8,128)S(1)} %get-tuple-element.36), channel_id=1, source_target_pairs={{0,1},{1,0},{2,3},{3,2},{4,5},{5,4},{6,7},{7,6},{8,16},{9,17},{10,... | collective-permute-start | bytes 933896 | tf_op jit(solution)/shard_map/ppermute | solution.py:552
  4.1 0.0 collective-permute-done.2.near
  4.1 0.1 shard_map.96
  4.2 2.9 %collective-permute-start.3 = (f32[3,28,128]{2,1,0:T(8,128)S(1)}, f32[3,28,128]{2,1,0:T(8,128)S(1)}, u32[]{:S(2)}, u32[]{:S(2)}) collective-permute-start(f32[3,28,128]{2,1,0:T(8,128)S(1)} %shard_map.96), channel_id=1, source_target_pairs={{0,1},{1,0},{2,3},{3,2},{4,5},{5,4},{6,7},{7,6},{8,9},{9,8},{10,11... | collective-permute-start | bytes 129032 | tf_op jit(solution)/shard_map/ppermute | solution.py:554
  7.8 0.0 collective-permute-done.1.y_other
  7.8 1.4 %collective-permute-done.3.y_pair = f32[3,28,128]{2,1,0:T(8,128)S(1)} collective-permute-done((f32[3,28,128]{2,1,0:T(8,128)S(1)}, f32[3,28,128]{2,1,0:T(8,128)S(1)}, u32[]{:S(2)}, u32[]{:S(2)}) %collective-permute-start.3) | collective-permute-done | bytes 43040 | tf_op jit(solution)/shard_map/ppermute | solution.py:554
  9.2 0.1 shard_map.98
  9.2 3.9 %collective-permute-start.4 = (f32[104,128]{1,0:T(8,128)S(1)}, f32[104,128]{1,0:T(8,128)S(1)}, u32[]{:S(2)}, u32[]{:S(2)}) collective-permute-start(f32[104,128]{1,0:T(8,128)S(1)} %get-tuple-element.39), channel_id=1, source_target_pairs={{0,1},{1,0},{2,3},{3,2},{4,5},{5,4},{6,7},{7,6},{8,16},{9,17},{10,... | collective-permute-start | bytes 159752 | tf_op jit(solution)/shard_map/ppermute | solution.py:563
  13.1 0.0 collective-permute-start.5
  13.1 0.0 copy-start
  13.1 0.9 %shard_map.99 = (f32[4,128,128]{2,1,0:T(8,128)S(1)}, bf16[128,1024]{1,0:T(8,128)(2,1)S(1)}) custom-call(s32[8,128]{1,0:T(8,128)S(1)} %get-tuple-element.42.cells, f32[3,8,128]{2,1,0:T(8,128)S(1)} %get-tuple-element.35.mult), custom_call_target="tpu_custom_call" | custom-call | flops 5000000000 | bytes 1000 | tf_op jit(solution)/shard_map/pallas_call | solution.py:555
  14.1 0.3 collective-permute-done.5.corner_near
  14.3 0.0 copy-done
  14.3 2.6 %shard_map.100 = (f32[2560,128]{1,0:T(8,128)S(1)}, f32[2400,128]{1,0:T(8,128)S(1)}, f32[2400,128]{1,0:T(8,128)S(1)}, f32[1200,128]{1,0:T(8,128)S(1)}, f32[1200,1...) custom-call(f32[8,6]{1,0:T(8,128)S(1)} %copy-done, ...), custom_call_target="tpu_custom_call" | custom-call | flops 1000 | bytes 1000 | tf_op jit(solution)/shard_map/pallas_call | solution.py:567
  17.0 0.1 collective-permute-done.far
  17.1 0.4 %shard_map.101.ribbon = f32[4,192,128]{2,1,0:T(8,128)S(1)} custom-call(f32[608,128]{1,0:T(8,128)S(1)} %collective-permute-done.far, f32[608,128]{1,0:T(8,128)S(1)} %collective-permute-done.2.near, f32[4,128,128]{2,1,0:T(8,128)S(1)} %get-tuple-element.43.dense, f32[96,128]{1,0:T(8,128)S(1)} %get-tuple-element.45.last), custom_call_target="tpu_custom_call" | custom-call | flops 1000 | bytes 1000 | tf_op jit(solution)/shard_map/pallas_call | solution.py:570
  17.5 0.2 collective-permute-done.4.corner
  17.7 1.9 %shard_map.102 = (f32[8,48,128]{2,1,0:T(8,128)S(1)}, f32[1200,128]{1,0:T(8,128)S(1)}, f32[3,8,128]{2,1,0:T(8,128)S(1)}) custom-call(f32[608,128]{1,0:T(8,128)S(1)} %collective-permute-done.far, f32[104,128]{1,0:T(8,128)S(1)} %collective-permute-done.4.corner, f32[104,128]{1,0:T(8,128)S(1)} %collective-permute-done.5.corner_near, ...), custom_call_target="tpu_custom_call" | custom-call | flops 1000 | bytes 1000 | tf_op jit(solution)/shard_map/pallas_call | solution.py:571
  19.6 12.6 %all_to_all.5.gathered = f32[8,48,128]{2,1,0:T(8,128)S(1)} all-to-all(f32[8,48,128]{2,1,0:T(8,128)S(1)} %get-tuple-element.59), channel_id=1, replica_groups=mesh['gx'=32,'gy'=8] {'gy'}, dimensions={0} | all-to-all | bytes 393216 | tf_op jit(solution)/shard_map/all_to_all | solution.py:577
  32.2 0.9 %shard_map.103 = (f32[384,128]{1,0:T(8,128)}, f32[3,8,128]{2,1,0:T(8,128)}, f32[3,128,128]{2,1,0:T(8,128)}) custom-call(f32[3,8,128]{2,1,0:T(8,128)S(1)} %get-tuple-element.57.updated, f32[1200,128]{1,0:T(8,128)S(1)} %get-tuple-element.58.low, f32[1200,128]{1,0:T(8,128)S(1)} %get-tuple-element.54.near_second.high, f32[8,48,128]{2,1,0:T(8,128)S(1)} %all_to_all.5.gathered), custom_call_target="tpu_custom_call" | custom-call | flops 1000 | bytes 1000 | tf_op jit(solution)/shard_map/pallas_call | solution.py:578
  (2 shorter events, 0.1 us)
Async XLA Ops:
  2.0 2.2 %collective-permute-start.2 = (f32[608,128]{1,0:T(8,128)S(1)}, f32[608,128]{1,0:T(8,128)S(1)}, u32[]{:S(2)}, u32[]{:S(2)}) collective-permute-start(f32[608,128]{1,0:T(8,128)S(1)} %get-tuple-element.38), channel_id=1, source_target_pairs={{0,8},{8,0},{16,24},{24,16},{32,40},{40,32},{48,56},{56,48},{64,72... | collective-permute-start | bytes 933896 | tf_op jit(solution)/shard_map/ppermute | solution.py:551
  2.1 5.7 %collective-permute-start.1 = (f32[3,28,128]{2,1,0:T(8,128)S(1)}, f32[3,28,128]{2,1,0:T(8,128)S(1)}, u32[]{:S(2)}, u32[]{:S(2)}) collective-permute-start(f32[3,28,128]{2,1,0:T(8,128)S(1)} %get-tuple-element.37), channel_id=1, source_target_pairs={{0,8},{1,2},{2,1},{3,4},{4,3},{5,6},{6,5},{7,15},{8,0},{9,10},{10,... | collective-permute-start | bytes 129032 | tf_op jit(solution)/shard_map/ppermute | solution.py:548
  2.6 14.5 %collective-permute-start = (f32[608,128]{1,0:T(8,128)S(1)}, f32[608,128]{1,0:T(8,128)S(1)}, u32[]{:S(2)}, u32[]{:S(2)}) collective-permute-start(f32[608,128]{1,0:T(8,128)S(1)} %get-tuple-element.36), channel_id=1, source_target_pairs={{0,1},{1,0},{2,3},{3,2},{4,5},{5,4},{6,7},{7,6},{8,16},{9,17},{10,... | collective-permute-start | bytes 933896 | tf_op jit(solution)/shard_map/ppermute | solution.py:552
  4.2 4.9 %collective-permute-start.3 = (f32[3,28,128]{2,1,0:T(8,128)S(1)}, f32[3,28,128]{2,1,0:T(8,128)S(1)}, u32[]{:S(2)}, u32[]{:S(2)}) collective-permute-start(f32[3,28,128]{2,1,0:T(8,128)S(1)} %shard_map.96), channel_id=1, source_target_pairs={{0,1},{1,0},{2,3},{3,2},{4,5},{5,4},{6,7},{7,6},{8,9},{9,8},{10,11... | collective-permute-start | bytes 129032 | tf_op jit(solution)/shard_map/ppermute | solution.py:554
  9.2 8.4 %collective-permute-start.4 = (f32[104,128]{1,0:T(8,128)S(1)}, f32[104,128]{1,0:T(8,128)S(1)}, u32[]{:S(2)}, u32[]{:S(2)}) collective-permute-start(f32[104,128]{1,0:T(8,128)S(1)} %get-tuple-element.39), channel_id=1, source_target_pairs={{0,1},{1,0},{2,3},{3,2},{4,5},{5,4},{6,7},{7,6},{8,16},{9,17},{10,... | collective-permute-start | bytes 159752 | tf_op jit(solution)/shard_map/ppermute | solution.py:563
  13.1 1.2 %collective-permute-start.5 = (f32[104,128]{1,0:T(8,128)S(1)}, f32[104,128]{1,0:T(8,128)S(1)}, u32[]{:S(2)}, u32[]{:S(2)}) collective-permute-start(f32[104,128]{1,0:T(8,128)S(1)} %get-tuple-element.40), channel_id=1, source_target_pairs={{0,8},{8,0},{16,24},{24,16},{32,40},{40,32},{48,56},{56,48},{64,72... | collective-permute-start | bytes 159752 | tf_op jit(solution)/shard_map/ppermute | solution.py:564
  13.1 1.2 %copy-start = (f32[8,6]{1,0:T(8,128)S(1)}, f32[8,6]{1,0:T(8,128)}, u32[]{:S(2)}) copy-start(f32[8,6]{1,0:T(8,128)} %stiffness.1) | copy-start | bytes 580

commit v9 on v8

--- a/solution.py
+++ b/solution.py
@@ -92,8 +92,8 @@
 
 def pack_first(
     disp, rhs, labels, cells_in, mult_in,
-    y_other, own, cells, mult,
-    raw_labels, arrived,
+    far, near, own, cells, mult,
+    raw_labels, raw_cells, arrived,
 ):
     flip = odd("gx")
     pairs = []
@@ -103,22 +103,13 @@
         for c in range(3):
             pairs.append((disp.at[rows_of(c * CX + x, CY)], own.at[rows_of(c * CX + g, CY)]))
             pairs.append((rhs.at[rows_of(c * CX + x, CY)], own.at[rows_of(OWN_RHS0 + c * CX + g, CY)]))
-    pairs += [(cells_in, cells), (mult_in, mult)]
+    pairs += [(cells_in, raw_cells), (mult_in, mult)]
     copies = [pltpu.make_async_copy(a, b, arrived.at[i]) for i, (a, b) in enumerate(pairs)]
     for copy in copies:
         copy.start()
     for copy in copies:
         copy.wait()
     own[pl.ds(OWN_LAB0 * CY, CX * CY), :] = raw_labels[...].astype(F32)
-    up = odd("gy") == 0
-    for k in range(HALO):
-        first = own[pl.ds(k, OWN, stride=CY), :]
-        last = own[pl.ds(CY - HALO + k, OWN, stride=CY), :]
-        y_other[k] = jnp.where(up, first, last)
-
-
-def pack_sides(own, raw_cells, mult, far, near, cells):
-    flip = odd("gx")
     block_plane = raw_cells[...] // (CY * NZ)
     turned = raw_cells[...] + flip * (CX - 1 - 2 * block_plane) * (CY * NZ)
     cells[...] = turned
@@ -131,12 +122,13 @@
             side[pl.ds(SIDE * CY + (1 + c) * SLOT_ROWS, SLOT_ROWS), :] = mult[c]
 
 
-def pack_pair(own, near, y_pair):
+def pack_y(own, near, y_other, y_pair):
     up = odd("gy") == 0
     for k in range(HALO):
         first = own[pl.ds(k, OWN, stride=CY), :]
         last = own[pl.ds(CY - HALO + k, OWN, stride=CY), :]
         y_pair[k] = jnp.where(up, last, first)
+        y_other[k] = jnp.where(up, first, last)
 
 
 def reach():
@@ -533,11 +525,16 @@
     block = CX * CY
     copies = 2 + 7 * CX
     slots = jax.ShapeDtypeStruct((SLOT_ROWS, 128), jnp.int32)
-    y_other, own, raw_cells, mult = call(
+    side = f32(SIDE * CY + IFACE, NZ)
+    far, near, own, cells, mult = call(
         pack_first,
-        [f32(HALO, OWN, NZ), f32(OWN * CY, NZ), slots, f32(3, SLOT_ROWS, 128)],
+        [side, side, f32(OWN * CY, NZ), slots, f32(3, SLOT_ROWS, 128)],
         [HBM] * 5,
-        scratch=[pltpu.VMEM((block, NZ), jnp.int32), pltpu.SemaphoreType.DMA((copies,))],
+        scratch=[
+            pltpu.VMEM((block, NZ), jnp.int32),
+            pltpu.VMEM((SLOT_ROWS, 128), jnp.int32),
+            pltpu.SemaphoreType.DMA((copies,)),
+        ],
     )(
         in_hbm(displacement.reshape(3 * block, NZ)),
         in_hbm(rhs.reshape(3 * block, NZ)),
@@ -545,12 +542,10 @@
         in_hbm(rows.reshape(SLOT_ROWS, 128)),
         in_hbm(multipliers.reshape(3, SLOT_ROWS, 128)),
     )
-    y_other = lax.ppermute(y_other, ("gx", "gy"), other_y())
-    side = f32(SIDE * CY + IFACE, NZ)
-    far, near, cells = call(pack_sides, [side, side, slots], [VMEM] * 3)(own, raw_cells, mult)
     near = lax.ppermute(near, "gx", pair(N_GX))
     far = lax.ppermute(far, ("gx", "gy"), other_x())
-    (y_pair,) = call(pack_pair, [f32(HALO, OWN, NZ)], [VMEM] * 2)(own, near)
+    y_other, y_pair = call(pack_y, [f32(HALO, OWN, NZ)] * 2, [VMEM] * 2)(own, near)
+    y_other = lax.ppermute(y_other, ("gx", "gy"), other_y())
     y_pair = lax.ppermute(y_pair, "gy", pair(N_GY))
     dense, at_depth = call(
         spread_own, [f32(4, block, NZ), jax.ShapeDtypeStruct((NZ, 8 * 128), BF16)], [VMEM] * 2, flops=5 * 10**9

time: 33.4 us -> 36.9 us (1.10)
  the two profiles are of different devices: /device:TPU:128 before, /device:TPU:71 now
where the time goes in v9:
time: 36.9 us; the launch traced here: 36.6 us
  blocking collectives  14.3 us (39%)
  starting transfers between devices  10.1 us (27%)
  Pallas kernels  8.25 us (22%)
  waiting for transfers between devices  2.57 us (7%)
  between operations  1.36 us (4%)
    all_to_all x1, blocking collectives, body(): gathered = lax.all_to_all(message, 'gy', 0, 0)  14.3 us
    ppermute x1, starting transfers between devices, body(): far = lax.ppermute(far, ('gx', 'gy'), other_x())  4.1 us
    pallas_call x1, Pallas kernels, body(): call(near_part, arrays + [f32(LABELS * 6, NZ), f32(3 * CY, NZ)], [SMEM, V...  2.61 us
    ppermute x1, starting transfers between devices, body(): corner = lax.ppermute(corner, ('gx', 'gy'), other_x())  2.6 us
    ppermute x1, starting transfers between devices, body(): y_pair = lax.ppermute(y_pair, 'gy', pair(N_GY))  2.58 us
    pallas_call x1, Pallas kernels, body(): call(far_part, [f32(N_GY, 3 * CY // 2, NZ), three, f32(3, SLOT_ROWS, 128)...  1.92 us
    pallas_call x1, Pallas kernels, body(): call(pack_first, [side, side, f32(OWN * CY, NZ), slots, f32(3, SLOT_ROWS,...  1.29 us
    ppermute x1, waiting for transfers between devices, body(): y_pair = lax.ppermute(y_pair, 'gy', pair(N_GY))  1.27 us
  transfers between devices with their start and end apart: 6, of which 3 were waited for; matrix products, arithmetic and copies ran while one was open for 0% of the time, Pallas kernels for 11%

profile of v9, /device:TPU:71, one launch (start us, length us, event | category | flops | bytes accessed | tf_op | source)
XLA Modules:
  0.0 36.6 jit_solution(12813878472250296124)
XLA Ops:
  0.6 1.3 %shard_map.94 = (f32[608,128]{1,0:T(8,128)S(1)}, f32[608,128]{1,0:T(8,128)S(1)}, f32[896,128]{1,0:T(8,128)S(1)}, s32[8,128]{1,0:T(8,128)S(1)}, f32[3,8,128]{2,1,0:T(8,128)S(1)}) custom-call(f32[384,128]{1,0:T(8,128)} %bitcast.10, f32[384,128]{1,0:T(8,128)} %bitcast.11, s32[128,128]{1,0:T(8,128)} %bitcast.12, s32[8,128]{1,0:T(8,128)} %bitcast.14, ...), custom_call_target="tpu_custom_call" | custom-call | flops 1000 | bytes 1000 | tf_op jit(solution)/shard_map/pallas_call | solution.py:529
  1.9 0.8 %collective-permute-start.1 = (f32[608,128]{1,0:T(8,128)S(1)}, f32[608,128]{1,0:T(8,128)S(1)}, u32[]{:S(2)}, u32[]{:S(2)}) collective-permute-start(f32[608,128]{1,0:T(8,128)S(1)} %get-tuple-element.35), channel_id=1, source_target_pairs={{0,8},{8,0},{16,24},{24,16},{32,40},{40,32},{48,56},{56,48},{64,72... | collective-permute-start | bytes 933896 | tf_op jit(solution)/shard_map/ppermute | solution.py:545
  2.7 4.1 %collective-permute-start = (f32[608,128]{1,0:T(8,128)S(1)}, f32[608,128]{1,0:T(8,128)S(1)}, u32[]{:S(2)}, u32[]{:S(2)}) collective-permute-start(f32[608,128]{1,0:T(8,128)S(1)} %get-tuple-element.33), channel_id=1, source_target_pairs={{0,1},{1,0},{2,3},{3,2},{4,5},{5,4},{6,7},{7,6},{8,16},{9,17},{10,... | collective-permute-start | bytes 933896 | tf_op jit(solution)/shard_map/ppermute | solution.py:546
  6.8 0.0 collective-permute-done.1.near
  6.8 0.1 shard_map.95
  6.9 0.1 collective-permute-start.2
  7.0 2.6 %collective-permute-start.3 = (f32[3,28,128]{2,1,0:T(8,128)S(1)}, f32[3,28,128]{2,1,0:T(8,128)S(1)}, u32[]{:S(2)}, u32[]{:S(2)}) collective-permute-start(f32[3,28,128]{2,1,0:T(8,128)S(1)} %get-tuple-element.37), channel_id=1, source_target_pairs={{0,1},{1,0},{2,3},{3,2},{4,5},{5,4},{6,7},{7,6},{8,9},{9,8},{10,11... | collective-permute-start | bytes 129032 | tf_op jit(solution)/shard_map/ppermute | solution.py:549
  10.2 0.0 collective-permute-done.2.y_other
  10.2 1.3 %collective-permute-done.3.y_pair = f32[3,28,128]{2,1,0:T(8,128)S(1)} collective-permute-done((f32[3,28,128]{2,1,0:T(8,128)S(1)}, f32[3,28,128]{2,1,0:T(8,128)S(1)}, u32[]{:S(2)}, u32[]{:S(2)}) %collective-permute-start.3) | collective-permute-done | bytes 43040 | tf_op jit(solution)/shard_map/ppermute | solution.py:549
  11.5 0.1 shard_map.97
  11.6 2.6 %collective-permute-start.4 = (f32[104,128]{1,0:T(8,128)S(1)}, f32[104,128]{1,0:T(8,128)S(1)}, u32[]{:S(2)}, u32[]{:S(2)}) collective-permute-start(f32[104,128]{1,0:T(8,128)S(1)} %get-tuple-element.38), channel_id=1, source_target_pairs={{0,1},{1,0},{2,3},{3,2},{4,5},{5,4},{6,7},{7,6},{8,16},{9,17},{10,... | collective-permute-start | bytes 159752 | tf_op jit(solution)/shard_map/ppermute | solution.py:558
  14.2 0.0 collective-permute-start.5
  14.2 0.0 copy-start
  14.2 0.9 %shard_map.98 = (f32[4,128,128]{2,1,0:T(8,128)S(1)}, bf16[128,1024]{1,0:T(8,128)(2,1)S(1)}) custom-call(s32[8,128]{1,0:T(8,128)S(1)} %get-tuple-element.41.cells, f32[3,8,128]{2,1,0:T(8,128)S(1)} %get-tuple-element.42.mult), custom_call_target="tpu_custom_call" | custom-call | flops 5000000000 | bytes 1000 | tf_op jit(solution)/shard_map/pallas_call | solution.py:550
  15.2 0.3 collective-permute-done.5.corner_near
  15.4 0.0 copy-done
  15.4 2.6 %shard_map.99 = (f32[2560,128]{1,0:T(8,128)S(1)}, f32[2400,128]{1,0:T(8,128)S(1)}, f32[2400,128]{1,0:T(8,128)S(1)}, f32[1200,128]{1,0:T(8,128)S(1)}, f32[1200,12...) custom-call(f32[8,6]{1,0:T(8,128)S(1)} %copy-done, ...), custom_call_target="tpu_custom_call" | custom-call | flops 1000 | bytes 1000 | tf_op jit(solution)/shard_map/pallas_call | solution.py:562
  18.1 0.0 collective-permute-done.far
  18.1 0.4 %shard_map.100.ribbon = f32[4,192,128]{2,1,0:T(8,128)S(1)} custom-call(f32[608,128]{1,0:T(8,128)S(1)} %collective-permute-done.far, f32[608,128]{1,0:T(8,128)S(1)} %collective-permute-done.1.near, f32[4,128,128]{2,1,0:T(8,128)S(1)} %get-tuple-element.43.dense, f32[96,128]{1,0:T(8,128)S(1)} %get-tuple-element.45.last), custom_call_target="tpu_custom_call" | custom-call | flops 1000 | bytes 1000 | tf_op jit(solution)/shard_map/pallas_call | solution.py:565
  18.4 1.0 %collective-permute-done.4.corner = f32[104,128]{1,0:T(8,128)S(1)} collective-permute-done((f32[104,128]{1,0:T(8,128)S(1)}, f32[104,128]{1,0:T(8,128)S(1)}, u32[]{:S(2)}, u32[]{:S(2)}) %collective-permute-start.4) | collective-permute-done | bytes 53280 | tf_op jit(solution)/shard_map/ppermute | solution.py:558
  19.5 1.9 %shard_map.101 = (f32[8,48,128]{2,1,0:T(8,128)S(1)}, f32[1200,128]{1,0:T(8,128)S(1)}, f32[3,8,128]{2,1,0:T(8,128)S(1)}) custom-call(f32[608,128]{1,0:T(8,128)S(1)} %collective-permute-done.far, f32[104,128]{1,0:T(8,128)S(1)} %collective-permute-done.4.corner, f32[104,128]{1,0:T(8,128)S(1)} %collective-permute-done.5.corner_near, ...), custom_call_target="tpu_custom_call" | custom-call | flops 1000 | bytes 1000 | tf_op jit(solution)/shard_map/pallas_call | solution.py:566
  21.4 14.3 %all_to_all.5.gathered = f32[8,48,128]{2,1,0:T(8,128)S(1)} all-to-all(f32[8,48,128]{2,1,0:T(8,128)S(1)} %get-tuple-element.59), channel_id=1, replica_groups=mesh['gx'=32,'gy'=8] {'gy'}, dimensions={0} | all-to-all | bytes 393216 | tf_op jit(solution)/shard_map/all_to_all | solution.py:572
  35.7 0.9 %shard_map.102 = (f32[384,128]{1,0:T(8,128)}, f32[3,8,128]{2,1,0:T(8,128)}, f32[3,128,128]{2,1,0:T(8,128)}) custom-call(f32[3,8,128]{2,1,0:T(8,128)S(1)} %get-tuple-element.57.updated, f32[1200,128]{1,0:T(8,128)S(1)} %get-tuple-element.58.low, f32[1200,128]{1,0:T(8,128)S(1)} %get-tuple-element.54.near_second.high, f32[8,48,128]{2,1,0:T(8,128)S(1)} %all_to_all.5.gathered), custom_call_target="tpu_custom_call" | custom-call | flops 1000 | bytes 1000 | tf_op jit(solution)/shard_map/pallas_call | solution.py:573
  (1 shorter events, 0.0 us)
Async XLA Ops:
  1.9 4.9 %collective-permute-start.1 = (f32[608,128]{1,0:T(8,128)S(1)}, f32[608,128]{1,0:T(8,128)S(1)}, u32[]{:S(2)}, u32[]{:S(2)}) collective-permute-start(f32[608,128]{1,0:T(8,128)S(1)} %get-tuple-element.35), channel_id=1, source_target_pairs={{0,8},{8,0},{16,24},{24,16},{32,40},{40,32},{48,56},{56,48},{64,72... | collective-permute-start | bytes 933896 | tf_op jit(solution)/shard_map/ppermute | solution.py:545
  2.7 15.4 %collective-permute-start = (f32[608,128]{1,0:T(8,128)S(1)}, f32[608,128]{1,0:T(8,128)S(1)}, u32[]{:S(2)}, u32[]{:S(2)}) collective-permute-start(f32[608,128]{1,0:T(8,128)S(1)} %get-tuple-element.33), channel_id=1, source_target_pairs={{0,1},{1,0},{2,3},{3,2},{4,5},{5,4},{6,7},{7,6},{8,16},{9,17},{10,... | collective-permute-start | bytes 933896 | tf_op jit(solution)/shard_map/ppermute | solution.py:546
  6.9 3.4 %collective-permute-start.2 = (f32[3,28,128]{2,1,0:T(8,128)S(1)}, f32[3,28,128]{2,1,0:T(8,128)S(1)}, u32[]{:S(2)}, u32[]{:S(2)}) collective-permute-start(f32[3,28,128]{2,1,0:T(8,128)S(1)} %get-tuple-element.36), channel_id=1, source_target_pairs={{0,8},{1,2},{2,1},{3,4},{4,3},{5,6},{6,5},{7,15},{8,0},{9,10},{10,... | collective-permute-start | bytes 129032 | tf_op jit(solution)/shard_map/ppermute | solution.py:548
  7.0 4.6 %collective-permute-start.3 = (f32[3,28,128]{2,1,0:T(8,128)S(1)}, f32[3,28,128]{2,1,0:T(8,128)S(1)}, u32[]{:S(2)}, u32[]{:S(2)}) collective-permute-start(f32[3,28,128]{2,1,0:T(8,128)S(1)} %get-tuple-element.37), channel_id=1, source_target_pairs={{0,1},{1,0},{2,3},{3,2},{4,5},{5,4},{6,7},{7,6},{8,9},{9,8},{10,11... | collective-permute-start | bytes 129032 | tf_op jit(solution)/shard_map/ppermute | solution.py:549
  11.6 7.9 %collective-permute-start.4 = (f32[104,128]{1,0:T(8,128)S(1)}, f32[104,128]{1,0:T(8,128)S(1)}, u32[]{:S(2)}, u32[]{:S(2)}) collective-permute-start(f32[104,128]{1,0:T(8,128)S(1)} %get-tuple-element.38), channel_id=1, source_target_pairs={{0,1},{1,0},{2,3},{3,2},{4,5},{5,4},{6,7},{7,6},{8,16},{9,17},{10,... | collective-permute-start | bytes 159752 | tf_op jit(solution)/shard_map/ppermute | solution.py:558
  14.2 1.2 %collective-permute-start.5 = (f32[104,128]{1,0:T(8,128)S(1)}, f32[104,128]{1,0:T(8,128)S(1)}, u32[]{:S(2)}, u32[]{:S(2)}) collective-permute-start(f32[104,128]{1,0:T(8,128)S(1)} %get-tuple-element.39), channel_id=1, source_target_pairs={{0,8},{8,0},{16,24},{24,16},{32,40},{40,32},{48,56},{56,48},{64,72... | collective-permute-start | bytes 159752 | tf_op jit(solution)/shard_map/ppermute | solution.py:559
  14.2 1.2 %copy-start = (f32[8,6]{1,0:T(8,128)S(1)}, f32[8,6]{1,0:T(8,128)}, u32[]{:S(2)}) copy-start(f32[8,6]{1,0:T(8,128)} %stiffness.1) | copy-start | bytes 580

commit v10 on v8

--- a/solution.py
+++ b/solution.py
@@ -24,6 +24,8 @@
 OWN_LAB0 = 3 * CX
 OWN_RHS0 = OWN_LAB0 + CX
 OWN = OWN_RHS0 + 3 * CX
+ROOM = 32
+SPARE = 8
 SIDE = 3 * HALO + HALO + 3 * (HALO - 1)
 SLOT_ROWS = SLOTS // 128
 IFACE = 4 * SLOT_ROWS
@@ -156,7 +158,7 @@
 def pack_second(y_other, y_pair, count, inner, corner_far, corner_near, wide, limit):
     low, high = reach()
     up = odd("gy") == 0
-    wide[...] = inner[...]
+    wide[pl.ds(0, OWN * ROWS), :] = inner[pl.ds(0, OWN * ROWS), :]
     for k in range(HALO):
         wide[pl.ds(CY + k, OWN, stride=ROWS), :] = high * jnp.where(up, y_pair[k], y_other[k])
         wide[pl.ds(ROWS - HALO + k, OWN, stride=ROWS), :] = low * jnp.where(up, y_other[k], y_pair[k])
@@ -535,7 +537,7 @@
     slots = jax.ShapeDtypeStruct((SLOT_ROWS, 128), jnp.int32)
     y_other, own, raw_cells, mult = call(
         pack_first,
-        [f32(HALO, OWN, NZ), f32(OWN * CY, NZ), slots, f32(3, SLOT_ROWS, 128)],
+        [f32(HALO, OWN, NZ), f32(ROOM * CY, NZ), slots, f32(3, SLOT_ROWS, 128)],
         [HBM] * 5,
         scratch=[pltpu.VMEM((block, NZ), jnp.int32), pltpu.SemaphoreType.DMA((copies,))],
     )(
@@ -555,15 +557,15 @@
     dense, at_depth = call(
         spread_own, [f32(4, block, NZ), jax.ShapeDtypeStruct((NZ, 8 * 128), BF16)], [VMEM] * 2, flops=5 * 10**9
     )(cells, mult)
-    (inner,) = call(pack_wide, [f32(OWN * ROWS, NZ)], [VMEM], flops=5 * 10**9)(own)
+    (inner,) = call(pack_wide, [f32(ROOM * ROWS, NZ)], [VMEM], flops=5 * 10**9)(own)
     tile = f32(CORNER + SLOT_ROWS, NZ)
     corner, corner_near, own, limit = call(
-        pack_second, [tile, tile, f32(OWN * ROWS, NZ), f32(SLOT_ROWS, NZ)], [VMEM, VMEM, SMEM, VMEM]
+        pack_second, [tile, tile, f32(ROOM * ROWS, NZ), f32(SLOT_ROWS, NZ)], [VMEM, VMEM, SMEM, VMEM]
     )(y_other, y_pair, counts, inner)
     corner = lax.ppermute(corner, ("gx", "gy"), other_x())
     corner_near = lax.ppermute(corner_near, "gx", pair(N_GX))
     three, six = f32(3 * PX * ROWS, NZ), f32(6 * PX * ROWS, NZ)
-    arrays = [f32(FIELDS * ROWS, NZ), six, six] + [three] * 6
+    arrays = [f32(FIELDS * ROWS + SPARE, NZ), six, six] + [three] * 6
     half = call(
         near_part, arrays + [f32(LABELS * 6, NZ), f32(3 * CY, NZ)], [SMEM, VMEM, VMEM, VMEM]
     )(stiffness, own, near, corner_near)

time: 33.4 us -> 33.4 us (level)
    ppermute x1, waiting for transfers between devices: 0.12 us -> 0.53 us  [body(): far = lax.ppermute(far, ('gx', 'gy'), other_x())]
  transfers between devices with their start and end apart: 6 -> 6, of which waited for: 4 -> 3; matrix products, arithmetic and copies ran while one was open for 0% -> 0% of each run, Pallas kernels for 12% -> 13%
where the time goes in v10:
time: 33.4 us; the launch traced here: 33.1 us
  blocking collectives  12.6 us (38%)
  starting transfers between devices  8.69 us (26%)
  Pallas kernels  8.36 us (25%)
  waiting for transfers between devices  2.1 us (6%)
  between operations  1.38 us (4%)
    all_to_all x1, blocking collectives, body(): gathered = lax.all_to_all(message, 'gy', 0, 0)  12.6 us
    ppermute x1, starting transfers between devices, body(): corner = lax.ppermute(corner, ('gx', 'gy'), other_x())  3.58 us
    ppermute x1, starting transfers between devices, body(): y_pair = lax.ppermute(y_pair, 'gy', pair(N_GY))  2.88 us
    pallas_call x1, Pallas kernels, body(): call(near_part, arrays + [f32(LABELS * 6, NZ), f32(3 * CY, NZ)], [SMEM, V...  2.66 us
    pallas_call x1, Pallas kernels, body(): call(far_part, [f32(N_GY, 3 * CY // 2, NZ), three, f32(3, SLOT_ROWS, 128)...  1.93 us
    ppermute x1, starting transfers between devices, body(): far = lax.ppermute(far, ('gx', 'gy'), other_x())  1.55 us
    ppermute x1, waiting for transfers between devices, body(): y_pair = lax.ppermute(y_pair, 'gy', pair(N_GY))  1.37 us
    pallas_call x1, Pallas kernels, body(): call(pack_first, [f32(HALO, OWN, NZ), f32(ROOM * CY, NZ), slots, f32(3, S...  1.3 us
  transfers between devices with their start and end apart: 6, of which 3 were waited for; matrix products, arithmetic and copies ran while one was open for 0% of the time, Pallas kernels for 13%

profile of v10, /device:TPU:128, one launch (start us, length us, event | category | flops | bytes accessed | tf_op | source)
XLA Modules:
  0.0 33.1 jit_solution(918756068398802113)
XLA Ops:
  0.6 1.3 %shard_map.94 = (f32[3,28,128]{2,1,0:T(8,128)S(1)}, f32[1024,128]{1,0:T(8,128)S(1)}, s32[8,128]{1,0:T(8,128)S(1)}, f32[3,8,128]{2,1,0:T(8,128)S(1)}) custom-call(f32[384,128]{1,0:T(8,128)} %bitcast.10, f32[384,128]{1,0:T(8,128)} %bitcast.11, s32[128,128]{1,0:T(8,128)} %bitcast.12, s32[8,128]{1,0:T(8,128)} %bitcast.14, f32[3,8,128]{2,1,0:T(8,128)} %bitcast.13), custom_call_target="tpu_custom_call" | custom-call | flops 1000 | bytes 1000 | tf_op jit(solution)/shard_map/pallas_call | solution.py:538
  2.0 0.1 collective-permute-start.2
  2.1 0.5 %collective-permute-start.1 = (f32[3,28,128]{2,1,0:T(8,128)S(1)}, f32[3,28,128]{2,1,0:T(8,128)S(1)}, u32[]{:S(2)}, u32[]{:S(2)}) collective-permute-start(f32[3,28,128]{2,1,0:T(8,128)S(1)} %get-tuple-element.37), channel_id=1, source_target_pairs={{0,8},{1,2},{2,1},{3,4},{4,3},{5,6},{6,5},{7,15},{8,0},{9,10},{10,... | collective-permute-start | bytes 129032 | tf_op jit(solution)/shard_map/ppermute | solution.py:550
  2.6 1.6 %collective-permute-start = (f32[608,128]{1,0:T(8,128)S(1)}, f32[608,128]{1,0:T(8,128)S(1)}, u32[]{:S(2)}, u32[]{:S(2)}) collective-permute-start(f32[608,128]{1,0:T(8,128)S(1)} %get-tuple-element.36), channel_id=1, source_target_pairs={{0,1},{1,0},{2,3},{3,2},{4,5},{5,4},{6,7},{7,6},{8,16},{9,17},{10,... | collective-permute-start | bytes 933896 | tf_op jit(solution)/shard_map/ppermute | solution.py:554
  4.1 0.0 collective-permute-done.2.near
  4.1 0.1 shard_map.96
  4.2 2.9 %collective-permute-start.3 = (f32[3,28,128]{2,1,0:T(8,128)S(1)}, f32[3,28,128]{2,1,0:T(8,128)S(1)}, u32[]{:S(2)}, u32[]{:S(2)}) collective-permute-start(f32[3,28,128]{2,1,0:T(8,128)S(1)} %shard_map.96), channel_id=1, source_target_pairs={{0,1},{1,0},{2,3},{3,2},{4,5},{5,4},{6,7},{7,6},{8,9},{9,8},{10,11... | collective-permute-start | bytes 129032 | tf_op jit(solution)/shard_map/ppermute | solution.py:556
  7.8 0.0 collective-permute-done.1.y_other
  7.8 1.4 %collective-permute-done.3.y_pair = f32[3,28,128]{2,1,0:T(8,128)S(1)} collective-permute-done((f32[3,28,128]{2,1,0:T(8,128)S(1)}, f32[3,28,128]{2,1,0:T(8,128)S(1)}, u32[]{:S(2)}, u32[]{:S(2)}) %collective-permute-start.3) | collective-permute-done | bytes 43040 | tf_op jit(solution)/shard_map/ppermute | solution.py:556
  9.2 0.1 shard_map.98
  9.2 0.1 collective-permute-start.5
  9.3 3.6 %collective-permute-start.4 = (f32[104,128]{1,0:T(8,128)S(1)}, f32[104,128]{1,0:T(8,128)S(1)}, u32[]{:S(2)}, u32[]{:S(2)}) collective-permute-start(f32[104,128]{1,0:T(8,128)S(1)} %get-tuple-element.39), channel_id=1, source_target_pairs={{0,1},{1,0},{2,3},{3,2},{4,5},{5,4},{6,7},{7,6},{8,16},{9,17},{10,... | collective-permute-start | bytes 159752 | tf_op jit(solution)/shard_map/ppermute | solution.py:565
  12.9 0.0 copy-start
  12.9 0.9 %shard_map.99 = (f32[4,128,128]{2,1,0:T(8,128)S(1)}, bf16[128,1024]{1,0:T(8,128)(2,1)S(1)}) custom-call(s32[8,128]{1,0:T(8,128)S(1)} %get-tuple-element.42.cells, f32[3,8,128]{2,1,0:T(8,128)S(1)} %get-tuple-element.35.mult), custom_call_target="tpu_custom_call" | custom-call | flops 5000000000 | bytes 1000 | tf_op jit(solution)/shard_map/pallas_call | solution.py:557
  13.9 0.0 collective-permute-done.5.corner_near
  13.9 0.0 copy-done
  13.9 2.7 %shard_map.100 = (f32[2568,128]{1,0:T(8,128)S(1)}, f32[2400,128]{1,0:T(8,128)S(1)}, f32[2400,128]{1,0:T(8,128)S(1)}, f32[1200,128]{1,0:T(8,128)S(1)}, f32[1200,1...) custom-call(f32[8,6]{1,0:T(8,128)S(1)} %copy-done, ...), custom_call_target="tpu_custom_call" | custom-call | flops 1000 | bytes 1000 | tf_op jit(solution)/shard_map/pallas_call | solution.py:569
  16.6 0.5 %collective-permute-done.far = f32[608,128]{1,0:T(8,128)S(1)} collective-permute-done((f32[608,128]{1,0:T(8,128)S(1)}, f32[608,128]{1,0:T(8,128)S(1)}, u32[]{:S(2)}, u32[]{:S(2)}) %collective-permute-start) | collective-permute-done | bytes 311328 | tf_op jit(solution)/shard_map/ppermute | solution.py:554
  17.1 0.4 %shard_map.101.ribbon = f32[4,192,128]{2,1,0:T(8,128)S(1)} custom-call(f32[608,128]{1,0:T(8,128)S(1)} %collective-permute-done.far, f32[608,128]{1,0:T(8,128)S(1)} %collective-permute-done.2.near, f32[4,128,128]{2,1,0:T(8,128)S(1)} %get-tuple-element.43.dense, f32[96,128]{1,0:T(8,128)S(1)} %get-tuple-element.45.last), custom_call_target="tpu_custom_call" | custom-call | flops 1000 | bytes 1000 | tf_op jit(solution)/shard_map/pallas_call | solution.py:572
  17.5 0.2 collective-permute-done.4.corner
  17.7 1.9 %shard_map.102 = (f32[8,48,128]{2,1,0:T(8,128)S(1)}, f32[1200,128]{1,0:T(8,128)S(1)}, f32[3,8,128]{2,1,0:T(8,128)S(1)}) custom-call(f32[608,128]{1,0:T(8,128)S(1)} %collective-permute-done.far, f32[104,128]{1,0:T(8,128)S(1)} %collective-permute-done.4.corner, f32[104,128]{1,0:T(8,128)S(1)} %collective-permute-done.5.corner_near, ...), custom_call_target="tpu_custom_call" | custom-call | flops 1000 | bytes 1000 | tf_op jit(solution)/shard_map/pallas_call | solution.py:573
  19.6 12.6 %all_to_all.5.gathered = f32[8,48,128]{2,1,0:T(8,128)S(1)} all-to-all(f32[8,48,128]{2,1,0:T(8,128)S(1)} %get-tuple-element.59), channel_id=1, replica_groups=mesh['gx'=32,'gy'=8] {'gy'}, dimensions={0} | all-to-all | bytes 393216 | tf_op jit(solution)/shard_map/all_to_all | solution.py:579
  32.2 0.9 %shard_map.103 = (f32[384,128]{1,0:T(8,128)}, f32[3,8,128]{2,1,0:T(8,128)}, f32[3,128,128]{2,1,0:T(8,128)}) custom-call(f32[3,8,128]{2,1,0:T(8,128)S(1)} %get-tuple-element.57.updated, f32[1200,128]{1,0:T(8,128)S(1)} %get-tuple-element.58.low, f32[1200,128]{1,0:T(8,128)S(1)} %get-tuple-element.54.near_second.high, f32[8,48,128]{2,1,0:T(8,128)S(1)} %all_to_all.5.gathered), custom_call_target="tpu_custom_call" | custom-call | flops 1000 | bytes 1000 | tf_op jit(solution)/shard_map/pallas_call | solution.py:580
  (2 shorter events, 0.1 us)
Async XLA Ops:
  2.0 2.2 %collective-permute-start.2 = (f32[608,128]{1,0:T(8,128)S(1)}, f32[608,128]{1,0:T(8,128)S(1)}, u32[]{:S(2)}, u32[]{:S(2)}) collective-permute-start(f32[608,128]{1,0:T(8,128)S(1)} %get-tuple-element.38), channel_id=1, source_target_pairs={{0,8},{8,0},{16,24},{24,16},{32,40},{40,32},{48,56},{56,48},{64,72... | collective-permute-start | bytes 933896 | tf_op jit(solution)/shard_map/ppermute | solution.py:553
  2.1 5.7 %collective-permute-start.1 = (f32[3,28,128]{2,1,0:T(8,128)S(1)}, f32[3,28,128]{2,1,0:T(8,128)S(1)}, u32[]{:S(2)}, u32[]{:S(2)}) collective-permute-start(f32[3,28,128]{2,1,0:T(8,128)S(1)} %get-tuple-element.37), channel_id=1, source_target_pairs={{0,8},{1,2},{2,1},{3,4},{4,3},{5,6},{6,5},{7,15},{8,0},{9,10},{10,... | collective-permute-start | bytes 129032 | tf_op jit(solution)/shard_map/ppermute | solution.py:550
  2.6 14.5 %collective-permute-start = (f32[608,128]{1,0:T(8,128)S(1)}, f32[608,128]{1,0:T(8,128)S(1)}, u32[]{:S(2)}, u32[]{:S(2)}) collective-permute-start(f32[608,128]{1,0:T(8,128)S(1)} %get-tuple-element.36), channel_id=1, source_target_pairs={{0,1},{1,0},{2,3},{3,2},{4,5},{5,4},{6,7},{7,6},{8,16},{9,17},{10,... | collective-permute-start | bytes 933896 | tf_op jit(solution)/shard_map/ppermute | solution.py:554
  4.2 4.9 %collective-permute-start.3 = (f32[3,28,128]{2,1,0:T(8,128)S(1)}, f32[3,28,128]{2,1,0:T(8,128)S(1)}, u32[]{:S(2)}, u32[]{:S(2)}) collective-permute-start(f32[3,28,128]{2,1,0:T(8,128)S(1)} %shard_map.96), channel_id=1, source_target_pairs={{0,1},{1,0},{2,3},{3,2},{4,5},{5,4},{6,7},{7,6},{8,9},{9,8},{10,11... | collective-permute-start | bytes 129032 | tf_op jit(solution)/shard_map/ppermute | solution.py:556
  9.2 4.6 %collective-permute-start.5 = (f32[104,128]{1,0:T(8,128)S(1)}, f32[104,128]{1,0:T(8,128)S(1)}, u32[]{:S(2)}, u32[]{:S(2)}) collective-permute-start(f32[104,128]{1,0:T(8,128)S(1)} %get-tuple-element.40), channel_id=1, source_target_pairs={{0,8},{8,0},{16,24},{24,16},{32,40},{40,32},{48,56},{56,48},{64,72... | collective-permute-start | bytes 159752 | tf_op jit(solution)/shard_map/ppermute | solution.py:566
  9.3 8.3 %collective-permute-start.4 = (f32[104,128]{1,0:T(8,128)S(1)}, f32[104,128]{1,0:T(8,128)S(1)}, u32[]{:S(2)}, u32[]{:S(2)}) collective-permute-start(f32[104,128]{1,0:T(8,128)S(1)} %get-tuple-element.39), channel_id=1, source_target_pairs={{0,1},{1,0},{2,3},{3,2},{4,5},{5,4},{6,7},{7,6},{8,16},{9,17},{10,... | collective-permute-start | bytes 159752 | tf_op jit(solution)/shard_map/ppermute | solution.py:565
  12.9 1.0 %copy-start = (f32[8,6]{1,0:T(8,128)S(1)}, f32[8,6]{1,0:T(8,128)}, u32[]{:S(2)}) copy-start(f32[8,6]{1,0:T(8,128)} %stiffness.1) | copy-start | bytes 580

commit v11 on v10

--- a/solution.py
+++ b/solution.py
@@ -155,7 +155,7 @@
         wide[pl.ds(j * ROWS + CY, ROWS - CY), :] = jnp.zeros((ROWS - CY, NZ), F32)
 
 
-def pack_second(y_other, y_pair, count, inner, corner_far, corner_near, wide, limit):
+def pack_second(y_other, y_pair, count, inner, dense, corner_far, corner_near, wide, limit):
     low, high = reach()
     up = odd("gy") == 0
     wide[pl.ds(0, OWN * ROWS), :] = inner[pl.ds(0, OWN * ROWS), :]
@@ -560,8 +560,8 @@
     (inner,) = call(pack_wide, [f32(ROOM * ROWS, NZ)], [VMEM], flops=5 * 10**9)(own)
     tile = f32(CORNER + SLOT_ROWS, NZ)
     corner, corner_near, own, limit = call(
-        pack_second, [tile, tile, f32(ROOM * ROWS, NZ), f32(SLOT_ROWS, NZ)], [VMEM, VMEM, SMEM, VMEM]
-    )(y_other, y_pair, counts, inner)
+        pack_second, [tile, tile, f32(ROOM * ROWS, NZ), f32(SLOT_ROWS, NZ)], [VMEM, VMEM, SMEM, VMEM, VMEM]
+    )(y_other, y_pair, counts, inner, dense)
     corner = lax.ppermute(corner, ("gx", "gy"), other_x())
     corner_near = lax.ppermute(corner_near, "gx", pair(N_GX))
     three, six = f32(3 * PX * ROWS, NZ), f32(6 * PX * ROWS, NZ)

time: 33.4 us -> 35 us (1.048)
  the two profiles are of different devices: /device:TPU:128 before, /device:TPU:71 now
where the time goes in v11:
time: 35 us; the launch traced here: 34.7 us
  starting transfers between devices  9.81 us (28%)
  blocking collectives  9.72 us (28%)
  Pallas kernels  8.35 us (24%)
  waiting for transfers between devices  5.47 us (16%)
  between operations  1.35 us (4%)
    all_to_all x1, blocking collectives, body(): gathered = lax.all_to_all(message, 'gy', 0, 0)  9.72 us
    ppermute x1, starting transfers between devices, body(): far = lax.ppermute(far, ('gx', 'gy'), other_x())  4.11 us
    ppermute x1, waiting for transfers between devices, body(): corner = lax.ppermute(corner, ('gx', 'gy'), other_x())  3.53 us
    ppermute x1, starting transfers between devices, body(): y_pair = lax.ppermute(y_pair, 'gy', pair(N_GY))  2.94 us
    pallas_call x1, Pallas kernels, body(): call(near_part, arrays + [f32(LABELS * 6, NZ), f32(3 * CY, NZ)], [SMEM, V...  2.65 us
    pallas_call x1, Pallas kernels, body(): call(far_part, [f32(N_GY, 3 * CY // 2, NZ), three, f32(3, SLOT_ROWS, 128)...  1.93 us
    ppermute x1, waiting for transfers between devices, body(): near = lax.ppermute(near, 'gx', pair(N_GX))  1.56 us
    pallas_call x1, Pallas kernels, body(): call(pack_first, [f32(HALO, OWN, NZ), f32(ROOM * CY, NZ), slots, f32(3, S...  1.3 us
  transfers between devices with their start and end apart: 6, of which 3 were waited for; matrix products, arithmetic and copies ran while one was open for 0% of the time, Pallas kernels for 12%

profile of v11, /device:TPU:71, one launch (start us, length us, event | category | flops | bytes accessed | tf_op | source)
XLA Modules:
  0.0 34.7 jit_solution(9604650360534256542)
XLA Ops:
  0.6 1.3 %shard_map.94 = (f32[3,28,128]{2,1,0:T(8,128)S(1)}, f32[1024,128]{1,0:T(8,128)S(1)}, s32[8,128]{1,0:T(8,128)S(1)}, f32[3,8,128]{2,1,0:T(8,128)S(1)}) custom-call(f32[384,128]{1,0:T(8,128)} %bitcast.10, f32[384,128]{1,0:T(8,128)} %bitcast.11, s32[128,128]{1,0:T(8,128)} %bitcast.12, s32[8,128]{1,0:T(8,128)} %bitcast.14, f32[3,8,128]{2,1,0:T(8,128)} %bitcast.13), custom_call_target="tpu_custom_call" | custom-call | flops 1000 | bytes 1000 | tf_op jit(solution)/shard_map/pallas_call | solution.py:538
  1.9 0.8 %collective-permute-start.1 = (f32[3,28,128]{2,1,0:T(8,128)S(1)}, f32[3,28,128]{2,1,0:T(8,128)S(1)}, u32[]{:S(2)}, u32[]{:S(2)}) collective-permute-start(f32[3,28,128]{2,1,0:T(8,128)S(1)} %get-tuple-element.37), channel_id=1, source_target_pairs={{0,8},{1,2},{2,1},{3,4},{4,3},{5,6},{6,5},{7,15},{8,0},{9,10},{10,... | collective-permute-start | bytes 129032 | tf_op jit(solution)/shard_map/ppermute | solution.py:550
  2.7 4.1 %collective-permute-start = (f32[608,128]{1,0:T(8,128)S(1)}, f32[608,128]{1,0:T(8,128)S(1)}, u32[]{:S(2)}, u32[]{:S(2)}) collective-permute-start(f32[608,128]{1,0:T(8,128)S(1)} %get-tuple-element.36), channel_id=1, source_target_pairs={{0,1},{1,0},{2,3},{3,2},{4,5},{5,4},{6,7},{7,6},{8,16},{9,17},{10,... | collective-permute-start | bytes 933896 | tf_op jit(solution)/shard_map/ppermute | solution.py:554
  6.9 0.0 collective-permute-start.2
  6.9 1.6 %collective-permute-done.2.near = f32[608,128]{1,0:T(8,128)S(1)} collective-permute-done((f32[608,128]{1,0:T(8,128)S(1)}, f32[608,128]{1,0:T(8,128)S(1)}, u32[]{:S(2)}, u32[]{:S(2)}) %collective-permute-start.2) | collective-permute-done | bytes 311328 | tf_op jit(solution)/shard_map/ppermute | solution.py:553
  8.5 0.1 shard_map.96
  8.5 2.9 %collective-permute-start.3 = (f32[3,28,128]{2,1,0:T(8,128)S(1)}, f32[3,28,128]{2,1,0:T(8,128)S(1)}, u32[]{:S(2)}, u32[]{:S(2)}) collective-permute-start(f32[3,28,128]{2,1,0:T(8,128)S(1)} %shard_map.96), channel_id=1, source_target_pairs={{0,1},{1,0},{2,3},{3,2},{4,5},{5,4},{6,7},{7,6},{8,9},{9,8},{10,11... | collective-permute-start | bytes 129032 | tf_op jit(solution)/shard_map/ppermute | solution.py:556
  11.5 0.0 copy-start
  11.5 0.9 %shard_map.98 = (f32[4,128,128]{2,1,0:T(8,128)S(1)}, bf16[128,1024]{1,0:T(8,128)(2,1)S(1)}) custom-call(s32[8,128]{1,0:T(8,128)S(1)} %get-tuple-element.39.cells, f32[3,8,128]{2,1,0:T(8,128)S(1)} %get-tuple-element.35.mult), custom_call_target="tpu_custom_call" | custom-call | flops 5000000000 | bytes 1000 | tf_op jit(solution)/shard_map/pallas_call | solution.py:557
  13.1 0.0 collective-permute-done.1.y_other
  13.1 0.4 %collective-permute-done.3.y_pair = f32[3,28,128]{2,1,0:T(8,128)S(1)} collective-permute-done((f32[3,28,128]{2,1,0:T(8,128)S(1)}, f32[3,28,128]{2,1,0:T(8,128)S(1)}, u32[]{:S(2)}, u32[]{:S(2)}) %collective-permute-start.3) | collective-permute-done | bytes 43040 | tf_op jit(solution)/shard_map/ppermute | solution.py:556
  13.4 0.1 shard_map.99
  13.5 0.8 %collective-permute-start.5 = (f32[104,128]{1,0:T(8,128)S(1)}, f32[104,128]{1,0:T(8,128)S(1)}, u32[]{:S(2)}, u32[]{:S(2)}) collective-permute-start(f32[104,128]{1,0:T(8,128)S(1)} %get-tuple-element.42), channel_id=1, source_target_pairs={{0,8},{8,0},{16,24},{24,16},{32,40},{40,32},{48,56},{56,48},{64,72... | collective-permute-start | bytes 159752 | tf_op jit(solution)/shard_map/ppermute | solution.py:566
  14.3 1.2 %collective-permute-start.4 = (f32[104,128]{1,0:T(8,128)S(1)}, f32[104,128]{1,0:T(8,128)S(1)}, u32[]{:S(2)}, u32[]{:S(2)}) collective-permute-start(f32[104,128]{1,0:T(8,128)S(1)} %get-tuple-element.41), channel_id=1, source_target_pairs={{0,1},{1,0},{2,3},{3,2},{4,5},{5,4},{6,7},{7,6},{8,16},{9,17},{10,... | collective-permute-start | bytes 159752 | tf_op jit(solution)/shard_map/ppermute | solution.py:565
  15.5 0.0 collective-permute-done.5.corner_near
  15.5 0.0 copy-done
  15.5 2.6 %shard_map.100 = (f32[2568,128]{1,0:T(8,128)S(1)}, f32[2400,128]{1,0:T(8,128)S(1)}, f32[2400,128]{1,0:T(8,128)S(1)}, f32[1200,128]{1,0:T(8,128)S(1)}, f32[1200,1...) custom-call(f32[8,6]{1,0:T(8,128)S(1)} %copy-done, ...), custom_call_target="tpu_custom_call" | custom-call | flops 1000 | bytes 1000 | tf_op jit(solution)/shard_map/pallas_call | solution.py:569
  18.2 0.0 collective-permute-done.far
  18.2 0.4 %shard_map.101.ribbon = f32[4,192,128]{2,1,0:T(8,128)S(1)} custom-call(f32[608,128]{1,0:T(8,128)S(1)} %collective-permute-done.far, f32[608,128]{1,0:T(8,128)S(1)} %collective-permute-done.2.near, f32[4,128,128]{2,1,0:T(8,128)S(1)} %get-tuple-element.40.dense, f32[96,128]{1,0:T(8,128)S(1)} %get-tuple-element.45.last), custom_call_target="tpu_custom_call" | custom-call | flops 1000 | bytes 1000 | tf_op jit(solution)/shard_map/pallas_call | solution.py:572
  18.6 3.5 %collective-permute-done.4.corner = f32[104,128]{1,0:T(8,128)S(1)} collective-permute-done((f32[104,128]{1,0:T(8,128)S(1)}, f32[104,128]{1,0:T(8,128)S(1)}, u32[]{:S(2)}, u32[]{:S(2)}) %collective-permute-start.4) | collective-permute-done | bytes 53280 | tf_op jit(solution)/shard_map/ppermute | solution.py:565
  22.1 1.9 %shard_map.102 = (f32[8,48,128]{2,1,0:T(8,128)S(1)}, f32[1200,128]{1,0:T(8,128)S(1)}, f32[3,8,128]{2,1,0:T(8,128)S(1)}) custom-call(f32[608,128]{1,0:T(8,128)S(1)} %collective-permute-done.far, f32[104,128]{1,0:T(8,128)S(1)} %collective-permute-done.4.corner, f32[104,128]{1,0:T(8,128)S(1)} %collective-permute-done.5.corner_near, ...), custom_call_target="tpu_custom_call" | custom-call | flops 1000 | bytes 1000 | tf_op jit(solution)/shard_map/pallas_call | solution.py:573
  24.0 9.7 %all_to_all.5.gathered = f32[8,48,128]{2,1,0:T(8,128)S(1)} all-to-all(f32[8,48,128]{2,1,0:T(8,128)S(1)} %get-tuple-element.59), channel_id=1, replica_groups=mesh['gx'=32,'gy'=8] {'gy'}, dimensions={0} | all-to-all | bytes 393216 | tf_op jit(solution)/shard_map/all_to_all | solution.py:579
  33.8 0.9 %shard_map.103 = (f32[384,128]{1,0:T(8,128)}, f32[3,8,128]{2,1,0:T(8,128)}, f32[3,128,128]{2,1,0:T(8,128)}) custom-call(f32[3,8,128]{2,1,0:T(8,128)S(1)} %get-tuple-element.57.updated, f32[1200,128]{1,0:T(8,128)S(1)} %get-tuple-element.58.low, f32[1200,128]{1,0:T(8,128)S(1)} %get-tuple-element.54.near_second.high, f32[8,48,128]{2,1,0:T(8,128)S(1)} %all_to_all.5.gathered), custom_call_target="tpu_custom_call" | custom-call | flops 1000 | bytes 1000 | tf_op jit(solution)/shard_map/pallas_call | solution.py:580
  (2 shorter events, 0.1 us)
Async XLA Ops:
  1.9 11.1 %collective-permute-start.1 = (f32[3,28,128]{2,1,0:T(8,128)S(1)}, f32[3,28,128]{2,1,0:T(8,128)S(1)}, u32[]{:S(2)}, u32[]{:S(2)}) collective-permute-start(f32[3,28,128]{2,1,0:T(8,128)S(1)} %get-tuple-element.37), channel_id=1, source_target_pairs={{0,8},{1,2},{2,1},{3,4},{4,3},{5,6},{6,5},{7,15},{8,0},{9,10},{10,... | collective-permute-start | bytes 129032 | tf_op jit(solution)/shard_map/ppermute | solution.py:550
  2.7 15.4 %collective-permute-start = (f32[608,128]{1,0:T(8,128)S(1)}, f32[608,128]{1,0:T(8,128)S(1)}, u32[]{:S(2)}, u32[]{:S(2)}) collective-permute-start(f32[608,128]{1,0:T(8,128)S(1)} %get-tuple-element.36), channel_id=1, source_target_pairs={{0,1},{1,0},{2,3},{3,2},{4,5},{5,4},{6,7},{7,6},{8,16},{9,17},{10,... | collective-permute-start | bytes 933896 | tf_op jit(solution)/shard_map/ppermute | solution.py:554
  6.9 1.6 %collective-permute-start.2 = (f32[608,128]{1,0:T(8,128)S(1)}, f32[608,128]{1,0:T(8,128)S(1)}, u32[]{:S(2)}, u32[]{:S(2)}) collective-permute-start(f32[608,128]{1,0:T(8,128)S(1)} %get-tuple-element.38), channel_id=1, source_target_pairs={{0,8},{8,0},{16,24},{24,16},{32,40},{40,32},{48,56},{56,48},{64,72... | collective-permute-start | bytes 933896 | tf_op jit(solution)/shard_map/ppermute | solution.py:553
  8.5 4.9 %collective-permute-start.3 = (f32[3,28,128]{2,1,0:T(8,128)S(1)}, f32[3,28,128]{2,1,0:T(8,128)S(1)}, u32[]{:S(2)}, u32[]{:S(2)}) collective-permute-start(f32[3,28,128]{2,1,0:T(8,128)S(1)} %shard_map.96), channel_id=1, source_target_pairs={{0,1},{1,0},{2,3},{3,2},{4,5},{5,4},{6,7},{7,6},{8,9},{9,8},{10,11... | collective-permute-start | bytes 129032 | tf_op jit(solution)/shard_map/ppermute | solution.py:556
  11.5 4.1 %copy-start = (f32[8,6]{1,0:T(8,128)S(1)}, f32[8,6]{1,0:T(8,128)}, u32[]{:S(2)}) copy-start(f32[8,6]{1,0:T(8,128)} %stiffness.1) | copy-start | bytes 580
  13.5 2.0 %collective-permute-start.5 = (f32[104,128]{1,0:T(8,128)S(1)}, f32[104,128]{1,0:T(8,128)S(1)}, u32[]{:S(2)}, u32[]{:S(2)}) collective-permute-start(f32[104,128]{1,0:T(8,128)S(1)} %get-tuple-element.42), channel_id=1, source_target_pairs={{0,8},{8,0},{16,24},{24,16},{32,40},{40,32},{48,56},{56,48},{64,72... | collective-permute-start | bytes 159752 | tf_op jit(solution)/shard_map/ppermute | solution.py:566
  14.3 7.8 %collective-permute-start.4 = (f32[104,128]{1,0:T(8,128)S(1)}, f32[104,128]{1,0:T(8,128)S(1)}, u32[]{:S(2)}, u32[]{:S(2)}) collective-permute-start(f32[104,128]{1,0:T(8,128)S(1)} %get-tuple-element.41), channel_id=1, source_target_pairs={{0,1},{1,0},{2,3},{3,2},{4,5},{5,4},{6,7},{7,6},{8,16},{9,17},{10,... | collective-permute-start | bytes 159752 | tf_op jit(solution)/shard_map/ppermute | solution.py:565

commit v12 on v11

--- a/solution.py
+++ b/solution.py
@@ -198,11 +198,14 @@
     return [part[3 * c] + part[3 * c + 1] + part[3 * c + 2] for c in range(3)] + [part[9] + part[10]]
 
 
-def spread_own(cells, mult, dense, at_depth):
+def depth_table(cells, at_depth):
     depth = cells[...] % NZ
     for j in range(SLOT_ROWS // 2):
         hit = lax.broadcasted_iota(jnp.int32, (NZ, 256), 0) == paired(depth, j)
         at_depth[:, pl.ds(256 * j, 256)] = jnp.where(hit, 1.0, 0.0).astype(BF16)
+
+
+def spread_own(cells, mult, dense):
     values = spread(cells[...], [mult[c] for c in range(3)], 0, CX * CY)
     for i in range(4):
         dense[i] = values[i]
@@ -554,9 +557,8 @@
     far = lax.ppermute(far, ("gx", "gy"), other_x())
     (y_pair,) = call(pack_pair, [f32(HALO, OWN, NZ)], [VMEM] * 2)(own, near)
     y_pair = lax.ppermute(y_pair, "gy", pair(N_GY))
-    dense, at_depth = call(
-        spread_own, [f32(4, block, NZ), jax.ShapeDtypeStruct((NZ, 8 * 128), BF16)], [VMEM] * 2, flops=5 * 10**9
-    )(cells, mult)
+    (dense,) = call(spread_own, [f32(4, block, NZ)], [VMEM] * 2)(cells, mult)
+    (at_depth,) = call(depth_table, [jax.ShapeDtypeStruct((NZ, 8 * 128), BF16)], [VMEM], flops=5 * 10**9)(cells)
     (inner,) = call(pack_wide, [f32(ROOM * ROWS, NZ)], [VMEM], flops=5 * 10**9)(own)
     tile = f32(CORNER + SLOT_ROWS, NZ)
     corner, corner_near, own, limit = call(

time: 35 us -> 33.4 us (0.954)
  the two profiles are of different devices: /device:TPU:71 before, /device:TPU:128 now
where the time goes in v12:
time: 33.4 us; the launch traced here: 33.1 us
  blocking collectives  12.6 us (38%)
  starting transfers between devices  8.86 us (27%)
  Pallas kernels  8.38 us (25%)
  waiting for transfers between devices  1.9 us (6%)
  between operations  1.39 us (4%)
    all_to_all x1, blocking collectives, body(): gathered = lax.all_to_all(message, 'gy', 0, 0)  12.6 us
    ppermute x1, starting transfers between devices, body(): corner = lax.ppermute(corner, ('gx', 'gy'), other_x())  3.74 us
    ppermute x1, starting transfers between devices, body(): y_pair = lax.ppermute(y_pair, 'gy', pair(N_GY))  2.88 us
    pallas_call x1, Pallas kernels, body(): call(near_part, arrays + [f32(LABELS * 6, NZ), f32(3 * CY, NZ)], [SMEM, V...  2.65 us
    pallas_call x1, Pallas kernels, body(): call(far_part, [f32(N_GY, 3 * CY // 2, NZ), three, f32(3, SLOT_ROWS, 128)...  1.93 us
    ppermute x1, starting transfers between devices, body(): far = lax.ppermute(far, ('gx', 'gy'), other_x())  1.55 us
    pallas_call x1, Pallas kernels, body(): call(pack_first, [f32(HALO, OWN, NZ), f32(ROOM * CY, NZ), slots, f32(3, S...  1.3 us
    ppermute x1, waiting for transfers between devices, body(): far = lax.ppermute(far, ('gx', 'gy'), other_x())  1.26 us
  transfers between devices with their start and end apart: 6, of which 3 were waited for; matrix products, arithmetic and copies ran while one was open for 0% of the time, Pallas kernels for 13%

profile of v12, /device:TPU:128, one launch (start us, length us, event | category | flops | bytes accessed | tf_op | source)
XLA Modules:
  0.0 33.1 jit_solution(4803533008459603058)
XLA Ops:
  0.6 1.3 %shard_map.94 = (f32[3,28,128]{2,1,0:T(8,128)S(1)}, f32[1024,128]{1,0:T(8,128)S(1)}, s32[8,128]{1,0:T(8,128)S(1)}, f32[3,8,128]{2,1,0:T(8,128)S(1)}) custom-call(f32[384,128]{1,0:T(8,128)} %bitcast.10, f32[384,128]{1,0:T(8,128)} %bitcast.11, s32[128,128]{1,0:T(8,128)} %bitcast.12, s32[8,128]{1,0:T(8,128)} %bitcast.14, f32[3,8,128]{2,1,0:T(8,128)} %bitcast.13), custom_call_target="tpu_custom_call" | custom-call | flops 1000 | bytes 1000 | tf_op jit(solution)/shard_map/pallas_call | solution.py:541
  2.0 0.1 collective-permute-start.2
  2.1 0.5 %collective-permute-start.1 = (f32[3,28,128]{2,1,0:T(8,128)S(1)}, f32[3,28,128]{2,1,0:T(8,128)S(1)}, u32[]{:S(2)}, u32[]{:S(2)}) collective-permute-start(f32[3,28,128]{2,1,0:T(8,128)S(1)} %get-tuple-element.35), channel_id=1, source_target_pairs={{0,8},{1,2},{2,1},{3,4},{4,3},{5,6},{6,5},{7,15},{8,0},{9,10},{10,... | collective-permute-start | bytes 129032 | tf_op jit(solution)/shard_map/ppermute | solution.py:553
  2.6 1.6 %collective-permute-start = (f32[608,128]{1,0:T(8,128)S(1)}, f32[608,128]{1,0:T(8,128)S(1)}, u32[]{:S(2)}, u32[]{:S(2)}) collective-permute-start(f32[608,128]{1,0:T(8,128)S(1)} %get-tuple-element.34), channel_id=1, source_target_pairs={{0,1},{1,0},{2,3},{3,2},{4,5},{5,4},{6,7},{7,6},{8,16},{9,17},{10,... | collective-permute-start | bytes 933896 | tf_op jit(solution)/shard_map/ppermute | solution.py:557
  4.1 0.0 collective-permute-done.2.near
  4.1 0.1 shard_map.96
  4.2 2.9 %collective-permute-start.3 = (f32[3,28,128]{2,1,0:T(8,128)S(1)}, f32[3,28,128]{2,1,0:T(8,128)S(1)}, u32[]{:S(2)}, u32[]{:S(2)}) collective-permute-start(f32[3,28,128]{2,1,0:T(8,128)S(1)} %shard_map.96), channel_id=1, source_target_pairs={{0,1},{1,0},{2,3},{3,2},{4,5},{5,4},{6,7},{7,6},{8,9},{9,8},{10,11... | collective-permute-start | bytes 129032 | tf_op jit(solution)/shard_map/ppermute | solution.py:559
  7.1 0.9 %shard_map.98.dense = f32[4,128,128]{2,1,0:T(8,128)S(1)} custom-call(s32[8,128]{1,0:T(8,128)S(1)} %get-tuple-element.37.cells, f32[3,8,128]{2,1,0:T(8,128)S(1)} %get-tuple-element.33.mult), custom_call_target="tpu_custom_call" | custom-call | flops 1000 | bytes 1000 | tf_op jit(solution)/shard_map/pallas_call | solution.py:560
  8.7 0.0 collective-permute-done.1.y_other
  8.7 0.4 %collective-permute-done.3.y_pair = f32[3,28,128]{2,1,0:T(8,128)S(1)} collective-permute-done((f32[3,28,128]{2,1,0:T(8,128)S(1)}, f32[3,28,128]{2,1,0:T(8,128)S(1)}, u32[]{:S(2)}, u32[]{:S(2)}) %collective-permute-start.3) | collective-permute-done | bytes 43040 | tf_op jit(solution)/shard_map/ppermute | solution.py:559
  9.2 0.1 shard_map.99
  9.2 0.1 collective-permute-start.5
  9.3 0.0 copy-start
  9.3 3.7 %collective-permute-start.4 = (f32[104,128]{1,0:T(8,128)S(1)}, f32[104,128]{1,0:T(8,128)S(1)}, u32[]{:S(2)}, u32[]{:S(2)}) collective-permute-start(f32[104,128]{1,0:T(8,128)S(1)} %get-tuple-element.38), channel_id=1, source_target_pairs={{0,1},{1,0},{2,3},{3,2},{4,5},{5,4},{6,7},{7,6},{8,16},{9,17},{10,... | collective-permute-start | bytes 159752 | tf_op jit(solution)/shard_map/ppermute | solution.py:567
  13.1 0.1 shard_map.102.at_depth
  13.1 0.0 collective-permute-done.5.corner_near
  13.2 0.0 copy-done
  13.2 2.7 %shard_map.100 = (f32[2568,128]{1,0:T(8,128)S(1)}, f32[2400,128]{1,0:T(8,128)S(1)}, f32[2400,128]{1,0:T(8,128)S(1)}, f32[1200,128]{1,0:T(8,128)S(1)}, f32[1200,1...) custom-call(f32[8,6]{1,0:T(8,128)S(1)} %copy-done, ...), custom_call_target="tpu_custom_call" | custom-call | flops 1000 | bytes 1000 | tf_op jit(solution)/shard_map/pallas_call | solution.py:571
  15.8 1.3 %collective-permute-done.far = f32[608,128]{1,0:T(8,128)S(1)} collective-permute-done((f32[608,128]{1,0:T(8,128)S(1)}, f32[608,128]{1,0:T(8,128)S(1)}, u32[]{:S(2)}, u32[]{:S(2)}) %collective-permute-start) | collective-permute-done | bytes 311328 | tf_op jit(solution)/shard_map/ppermute | solution.py:557
  17.1 0.4 %shard_map.101.ribbon = f32[4,192,128]{2,1,0:T(8,128)S(1)} custom-call(f32[608,128]{1,0:T(8,128)S(1)} %collective-permute-done.far, f32[608,128]{1,0:T(8,128)S(1)} %collective-permute-done.2.near, f32[4,128,128]{2,1,0:T(8,128)S(1)} %shard_map.98.dense, f32[96,128]{1,0:T(8,128)S(1)} %get-tuple-element.42.last), custom_call_target="tpu_custom_call" | custom-call | flops 1000 | bytes 1000 | tf_op jit(solution)/shard_map/pallas_call | solution.py:574
  17.5 0.2 collective-permute-done.4.corner
  17.7 1.9 %shard_map.103 = (f32[8,48,128]{2,1,0:T(8,128)S(1)}, f32[1200,128]{1,0:T(8,128)S(1)}, f32[3,8,128]{2,1,0:T(8,128)S(1)}) custom-call(f32[608,128]{1,0:T(8,128)S(1)} %collective-permute-done.far, f32[104,128]{1,0:T(8,128)S(1)} %collective-permute-done.4.corner, f32[104,128]{1,0:T(8,128)S(1)} %collective-permute-done.5.corner_near, ...), custom_call_target="tpu_custom_call" | custom-call | flops 1000 | bytes 1000 | tf_op jit(solution)/shard_map/pallas_call | solution.py:575
  19.6 12.6 %all_to_all.5.gathered = f32[8,48,128]{2,1,0:T(8,128)S(1)} all-to-all(f32[8,48,128]{2,1,0:T(8,128)S(1)} %get-tuple-element.55), channel_id=1, replica_groups=mesh['gx'=32,'gy'=8] {'gy'}, dimensions={0} | all-to-all | bytes 393216 | tf_op jit(solution)/shard_map/all_to_all | solution.py:581
  32.2 0.9 %shard_map.104 = (f32[384,128]{1,0:T(8,128)}, f32[3,8,128]{2,1,0:T(8,128)}, f32[3,128,128]{2,1,0:T(8,128)}) custom-call(f32[3,8,128]{2,1,0:T(8,128)S(1)} %get-tuple-element.53.updated, f32[1200,128]{1,0:T(8,128)S(1)} %get-tuple-element.54.low, f32[1200,128]{1,0:T(8,128)S(1)} %get-tuple-element.50.near_second.high, f32[8,48,128]{2,1,0:T(8,128)S(1)} %all_to_all.5.gathered), custom_call_target="tpu_custom_call" | custom-call | flops 1000 | bytes 1000 | tf_op jit(solution)/shard_map/pallas_call | solution.py:582
  (2 shorter events, 0.1 us)
Async XLA Ops:
  2.0 2.2 %collective-permute-start.2 = (f32[608,128]{1,0:T(8,128)S(1)}, f32[608,128]{1,0:T(8,128)S(1)}, u32[]{:S(2)}, u32[]{:S(2)}) collective-permute-start(f32[608,128]{1,0:T(8,128)S(1)} %get-tuple-element.36), channel_id=1, source_target_pairs={{0,8},{8,0},{16,24},{24,16},{32,40},{40,32},{48,56},{56,48},{64,72... | collective-permute-start | bytes 933896 | tf_op jit(solution)/shard_map/ppermute | solution.py:556
  2.1 6.6 %collective-permute-start.1 = (f32[3,28,128]{2,1,0:T(8,128)S(1)}, f32[3,28,128]{2,1,0:T(8,128)S(1)}, u32[]{:S(2)}, u32[]{:S(2)}) collective-permute-start(f32[3,28,128]{2,1,0:T(8,128)S(1)} %get-tuple-element.35), channel_id=1, source_target_pairs={{0,8},{1,2},{2,1},{3,4},{4,3},{5,6},{6,5},{7,15},{8,0},{9,10},{10,... | collective-permute-start | bytes 129032 | tf_op jit(solution)/shard_map/ppermute | solution.py:553
  2.6 14.5 %collective-permute-start = (f32[608,128]{1,0:T(8,128)S(1)}, f32[608,128]{1,0:T(8,128)S(1)}, u32[]{:S(2)}, u32[]{:S(2)}) collective-permute-start(f32[608,128]{1,0:T(8,128)S(1)} %get-tuple-element.34), channel_id=1, source_target_pairs={{0,1},{1,0},{2,3},{3,2},{4,5},{5,4},{6,7},{7,6},{8,16},{9,17},{10,... | collective-permute-start | bytes 933896 | tf_op jit(solution)/shard_map/ppermute | solution.py:557
  4.2 4.9 %collective-permute-start.3 = (f32[3,28,128]{2,1,0:T(8,128)S(1)}, f32[3,28,128]{2,1,0:T(8,128)S(1)}, u32[]{:S(2)}, u32[]{:S(2)}) collective-permute-start(f32[3,28,128]{2,1,0:T(8,128)S(1)} %shard_map.96), channel_id=1, source_target_pairs={{0,1},{1,0},{2,3},{3,2},{4,5},{5,4},{6,7},{7,6},{8,9},{9,8},{10,11... | collective-permute-start | bytes 129032 | tf_op jit(solution)/shard_map/ppermute | solution.py:559
  9.2 3.9 %collective-permute-start.5 = (f32[104,128]{1,0:T(8,128)S(1)}, f32[104,128]{1,0:T(8,128)S(1)}, u32[]{:S(2)}, u32[]{:S(2)}) collective-permute-start(f32[104,128]{1,0:T(8,128)S(1)} %get-tuple-element.39), channel_id=1, source_target_pairs={{0,8},{8,0},{16,24},{24,16},{32,40},{40,32},{48,56},{56,48},{64,72... | collective-permute-start | bytes 159752 | tf_op jit(solution)/shard_map/ppermute | solution.py:568
  9.3 3.8 %copy-start = (f32[8,6]{1,0:T(8,128)S(1)}, f32[8,6]{1,0:T(8,128)}, u32[]{:S(2)}) copy-start(f32[8,6]{1,0:T(8,128)} %stiffness.1) | copy-start | bytes 580
  9.3 8.3 %collective-permute-start.4 = (f32[104,128]{1,0:T(8,128)S(1)}, f32[104,128]{1,0:T(8,128)S(1)}, u32[]{:S(2)}, u32[]{:S(2)}) collective-permute-start(f32[104,128]{1,0:T(8,128)S(1)} %get-tuple-element.38), channel_id=1, source_target_pairs={{0,1},{1,0},{2,3},{3,2},{4,5},{5,4},{6,7},{7,6},{8,16},{9,17},{10,... | collective-permute-start | bytes 159752 | tf_op jit(solution)/shard_map/ppermute | solution.py:567

commit v13 on v12

--- a/solution.py
+++ b/solution.py
@@ -26,6 +26,7 @@
 OWN = OWN_RHS0 + 3 * CX
 ROOM = 32
 SPARE = 8
+Y_ROWS = HALO * OWN_RHS0 + (HALO - 1) * OWN_RHS0
 SIDE = 3 * HALO + HALO + 3 * (HALO - 1)
 SLOT_ROWS = SLOTS // 128
 IFACE = 4 * SLOT_ROWS
@@ -90,6 +91,21 @@
     return lax.broadcasted_iota(jnp.int32, (SLOT_ROWS, 128), 0) * 128 + lax.broadcasted_iota(
         jnp.int32, (SLOT_ROWS, 128), 1
     )
+
+
+def y_planes():
+    for k in range(HALO):
+        yield k * OWN_RHS0, 0, OWN_RHS0, k
+    for k in range(HALO - 1):
+        yield (HALO + k) * OWN_RHS0, OWN_RHS0, OWN - OWN_RHS0, k
+
+
+def pack_y(own, out, low_face):
+    for at, plane, n, k in y_planes():
+        depth = HALO if plane == 0 else HALO - 1
+        first = own[pl.ds(plane * CY + k, n, stride=CY), :]
+        last = own[pl.ds(plane * CY + CY - depth + k, n, stride=CY), :]
+        out[pl.ds(at, n), :] = jnp.where(low_face, first, last)
 
 
 def pack_first(
@@ -113,10 +129,7 @@
         copy.wait()
     own[pl.ds(OWN_LAB0 * CY, CX * CY), :] = raw_labels[...].astype(F32)
     up = odd("gy") == 0
-    for k in range(HALO):
-        first = own[pl.ds(k, OWN, stride=CY), :]
-        last = own[pl.ds(CY - HALO + k, OWN, stride=CY), :]
-        y_other[k] = jnp.where(up, first, last)
+    pack_y(own, y_other, up)
 
 
 def pack_sides(own, raw_cells, mult, far, near, cells):
@@ -135,10 +148,7 @@
 
 def pack_pair(own, near, y_pair):
     up = odd("gy") == 0
-    for k in range(HALO):
-        first = own[pl.ds(k, OWN, stride=CY), :]
-        last = own[pl.ds(CY - HALO + k, OWN, stride=CY), :]
-        y_pair[k] = jnp.where(up, last, first)
+    pack_y(own, y_pair, jnp.logical_not(up))
 
 
 def reach():
@@ -159,9 +169,11 @@
     low, high = reach()
     up = odd("gy") == 0
     wide[pl.ds(0, OWN * ROWS), :] = inner[pl.ds(0, OWN * ROWS), :]
-    for k in range(HALO):
-        wide[pl.ds(CY + k, OWN, stride=ROWS), :] = high * jnp.where(up, y_pair[k], y_other[k])
-        wide[pl.ds(ROWS - HALO + k, OWN, stride=ROWS), :] = low * jnp.where(up, y_other[k], y_pair[k])
+    for at, plane, n, k in y_planes():
+        depth = HALO if plane == 0 else HALO - 1
+        one, two = y_pair[pl.ds(at, n), :], y_other[pl.ds(at, n), :]
+        wide[pl.ds(plane * ROWS + CY + k, n, stride=ROWS), :] = high * jnp.where(up, one, two)
+        wide[pl.ds(plane * ROWS + ROWS - depth + k, n, stride=ROWS), :] = low * jnp.where(up, two, one)
     live = jnp.full((SLOT_ROWS, 128), count[0, 0].astype(F32), F32)
     limit[...] = live
     planes = list(sent_planes())
@@ -540,7 +552,7 @@
     slots = jax.ShapeDtypeStruct((SLOT_ROWS, 128), jnp.int32)
     y_other, own, raw_cells, mult = call(
         pack_first,
-        [f32(HALO, OWN, NZ), f32(ROOM * CY, NZ), slots, f32(3, SLOT_ROWS, 128)],
+        [f32(Y_ROWS, NZ), f32(ROOM * CY, NZ), slots, f32(3, SLOT_ROWS, 128)],
         [HBM] * 5,
         scratch=[pltpu.VMEM((block, NZ), jnp.int32), pltpu.SemaphoreType.DMA((copies,))],
     )(
@@ -555,7 +567,7 @@
     far, near, cells = call(pack_sides, [side, side, slots], [VMEM] * 3)(own, raw_cells, mult)
     near = lax.ppermute(near, "gx", pair(N_GX))
     far = lax.ppermute(far, ("gx", "gy"), other_x())
-    (y_pair,) = call(pack_pair, [f32(HALO, OWN, NZ)], [VMEM] * 2)(own, near)
+    (y_pair,) = call(pack_pair, [f32(Y_ROWS, NZ)], [VMEM] * 2)(own, near)
     y_pair = lax.ppermute(y_pair, "gy", pair(N_GY))
     (dense,) = call(spread_own, [f32(4, block, NZ)], [VMEM] * 2)(cells, mult)
     (at_depth,) = call(depth_table, [jax.ShapeDtypeStruct((NZ, 8 * 128), BF16)], [VMEM], flops=5 * 10**9)(cells)

time: 33.4 us -> 33.4 us (level)
  no operation moved by 1% of the time
where the time goes in v13:
time: 33.4 us; the launch traced here: 33.1 us
  blocking collectives  12.6 us (38%)
  starting transfers between devices  8.94 us (27%)
  Pallas kernels  8.36 us (25%)
  waiting for transfers between devices  1.82 us (5%)
  between operations  1.39 us (4%)
    all_to_all x1, blocking collectives, body(): gathered = lax.all_to_all(message, 'gy', 0, 0)  12.6 us
    ppermute x1, starting transfers between devices, body(): corner = lax.ppermute(corner, ('gx', 'gy'), other_x())  3.83 us
    ppermute x1, starting transfers between devices, body(): y_pair = lax.ppermute(y_pair, 'gy', pair(N_GY))  2.88 us
    pallas_call x1, Pallas kernels, body(): call(near_part, arrays + [f32(LABELS * 6, NZ), f32(3 * CY, NZ)], [SMEM, V...  2.65 us
    pallas_call x1, Pallas kernels, body(): call(far_part, [f32(N_GY, 3 * CY // 2, NZ), three, f32(3, SLOT_ROWS, 128)...  1.93 us
    ppermute x1, starting transfers between devices, body(): far = lax.ppermute(far, ('gx', 'gy'), other_x())  1.55 us
    pallas_call x1, Pallas kernels, body(): call(pack_first, [f32(Y_ROWS, NZ), f32(ROOM * CY, NZ), slots, f32(3, SLOT...  1.3 us
    ppermute x1, waiting for transfers between devices, body(): far = lax.ppermute(far, ('gx', 'gy'), other_x())  1.27 us
  transfers between devices with their start and end apart: 6, of which 3 were waited for; matrix products, arithmetic and copies ran while one was open for 0% of the time, Pallas kernels for 13%

profile of v13, /device:TPU:128, one launch (start us, length us, event | category | flops | bytes accessed | tf_op | source)
XLA Modules:
  0.0 33.1 jit_solution(4812390647379551673)
XLA Ops:
  0.6 1.3 %shard_map.94 = (f32[80,128]{1,0:T(8,128)S(1)}, f32[1024,128]{1,0:T(8,128)S(1)}, s32[8,128]{1,0:T(8,128)S(1)}, f32[3,8,128]{2,1,0:T(8,128)S(1)}) custom-call(f32[384,128]{1,0:T(8,128)} %bitcast.10, f32[384,128]{1,0:T(8,128)} %bitcast.11, s32[128,128]{1,0:T(8,128)} %bitcast.12, s32[8,128]{1,0:T(8,128)} %bitcast.14, f32[3,8,128]{2,1,0:T(8,128)} %bitcast.13), custom_call_target="tpu_custom_call" | custom-call | flops 1000 | bytes 1000 | tf_op jit(solution)/shard_map/pallas_call | solution.py:553
  2.0 0.1 collective-permute-start.2
  2.1 0.5 %collective-permute-start.1 = (f32[80,128]{1,0:T(8,128)S(1)}, f32[80,128]{1,0:T(8,128)S(1)}, u32[]{:S(2)}, u32[]{:S(2)}) collective-permute-start(f32[80,128]{1,0:T(8,128)S(1)} %get-tuple-element.35), channel_id=1, source_target_pairs={{0,8},{1,2},{2,1},{3,4},{4,3},{5,6},{6,5},{7,15},{8,0},{9,10},{10,... | collective-permute-start | bytes 122888 | tf_op jit(solution)/shard_map/ppermute | solution.py:565
  2.6 1.6 %collective-permute-start = (f32[608,128]{1,0:T(8,128)S(1)}, f32[608,128]{1,0:T(8,128)S(1)}, u32[]{:S(2)}, u32[]{:S(2)}) collective-permute-start(f32[608,128]{1,0:T(8,128)S(1)} %get-tuple-element.34), channel_id=1, source_target_pairs={{0,1},{1,0},{2,3},{3,2},{4,5},{5,4},{6,7},{7,6},{8,16},{9,17},{10,... | collective-permute-start | bytes 933896 | tf_op jit(solution)/shard_map/ppermute | solution.py:569
  4.1 0.0 collective-permute-done.2.near
  4.2 2.9 %collective-permute-start.3 = (f32[80,128]{1,0:T(8,128)S(1)}, f32[80,128]{1,0:T(8,128)S(1)}, u32[]{:S(2)}, u32[]{:S(2)}) collective-permute-start(f32[80,128]{1,0:T(8,128)S(1)} %shard_map.96), channel_id=1, source_target_pairs={{0,1},{1,0},{2,3},{3,2},{4,5},{5,4},{6,7},{7,6},{8,9},{9,8},{10,11... | collective-permute-start | bytes 122888 | tf_op jit(solution)/shard_map/ppermute | solution.py:571
  7.1 0.9 %shard_map.98.dense = f32[4,128,128]{2,1,0:T(8,128)S(1)} custom-call(s32[8,128]{1,0:T(8,128)S(1)} %get-tuple-element.37.cells, f32[3,8,128]{2,1,0:T(8,128)S(1)} %get-tuple-element.33.mult), custom_call_target="tpu_custom_call" | custom-call | flops 1000 | bytes 1000 | tf_op jit(solution)/shard_map/pallas_call | solution.py:572
  8.7 0.0 collective-permute-done.1.y_other
  8.7 0.4 %collective-permute-done.3.y_pair = f32[80,128]{1,0:T(8,128)S(1)} collective-permute-done((f32[80,128]{1,0:T(8,128)S(1)}, f32[80,128]{1,0:T(8,128)S(1)}, u32[]{:S(2)}, u32[]{:S(2)}) %collective-permute-start.3) | collective-permute-done | bytes 40992 | tf_op jit(solution)/shard_map/ppermute | solution.py:571
  9.1 0.1 shard_map.99
  9.1 0.1 collective-permute-start.5
  9.2 0.0 copy-start
  9.2 3.8 %collective-permute-start.4 = (f32[104,128]{1,0:T(8,128)S(1)}, f32[104,128]{1,0:T(8,128)S(1)}, u32[]{:S(2)}, u32[]{:S(2)}) collective-permute-start(f32[104,128]{1,0:T(8,128)S(1)} %get-tuple-element.38), channel_id=1, source_target_pairs={{0,1},{1,0},{2,3},{3,2},{4,5},{5,4},{6,7},{7,6},{8,16},{9,17},{10,... | collective-permute-start | bytes 159752 | tf_op jit(solution)/shard_map/ppermute | solution.py:579
  13.1 0.1 shard_map.102.at_depth
  13.1 0.0 collective-permute-done.5.corner_near
  13.1 0.0 copy-done
  13.1 2.7 %shard_map.100 = (f32[2568,128]{1,0:T(8,128)S(1)}, f32[2400,128]{1,0:T(8,128)S(1)}, f32[2400,128]{1,0:T(8,128)S(1)}, f32[1200,128]{1,0:T(8,128)S(1)}, f32[1200,1...) custom-call(f32[8,6]{1,0:T(8,128)S(1)} %copy-done, ...), custom_call_target="tpu_custom_call" | custom-call | flops 1000 | bytes 1000 | tf_op jit(solution)/shard_map/pallas_call | solution.py:583
  15.8 1.3 %collective-permute-done.far = f32[608,128]{1,0:T(8,128)S(1)} collective-permute-done((f32[608,128]{1,0:T(8,128)S(1)}, f32[608,128]{1,0:T(8,128)S(1)}, u32[]{:S(2)}, u32[]{:S(2)}) %collective-permute-start) | collective-permute-done | bytes 311328 | tf_op jit(solution)/shard_map/ppermute | solution.py:569
  17.1 0.4 %shard_map.101.ribbon = f32[4,192,128]{2,1,0:T(8,128)S(1)} custom-call(f32[608,128]{1,0:T(8,128)S(1)} %collective-permute-done.far, f32[608,128]{1,0:T(8,128)S(1)} %collective-permute-done.2.near, f32[4,128,128]{2,1,0:T(8,128)S(1)} %shard_map.98.dense, f32[96,128]{1,0:T(8,128)S(1)} %get-tuple-element.42.last), custom_call_target="tpu_custom_call" | custom-call | flops 1000 | bytes 1000 | tf_op jit(solution)/shard_map/pallas_call | solution.py:586
  17.5 0.2 collective-permute-done.4.corner
  17.7 1.9 %shard_map.103 = (f32[8,48,128]{2,1,0:T(8,128)S(1)}, f32[1200,128]{1,0:T(8,128)S(1)}, f32[3,8,128]{2,1,0:T(8,128)S(1)}) custom-call(f32[608,128]{1,0:T(8,128)S(1)} %collective-permute-done.far, f32[104,128]{1,0:T(8,128)S(1)} %collective-permute-done.4.corner, f32[104,128]{1,0:T(8,128)S(1)} %collective-permute-done.5.corner_near, ...), custom_call_target="tpu_custom_call" | custom-call | flops 1000 | bytes 1000 | tf_op jit(solution)/shard_map/pallas_call | solution.py:587
  19.6 12.6 %all_to_all.5.gathered = f32[8,48,128]{2,1,0:T(8,128)S(1)} all-to-all(f32[8,48,128]{2,1,0:T(8,128)S(1)} %get-tuple-element.55), channel_id=1, replica_groups=mesh['gx'=32,'gy'=8] {'gy'}, dimensions={0} | all-to-all | bytes 393216 | tf_op jit(solution)/shard_map/all_to_all | solution.py:593
  32.2 0.9 %shard_map.104 = (f32[384,128]{1,0:T(8,128)}, f32[3,8,128]{2,1,0:T(8,128)}, f32[3,128,128]{2,1,0:T(8,128)}) custom-call(f32[3,8,128]{2,1,0:T(8,128)S(1)} %get-tuple-element.53.updated, f32[1200,128]{1,0:T(8,128)S(1)} %get-tuple-element.54.low, f32[1200,128]{1,0:T(8,128)S(1)} %get-tuple-element.50.near_second.high, f32[8,48,128]{2,1,0:T(8,128)S(1)} %all_to_all.5.gathered), custom_call_target="tpu_custom_call" | custom-call | flops 1000 | bytes 1000 | tf_op jit(solution)/shard_map/pallas_call | solution.py:594
  (3 shorter events, 0.1 us)
Async XLA Ops:
  2.0 2.2 %collective-permute-start.2 = (f32[608,128]{1,0:T(8,128)S(1)}, f32[608,128]{1,0:T(8,128)S(1)}, u32[]{:S(2)}, u32[]{:S(2)}) collective-permute-start(f32[608,128]{1,0:T(8,128)S(1)} %get-tuple-element.36), channel_id=1, source_target_pairs={{0,8},{8,0},{16,24},{24,16},{32,40},{40,32},{48,56},{56,48},{64,72... | collective-permute-start | bytes 933896 | tf_op jit(solution)/shard_map/ppermute | solution.py:568
  2.1 6.6 %collective-permute-start.1 = (f32[80,128]{1,0:T(8,128)S(1)}, f32[80,128]{1,0:T(8,128)S(1)}, u32[]{:S(2)}, u32[]{:S(2)}) collective-permute-start(f32[80,128]{1,0:T(8,128)S(1)} %get-tuple-element.35), channel_id=1, source_target_pairs={{0,8},{1,2},{2,1},{3,4},{4,3},{5,6},{6,5},{7,15},{8,0},{9,10},{10,... | collective-permute-start | bytes 122888 | tf_op jit(solution)/shard_map/ppermute | solution.py:565
  2.6 14.5 %collective-permute-start = (f32[608,128]{1,0:T(8,128)S(1)}, f32[608,128]{1,0:T(8,128)S(1)}, u32[]{:S(2)}, u32[]{:S(2)}) collective-permute-start(f32[608,128]{1,0:T(8,128)S(1)} %get-tuple-element.34), channel_id=1, source_target_pairs={{0,1},{1,0},{2,3},{3,2},{4,5},{5,4},{6,7},{7,6},{8,16},{9,17},{10,... | collective-permute-start | bytes 933896 | tf_op jit(solution)/shard_map/ppermute | solution.py:569
  4.2 4.9 %collective-permute-start.3 = (f32[80,128]{1,0:T(8,128)S(1)}, f32[80,128]{1,0:T(8,128)S(1)}, u32[]{:S(2)}, u32[]{:S(2)}) collective-permute-start(f32[80,128]{1,0:T(8,128)S(1)} %shard_map.96), channel_id=1, source_target_pairs={{0,1},{1,0},{2,3},{3,2},{4,5},{5,4},{6,7},{7,6},{8,9},{9,8},{10,11... | collective-permute-start | bytes 122888 | tf_op jit(solution)/shard_map/ppermute | solution.py:571
  9.1 4.0 %collective-permute-start.5 = (f32[104,128]{1,0:T(8,128)S(1)}, f32[104,128]{1,0:T(8,128)S(1)}, u32[]{:S(2)}, u32[]{:S(2)}) collective-permute-start(f32[104,128]{1,0:T(8,128)S(1)} %get-tuple-element.39), channel_id=1, source_target_pairs={{0,8},{8,0},{16,24},{24,16},{32,40},{40,32},{48,56},{56,48},{64,72... | collective-permute-start | bytes 159752 | tf_op jit(solution)/shard_map/ppermute | solution.py:580
  9.2 3.9 %copy-start = (f32[8,6]{1,0:T(8,128)S(1)}, f32[8,6]{1,0:T(8,128)}, u32[]{:S(2)}) copy-start(f32[8,6]{1,0:T(8,128)} %stiffness.1) | copy-start | bytes 580
  9.2 8.4 %collective-permute-start.4 = (f32[104,128]{1,0:T(8,128)S(1)}, f32[104,128]{1,0:T(8,128)S(1)}, u32[]{:S(2)}, u32[]{:S(2)}) collective-permute-start(f32[104,128]{1,0:T(8,128)S(1)} %get-tuple-element.38), channel_id=1, source_target_pairs={{0,1},{1,0},{2,3},{3,2},{4,5},{5,4},{6,7},{7,6},{8,16},{9,17},{10,... | collective-permute-start | bytes 159752 | tf_op jit(solution)/shard_map/ppermute | solution.py:579
